TPU v7x, 128 devices: a whole 4x4x4 slice. The times are simulated.
128 devices in a mesh: ctx: 16 (over y_lo, x, core), tp: 8 (over z, y_hi).
Axes of the slice: x: 4, y: 4 (y_hi: 2, y_lo: 2; y = y_hi * 2 + y_lo), z: 4, core: 2. Of those that a mesh axis runs over, the one named last changes fastest.
Arguments:
- hidden_in: bfloat16 [16384, 4096], P(('ctx', 'tp')), may hold values from -6 to 6
- gain: bfloat16 [4096], replicated, may hold values from 0.5 to 1.5
- positions: int32 [16384], P('ctx'), may hold values from 0 to 16383, as said below
- w_query: bfloat16 [4096, 4096], P(None, 'tp')
- w_key: bfloat16 [4096, 1024], P(None, 'tp')
- w_value: bfloat16 [4096, 1024], P(None, 'tp'), may hold values from -0.09375 to 0.09375
- w_out: bfloat16 [4096, 4096], P('tp'), may hold values from -0.09375 to 0.09375
Outputs:
- hidden_out: bfloat16 [16384, 4096], P(('ctx', 'tp'))
Inputs may be any that keep to these rules, and one draw needn't show every extreme that they name: A permutation of 0 to 16383. The 1024 rows of one index of ctx hold two blocks of 512 consecutive positions in rising order: block c, then block 31 - c, for some c; which c lies on which index is drawn.
All inputs are finite; a program needn't handle non-finite values.
Results may differ from a plain program's by a relative error of at most 0.015.
The roundings to bfloat16 on the way count: a program that leaves them out, or rounds other values in their place, can miss the bound.
Values may be sent and summed in bfloat16 or wider, within the bound.
No kernel may reach another device: no remote copies, remote signals or barrier semaphores. Data moves between devices by JAX's collectives and lax.ppermute only.
A program may use at most 128 MiB of HBM per device.

v0:
```python
import math

import jax
import jax.numpy as jnp
from jax import lax
from jax.sharding import PartitionSpec as P

HEAD = 128


EPS = 1e-05
BASE = 500000.0
NEGATIVE = -1e30


def rope_angles(positions, head):
    half = head // 2
    freq = BASE ** (-(jnp.arange(half, dtype=jnp.float32) * 2.0 / head))
    angle = positions.astype(jnp.float32)[:, None] * freq[None, :]
    return (jnp.cos(angle), jnp.sin(angle))


def rotate(vectors, cosine, sine):
    half = vectors.shape[-1] // 2
    first = vectors[..., :half]
    second = vectors[..., half:]
    cosine = cosine[:, None, :]
    sine = sine[:, None, :]
    return jnp.concatenate(
        [first * cosine - second * sine, second * cosine + first * sine], axis=-1
    )


def per_device(hidden_in, gain, positions, w_query, w_key, w_value, w_out):
    widened = hidden_in.astype(jnp.float32)
    scale_rows = lax.rsqrt(jnp.mean(widened * widened, axis=-1, keepdims=True) + EPS)
    normed = (widened * scale_rows * gain.astype(jnp.float32)).astype(jnp.bfloat16)
    query_cols = w_query.shape[1]
    key_cols = w_key.shape[1]
    query_heads = query_cols // HEAD
    key_heads = key_cols // HEAD
    group = query_heads // key_heads
    piece = lax.all_gather(normed, "tp", axis=0, tiled=True)
    projected = jnp.concatenate(
        [
            jnp.dot(piece, w_query, preferred_element_type=jnp.float32),
            jnp.dot(piece, w_key, preferred_element_type=jnp.float32),
            jnp.dot(piece, w_value, preferred_element_type=jnp.float32),
        ],
        axis=1,
    )
    count_rows = projected.shape[0]
    cosine, sine = rope_angles(positions, HEAD)
    query = rotate(
        projected[:, :query_cols].reshape(count_rows, query_heads, HEAD), cosine, sine
    ).astype(jnp.bfloat16)
    keys = rotate(
        projected[:, query_cols : query_cols + key_cols].reshape(count_rows, key_heads, HEAD),
        cosine,
        sine,
    )
    keys = keys.astype(jnp.bfloat16).reshape(count_rows, key_cols)
    values = projected[:, query_cols + key_cols :].astype(jnp.bfloat16)
    stacked = query.reshape(count_rows, key_heads, group, HEAD).transpose(1, 2, 0, 3)
    stacked = stacked.reshape(key_heads, group * count_rows, HEAD)
    query_pos = jnp.tile(positions, group)
    score_scale = 1.0 / HEAD**0.5

    def attend(carry, block):
        running_max, total, weighted = carry
        key_block, value_block, pos_block = block
        key_block = key_block.reshape(key_block.shape[0], key_heads, HEAD)
        value_block = value_block.reshape(value_block.shape[0], key_heads, HEAD)
        scores = (
            jnp.einsum("hqd,khd->hqk", stacked, key_block, preferred_element_type=jnp.float32)
            * score_scale
        )
        allowed = (query_pos[:, None] >= pos_block[None, :])[None]
        scores = jnp.where(allowed, scores, NEGATIVE)
        new_max = jnp.maximum(running_max, jnp.max(scores, axis=-1))
        weights = jnp.where(allowed, jnp.exp(scores - new_max[..., None]), 0.0)
        fade = jnp.exp(running_max - new_max)
        total = total * fade + jnp.sum(weights, axis=-1)
        weighted = weighted * fade[..., None] + jnp.einsum(
            "hqk,khd->hqd",
            weights.astype(jnp.bfloat16),
            value_block,
            preferred_element_type=jnp.float32,
        )
        return ((new_max, total, weighted), None)

    initial = (
        jnp.full((key_heads, group * count_rows), NEGATIVE, jnp.float32),
        jnp.zeros((key_heads, group * count_rows), jnp.float32),
        jnp.zeros((key_heads, group * count_rows, HEAD), jnp.float32),
    )
    carry = initial
    key_piece = lax.all_gather(keys, "ctx", axis=0, tiled=True)
    value_piece = lax.all_gather(values, "ctx", axis=0, tiled=True)
    pos_piece = lax.all_gather(positions, "ctx", axis=0, tiled=True)
    count_keys = key_piece.shape[0]
    block_len = math.gcd(count_keys, 512)
    blocks = count_keys // block_len
    split = (
        key_piece.reshape(blocks, block_len, key_cols),
        value_piece.reshape(blocks, block_len, key_cols),
        pos_piece.reshape(blocks, block_len),
    )
    carry, _ = lax.scan(attend, carry, split)
    running_max, total, weighted = carry
    mixed = weighted / total[..., None]
    mixed = mixed.reshape(key_heads, group, count_rows, HEAD).transpose(2, 0, 1, 3)
    mixed = mixed.reshape(count_rows, query_cols).astype(jnp.bfloat16)
    terms = jnp.dot(mixed, w_out, preferred_element_type=jnp.float32)
    summed = lax.psum_scatter(
        terms.astype(jnp.bfloat16), "tp", scatter_dimension=0, tiled=True
    ).astype(jnp.float32)
    return (widened + summed).astype(jnp.bfloat16)


def solution(mesh):
    in_specs = (
        P(("ctx", "tp"), None),
        P(),
        P("ctx"),
        P(None, "tp"),
        P(None, "tp"),
        P(None, "tp"),
        P("tp", None),
    )
    out_specs = P(("ctx", "tp"), None)
    return jax.shard_map(
        per_device, mesh=mesh, in_specs=in_specs, out_specs=out_specs, check_vma=False
    )
```

profile of v0, /device:TPU:1, one launch (start us, length us, event | category | flops | bytes accessed | tf_op | source)
XLA Modules:
  0.0 852.5 jit_solution(15687833635663465740)
XLA Ops:
  11.5 110.1 %all-gather.4.cloned.1.call-done = bf16[1024,4096]{1,0:T(8,128)(2,1)} async-done(((bf16[128,4096]{1,0:T(8,128)(2,1)}), bf16[1024,4096]{1,0:T(8,128)(2,1)}) %all-gather.4.cloned.1.call-update) | async-done | bytes 8388624 | tf_op jit(solution)/shard_map/all_gather | solution.py:43
  121.7 6.3 convolution_bitcast_fusion.1
  129.9 6.4 convolution_convert_fusion.1
  136.4 20.3 %all_gather.12 = s32[16384]{0:T(1024)S(1)} all-gather(s32[1024]{0:T(1024)S(1)} %copy-done.5), channel_id=1, replica_groups=mesh['ctx'=16,'tp'=8] {'ctx'}, dimensions={0}, use_global_device_ids=true | all-gather | bytes 69632 | tf_op jit(solution)/shard_map/all_gather | solution.py:100
  157.7 8.3 fusion.42
  167.9 6.5 copy.18
  174.4 30.7 %all-gather.8.cloned.1.call-done = bf16[16384,128]{1,0:T(8,128)(2,1)} async-done(((bf16[1024,128]{1,0:T(8,128)(2,1)}), bf16[16384,128]{1,0:T(8,128)(2,1)}) %all-gather.8.cloned.1.call-update) | async-done | bytes 4194320 | tf_op jit(solution)/shard_map/all_gather | solution.py:99
  205.1 511.7 %while.15 = (s32[]{:T(128)}, f32[1,4096]{1,0:T(1,128)S(1)}, f32[1,4096]{1,0:T(1,128)S(1)}, f32[1,4096,128]{2,1,0:T(8,128)S(1)}, s32[32,512]{1,0:T(8,128)S(1)}, /...) while((s32[]{:T(128)}, f32[1,4096]{1,0:T(1,128)S(1)}, ...), condition=%wide.region_4.5_spmd.clone, body=%wide.region_1.4_spmd.clone.sunk | while | flops 1108889600 | bytes 64601240 | solution.py:109
  205.1 5.8 fusion.60
  237.1 5.8 fusion.60
  269.1 5.8 fusion.60
  301.1 5.8 fusion.60
  333.0 5.8 fusion.60
  365.0 5.8 fusion.60
  397.0 5.8 fusion.60
  429.0 5.8 fusion.60
  461.0 5.8 fusion.60
  493.0 5.8 fusion.60
  524.9 5.8 fusion.60
  556.9 5.8 fusion.60
  588.9 5.8 fusion.60
  620.9 5.8 fusion.60
  720.6 9.2 %convolution_convert_fusion = bf16[1024,4096]{1,0:T(8,128)(2,1)} fusion(bf16[1024,512]{0,1:T(8,128)(2,1)S(1)} %bitcast.105, bf16[512,4096]{1,0:T(8,128)(2,1)} %param.15), kind=kOutput, calls=%fused_computation.34 | convolution fusion | flops 4299161600 | bytes 13631488 | tf_op jit(solution)/shard_map/dot_general | solution.py:114
  729.8 113.7 %reduce-scatter.2.cloned.1.call-done = bf16[128,4096]{1,0:T(8,128)(2,1)} async-done(((bf16[1024,4096]{1,0:T(8,128)(2,1)}), bf16[128,4096]{1,0:T(8,128)(2,1)}) %reduce-scatter.2.cloned.1.call-update) | async-done | bytes 1048592 | tf_op jit(solution)/shard_map/reduce_scatter | solution.py:115
  (378 shorter events, 443.8 us)
Async XLA Ops:
  6.5 115.1 %copy-start = (bf16[4096,128]{1,0:T(8,128)(2,1)S(1)}, bf16[4096,128]{1,0:T(8,128)(2,1)}, u32[]{:S(2)}) copy-start(bf16[4096,128]{1,0:T(8,128)(2,1)} %param.13) | copy-start | bytes 3145732
  6.5 115.1 %all-gather.4.cloned.1.call-start = ((), (), s32[]{:S(2)}) async-start(), calls=%async_computation.1 | async-start | bytes 9437184 | tf_op jit(solution)/shard_map/all_gather | solution.py:43
  11.4 156.4 %all-gather.6.cloned.1.call-start = ((), (), s32[]{:S(2)}) async-start(), calls=%async_computation.2 | async-start | bytes 4456448 | tf_op jit(solution)/shard_map/all_gather | solution.py:98
  11.5 118.4 %copy-start.6 = (bf16[4096,128]{1,0:T(8,128)(2,1)S(1)}, bf16[4096,128]{1,0:T(8,128)(2,1)}, u32[]{:S(2)}) copy-start(bf16[4096,128]{1,0:T(8,128)(2,1)} %param.14) | copy-start | bytes 3145732
  129.8 75.2 %all-gather.8.cloned.1.call-start = ((), (), s32[]{:S(2)}) async-start(), calls=%async_computation.3 | async-start | bytes 4456448 | tf_op jit(solution)/shard_map/all_gather | solution.py:99
  136.3 707.2 %reduce-scatter.2.cloned.1.call-start = ((), (), s32[]{:S(2)}) async-start(), calls=%async_computation.4 | async-start | bytes 9437184 | tf_op jit(solution)/shard_map/reduce_scatter | solution.py:115
  167.8 37.2 %copy-start.3 = (f32[1,4096,128]{2,1,0:T(8,128)S(1)}, f32[1,4096,128]{2,1,0:T(8,128)}, u32[]{:S(2)}) copy-start(f32[1,4096,128]{2,1,0:T(8,128)} %custom-call.2) | copy-start | bytes 6291460
  211.0 5.8 copy-start.1
  227.0 5.8 copy-start.1
  243.0 5.8 copy-start.1
  258.9 5.8 copy-start.1
  274.9 5.8 copy-start.1
  290.9 5.8 copy-start.1
  306.9 5.8 copy-start.1
  322.9 5.8 copy-start.1
  338.9 5.8 copy-start.1
  354.9 5.8 copy-start.1
  370.9 5.8 copy-start.1
  386.9 5.8 copy-start.1
  402.9 5.8 copy-start.1
  418.9 5.8 copy-start.1
  434.9 5.8 copy-start.1
  450.8 5.8 copy-start.1
  729.8 113.8 %copy-start.2 = (bf16[128,4096]{1,0:T(8,128)(2,1)S(1)}, bf16[128,4096]{1,0:T(8,128)(2,1)}, u32[]{:S(2)}) copy-start(bf16[128,4096]{1,0:T(8,128)(2,1)} %param.9) | copy-start | bytes 3145732
  (18 other events, 99.7 us)
Sparse Core Ops, SparseCore 0:
  11.5 110.0 all-gather.3
  130.0 35.8 all-gather.5
  167.6 37.4 all-gather.7
  729.9 113.5 reduce-scatter.1
where the time goes:
time: 854 us; the launch traced here: 853 us
  matrix products  352 us (41%)
  waiting for transfers between devices  255 us (30%)
  other arithmetic  187 us (22%)
  local copies, waits for them, and re-layouts  22.9 us (3%)
  blocking collectives  20.3 us (2%)
  between operations  13.3 us (2%)
    dot_general x32, matrix products, attend(): jnp.einsum('hqd,khd->hqk', stacked, key_block, preferred_element_type=jnp...  187 us
    reduce_sum x32, other arithmetic, attend(): total = total * fade + jnp.sum(weights, axis=-1)  172 us
    dot_general x32, matrix products, attend(): jnp.einsum('hqk,khd->hqd', weights.astype(jnp.bfloat16), value_block, pre...  135 us
    reduce_scatter x1, waiting for transfers between devices, per_device(): lax.psum_scatter(terms.astype(jnp.bfloat16), 'tp', scatter_dimension=0, t...  114 us
    all_gather x1, waiting for transfers between devices, per_device(): piece = lax.all_gather(normed, 'tp', axis=0, tiled=True)  110 us
    all_gather x1, waiting for transfers between devices, per_device(): value_piece = lax.all_gather(values, 'ctx', axis=0, tiled=True)  30.7 us
    all_gather x1, blocking collectives, per_device(): pos_piece = lax.all_gather(positions, 'ctx', axis=0, tiled=True)  20.3 us
  transfers between devices with their start and end apart: 4, of which 3 were waited for; matrix products, arithmetic and copies ran while one was open for 3% of the time, Pallas kernels for 0%

commit v1 on v0

v1 whole, which is shorter than its diff:
```python
import functools
import math

import jax
import jax.numpy as jnp
from jax import lax
from jax.experimental import pallas as pl
from jax.experimental.pallas import tpu as pltpu
from jax.sharding import Mesh
from jax.sharding import PartitionSpec as P

HEAD = 128
SPAN = 512
EPS = 1e-05
BASE = 500000.0
NEGATIVE = -1e30
PARTS = 2
VMEM_LIMIT = 56 * 2**20
SCORE_SCALE = math.log2(math.e) / HEAD**0.5


def rope_tables(positions):
    half = HEAD // 2
    freq = BASE ** (-(jnp.arange(half, dtype=jnp.float32) * 2.0 / HEAD))
    angle = positions.astype(jnp.float32)[:, None] * freq[None, :]
    cosine, sine = jnp.cos(angle), jnp.sin(angle)
    return (
        jnp.concatenate([cosine, cosine], axis=1),
        jnp.concatenate([-sine, sine], axis=1),
    )


def project_kernel(x_ref, wq_ref, wk_ref, wv_ref, cos_ref, sin_ref, q_ref, kv_ref):
    x = x_ref[...]
    cosine, sine = cos_ref[...], sin_ref[...]
    rows = x.shape[0]
    owned = HEAD
    piece = owned // PARTS

    def rope(u):
        return u * cosine + pltpu.roll(u, HEAD // 2, 1) * sine

    keys = jnp.dot(x, wk_ref[...], preferred_element_type=jnp.float32)
    kv_ref[:, :HEAD] = rope(keys).astype(jnp.bfloat16)
    values = jnp.dot(x, wv_ref[...], preferred_element_type=jnp.float32)
    kv_ref[:, HEAD:] = values.astype(jnp.bfloat16)
    query = jnp.dot(x, wq_ref[...], preferred_element_type=jnp.float32)
    for h in range(query.shape[1] // HEAD):
        turned = rope(query[:, h * HEAD : (h + 1) * HEAD]) * SCORE_SCALE
        turned = turned.astype(jnp.bfloat16)
        for t in range(rows // owned):
            for part in range(PARTS):
                start = t * owned + part * piece
                q_ref[part, 0, h, t * piece : (t + 1) * piece, :] = turned[
                    start : start + piece
                ]


def project(x, w_query, w_key, w_value, cosine, sine):
    count, width = x.shape
    step = 256
    heads = w_query.shape[1] // HEAD
    per_span = SPAN // step
    whole = lambda i: (0, 0)
    by_row = lambda i: (i, 0)
    flops = 2 * count * width * (w_query.shape[1] + 2 * HEAD)
    moved = 2 * (x.size + w_query.size + w_key.size + w_value.size)
    return pl.pallas_call(
        project_kernel,
        grid=(count // step,),
        in_specs=[
            pl.BlockSpec((step, width), by_row),
            pl.BlockSpec(w_query.shape, whole),
            pl.BlockSpec(w_key.shape, whole),
            pl.BlockSpec(w_value.shape, whole),
            pl.BlockSpec((step, HEAD), by_row),
            pl.BlockSpec((step, HEAD), by_row),
        ],
        out_specs=[
            pl.BlockSpec(
                (PARTS, 1, heads, step // PARTS, HEAD),
                lambda i: (0, i // per_span, 0, i % per_span, 0),
            ),
            pl.BlockSpec((step, 2 * HEAD), by_row),
        ],
        out_shape=[
            jax.ShapeDtypeStruct(
                (PARTS, count // SPAN, heads, SPAN // PARTS, HEAD), jnp.bfloat16
            ),
            jax.ShapeDtypeStruct((count, 2 * HEAD), jnp.bfloat16),
        ],
        compiler_params=pltpu.CompilerParams(vmem_limit_bytes=VMEM_LIMIT),
        cost_estimate=pl.CostEstimate(
            flops=flops, bytes_accessed=moved, transcendentals=0
        ),
    )(x, w_query, w_key, w_value, cosine, sine)


def attend_kernel(
    ids_ref, off_ref, q_ref, kv_ref, o_ref, max_ref, sum_ref, acc_ref,
    *, part, heads, pairs, key_step, row_step, unroll,
):
    per = q_ref.shape[0] // 2
    rows = per // heads
    piece = HEAD // PARTS

    def pair(which, block, masked):
        start = off_ref[block]
        for n in range(SPAN // key_step):
            at = pl.multiple_of(start + n * key_step, key_step)
            keys = kv_ref[pl.ds(at, key_step), :HEAD]
            values = kv_ref[pl.ds(at, key_step), HEAD:]
            for t in range(per // row_step):
                here = pl.ds(pl.multiple_of(which * per + t * row_step, row_step), row_step)
                scores = lax.dot_general(
                    q_ref[here, :], keys, (((1,), (1,)), ((), ())),
                    preferred_element_type=jnp.float32,
                )
                if masked:
                    row = lax.broadcasted_iota(jnp.int32, scores.shape, 0) & (rows - 1)
                    row = (row // piece) * HEAD + part * piece + (row & (piece - 1))
                    col = lax.broadcasted_iota(jnp.int32, scores.shape, 1) + n * key_step
                    scores = jnp.where(row >= col, scores, NEGATIVE)
                old = max_ref[here, :]
                new = jnp.maximum(old, jnp.max(scores, axis=1, keepdims=True))
                fade = jnp.exp2(old - new)
                weights = jnp.exp2(scores - jnp.concatenate([new] * (key_step // HEAD), axis=1))
                max_ref[here, :] = new
                added = weights[:, :HEAD]
                for u in range(1, key_step // HEAD):
                    added = added + weights[:, u * HEAD : (u + 1) * HEAD]
                sum_ref[here, :] = sum_ref[here, :] * fade + added
                acc_ref[here, :] = acc_ref[here, :] * fade + jnp.dot(
                    weights.astype(jnp.bfloat16), values, preferred_element_type=jnp.float32
                )

    max_ref[...] = jnp.full_like(max_ref, NEGATIVE)
    sum_ref[...] = jnp.zeros_like(sum_ref)
    acc_ref[...] = jnp.zeros_like(acc_ref)
    first = ids_ref[0]

    def plain(i):
        which = (i >= first).astype(jnp.int32)
        pair(which, i - which * first, False)

    def body(j, carry):
        for u in range(unroll):
            plain(j * unroll + u)
        return carry

    lax.fori_loop(0, pairs // unroll, body, 0)
    for i in range(pairs // unroll * unroll, pairs):
        plain(jnp.int32(i))
    for which in range(2):
        pair(which, ids_ref[which], True)
    for which in range(2):
        for h in range(heads):
            here = slice(which * per + h * rows, which * per + (h + 1) * rows)
            total = jnp.sum(sum_ref[here, :], axis=1, keepdims=True)
            o_ref[which * rows : (which + 1) * rows, h * HEAD : (h + 1) * HEAD] = (
                acc_ref[here, :] / total
            ).astype(jnp.bfloat16)


def attend(ids, offsets, query, kv, part):
    blocks, heads, rows, _ = query.shape
    pairs = kv.shape[0] // SPAN - 1
    query = query.reshape(blocks * heads * rows, HEAD)
    vmem = pl.BlockSpec(memory_space=pltpu.VMEM)
    smem = pl.BlockSpec(memory_space=pltpu.SMEM)
    scores = (pairs + 2) * heads * rows * SPAN
    return pl.pallas_call(
        functools.partial(
            attend_kernel, part=part, heads=heads, pairs=pairs,
            key_step=256, row_step=512, unroll=8,
        ),
        in_specs=[smem, smem, vmem, vmem],
        out_specs=vmem,
        out_shape=jax.ShapeDtypeStruct((blocks * rows, heads * HEAD), jnp.bfloat16),
        scratch_shapes=[pltpu.VMEM((blocks * heads * rows, HEAD), jnp.float32)] * 3,
        compiler_params=pltpu.CompilerParams(vmem_limit_bytes=VMEM_LIMIT),
        cost_estimate=pl.CostEstimate(
            flops=scores * HEAD * 8, bytes_accessed=2 * kv.size, transcendentals=scores
        ),
    )(ids, offsets, query, kv)


def per_device(hidden_in, gain, positions, w_query, w_key, w_value, w_out, *, n_ctx):
    widened = hidden_in.astype(jnp.float32)
    scale_rows = lax.rsqrt(jnp.mean(widened * widened, axis=-1, keepdims=True) + EPS)
    normed = (widened * scale_rows * gain.astype(jnp.float32)).astype(jnp.bfloat16)
    piece = lax.all_gather(normed, "tp", axis=0, tiled=True)
    cosine, sine = rope_tables(positions)

    ids = positions[::SPAN] // SPAN
    known = ids
    reach = 1
    while reach < n_ctx:
        shift = [(i, (i + reach) % n_ctx) for i in range(n_ctx)]
        known = jnp.concatenate([known, lax.ppermute(known, "ctx", shift)])
        reach *= 2
    owner = (lax.axis_index("ctx") - jnp.arange(n_ctx, dtype=jnp.int32)) % n_ctx
    at = (owner[:, None] * 2 + jnp.arange(2, dtype=jnp.int32)[None, :]).reshape(-1) * SPAN
    slots = jnp.arange(2 * n_ctx, dtype=jnp.int32)
    offsets = jnp.sum(jnp.where(known[:, None] == slots[None, :], at[:, None], 0), axis=0)

    piece, cosine, sine, offsets = lax.optimization_barrier((piece, cosine, sine, offsets))
    query, kv = project(piece, w_query, w_key, w_value, cosine, sine)
    kv = lax.all_gather(kv, "ctx", axis=0, tiled=True)
    terms = []
    for part in range(PARTS):
        mixed = attend(ids, offsets, query[part], kv, part)
        term = jnp.dot(mixed, w_out, preferred_element_type=jnp.float32).astype(jnp.bfloat16)
        terms.append(lax.psum_scatter(term, "tp", scatter_dimension=0, tiled=True))
    summed = jnp.concatenate(terms, axis=0).astype(jnp.float32)
    return (widened + summed).astype(jnp.bfloat16)


def solution(mesh):
    rows = P(("ctx", "tp"), None)
    in_specs = (
        rows, P(), P("ctx"), P(None, "tp"), P(None, "tp"), P(None, "tp"), P("tp", None),
    )
    return jax.shard_map(
        functools.partial(per_device, n_ctx=mesh.shape["ctx"]),
        mesh=mesh, in_specs=in_specs, out_specs=rows, check_vma=False,
    )
```

time: 854 us -> 399 us (0.47)
  matrix products: 352 us -> 10.7 us
  other arithmetic: 187 us -> 11.4 us
  Pallas kernels: 0 us -> 65.2 us
  waiting for transfers between devices: 255 us -> 289 us
  local copies, waits for them, and re-layouts: 22.9 us -> 2.55 us
  blocking collectives: 20.3 us -> 0 us
    dot_general x68 -> x2, matrix products: 352 us -> 10.7 us  [per_device(): jnp.dot(mixed, w_out, preferred_element_type=jnp.float32)]
    reduce_sum x32 -> x1, other arithmetic: 172 us -> 0.68 us  [per_device(): jnp.sum(jnp.where(known[:, None] == slots[None, :], at[:, None], 0), axis=0)]
    pallas_call x0 -> x3, Pallas kernels: none -> 65.2 us  [the longest x2 50.8 us: attend(): pl.pallas_call(functools.partial(attend_kernel, part=part, heads=heads, p...]
    reduce_scatter x1 -> x2, waiting for transfers between devices: 114 us -> 141 us  [per_device(): terms.append(lax.psum_scatter(term, 'tp', scatter_dimension=0, tiled=True))]
    all_gather x1 -> x0, blocking collectives: 20.3 us -> none  [per_device(): pos_piece = lax.all_gather(positions, 'ctx', axis=0, tiled=True)]
    all_gather x1, waiting for transfers between devices: 110 us -> 91 us  [per_device(): piece = lax.all_gather(normed, 'tp', axis=0, tiled=True)]
    all_gather x2 -> x1, waiting for transfers between devices: 30.7 us -> 48.3 us  [per_device(): kv = lax.all_gather(kv, 'ctx', axis=0, tiled=True)]
    while x160 -> x0, local copies, waits for them, and re-layouts: 12.9 us -> none
  transfers between devices with their start and end apart: 4 -> 8, of which waited for: 3 -> 7; matrix products, arithmetic and copies ran while one was open for 3% -> 3% of each run, Pallas kernels for 0% -> 6%
where the time goes in v1:
time: 399 us; the launch traced here: 398 us
  waiting for transfers between devices  289 us (72%)
  Pallas kernels  65.2 us (16%)
  between operations  13.2 us (3%)
  other arithmetic  11.4 us (3%)
  matrix products  10.7 us (3%)
  starting transfers between devices  5.86 us (1%)
    reduce_scatter x2, waiting for transfers between devices, per_device(): terms.append(lax.psum_scatter(term, 'tp', scatter_dimension=0, tiled=True))  141 us
    all_gather x1, waiting for transfers between devices, per_device(): piece = lax.all_gather(normed, 'tp', axis=0, tiled=True)  91 us
    pallas_call x2, Pallas kernels, attend(): pl.pallas_call(functools.partial(attend_kernel, part=part, heads=heads, p...  50.8 us
    all_gather x1, waiting for transfers between devices, per_device(): kv = lax.all_gather(kv, 'ctx', axis=0, tiled=True)  48.3 us
    pallas_call x1, Pallas kernels, project(): pl.pallas_call(project_kernel, grid=(count // step,), in_specs=[pl.BlockS...  14.3 us
    dot_general x2, matrix products, per_device(): jnp.dot(mixed, w_out, preferred_element_type=jnp.float32)  10.7 us
    ppermute x4, waiting for transfers between devices, per_device(): known = jnp.concatenate([known, lax.ppermute(known, 'ctx', shift)])  9.15 us
  transfers between devices with their start and end apart: 8, of which 7 were waited for; matrix products, arithmetic and copies ran while one was open for 3% of the time, Pallas kernels for 6%

profile of v1, /device:TPU:1, one launch (start us, length us, event | category | flops | bytes accessed | tf_op | source)
XLA Modules:
  0.0 398.3 jit_solution(11345247863373274375)
XLA Ops:
  6.5 1.5 fusion
  8.1 0.7 convert_element_type.25
  8.8 2.5 fusion.2
  11.5 2.7 collective-permute-start
  14.2 1.9 fusion.4
  16.1 1.3 pad_maximum_fusion
  17.6 1.2 collective-permute-start.1
  18.8 3.3 collective-permute-done.1
  22.1 0.3 collective-permute-start.2
  22.5 4.5 %collective-permute-done.2 = s32[8]{0:T(128)S(1)} collective-permute-done((s32[8]{0:T(128)S(1)}, s32[8]{0:T(128)S(1)}, u32[]{:S(2)}, u32[]{:S(2)}) %collective-permute-start.2) | collective-permute-done | bytes 64 | tf_op jit(solution)/shard_map/ppermute | solution.py:200
  27.0 1.3 collective-permute-start.3
  28.4 1.4 collective-permute-done.3
  29.9 0.7 select_reduce_fusion.off_ref
  30.6 91.0 %all-gather.3.cloned.1.call-done.x_ref = bf16[1024,4096]{1,0:T(8,128)(2,1)} async-done(((bf16[128,4096]{1,0:T(8,128)(2,1)}), bf16[1024,4096]{1,0:T(8,128)(2,1)}) %all-gather.3.cloned.1.call-update) | async-done | bytes 8388624 | tf_op jit(solution)/shard_map/all_gather | solution.py:192
  121.6 14.3 %shard_map.73 = (bf16[2,2,4,256,128]{4,3,2,1,0:T(8,128)(2,1)}, bf16[1024,256]{1,0:T(8,128)(2,1)}) custom-call(bf16[1024,4096]{1,0:T(8,128)(2,1)} %all-gather.3.cloned.1.call-done.x_ref, bf16[4096,512]{1,0:T(8,128)(2,1)} %wq_ref.1, bf16[4096,128]{1,0:T(8,128)(2,1)} %wk_ref.1, bf16[4096,128]{1,0:T(8,128)(2,1)} %wv_ref.1, ...), custom_call_target="tpu_custom_call" | custom-call | flops 6442450944 | bytes 14680064 | tf_op jit(solution)/shard_map/pallas_call | solution.py:68
  136.2 2.3 fusion.7
  138.4 48.3 %all-gather.5.cloned.1.call-done.kv_ref = bf16[16384,256]{1,0:T(8,128)(2,1)} async-done(((bf16[1024,256]{1,0:T(8,128)(2,1)}), bf16[16384,256]{1,0:T(8,128)(2,1)}) %all-gather.5.cloned.1.call-update) | async-done | bytes 8388624 | tf_op jit(solution)/shard_map/all_gather | solution.py:209
  186.7 25.2 %shard_map.74 = bf16[512,512]{1,0:T(8,128)(2,1)} custom-call(s32[2]{0:T(128)} %copy-done.1, s32[32]{0:T(128)} %select_reduce_fusion.off_ref, bf16[2048,128]{1,0:T(8,128)(2,1)} %bitcast.7, bf16[16384,256]{1,0:T(8,128)(2,1)} %all-gather.5.cloned.1.call-done.kv_ref), custom_call_target="tpu_custom_call" | custom-call | flops 17716740096 | bytes 8388608 | tf_op jit(solution)/shard_map/pallas_call | solution.py:172
  212.0 5.4 %convolution_convert_fusion.1 = bf16[512,4096]{1,0:T(8,128)(2,1)} fusion(bf16[512,512]{1,0:T(8,128)(2,1)} %shard_map.74, bf16[512,4096]{1,0:T(8,128)(2,1)S(1)} %copy-done.3), kind=kOutput, calls=%fused_computation.1 | convolution fusion | flops 2149580800 | bytes 8912896 | tf_op jit(solution)/shard_map/dot_general | solution.py:213
  217.4 25.6 %shard_map.75 = bf16[512,512]{1,0:T(8,128)(2,1)} custom-call(s32[2]{0:T(128)} %copy-done.1, s32[32]{0:T(128)} %select_reduce_fusion.off_ref, bf16[2048,128]{1,0:T(8,128)(2,1)} %bitcast.6, bf16[16384,256]{1,0:T(8,128)(2,1)} %all-gather.5.cloned.1.call-done.kv_ref), custom_call_target="tpu_custom_call" | custom-call | flops 17716740096 | bytes 8388608 | tf_op jit(solution)/shard_map/pallas_call | solution.py:172
  243.0 5.4 %convolution_convert_fusion = bf16[512,4096]{1,0:T(8,128)(2,1)} fusion(bf16[512,512]{1,0:T(8,128)(2,1)} %shard_map.75, bf16[512,4096]{1,0:T(8,128)(2,1)S(1)} %copy-done.4), kind=kOutput, calls=%fused_computation | convolution fusion | flops 2149580800 | bytes 8912896 | tf_op jit(solution)/shard_map/dot_general | solution.py:213
  248.4 53.3 %reduce-scatter.3.cloned.1.call-done = bf16[64,4096]{1,0:T(8,128)(2,1)} async-done(((bf16[512,4096]{1,0:T(8,128)(2,1)}), bf16[64,4096]{1,0:T(8,128)(2,1)}) %reduce-scatter.3.cloned.1.call-update) | async-done | bytes 524304 | tf_op jit(solution)/shard_map/reduce_scatter | solution.py:214
  301.6 87.7 %reduce-scatter.5.cloned.1.call-done = bf16[64,4096]{1,0:T(8,128)(2,1)} async-done(((bf16[512,4096]{1,0:T(8,128)(2,1)}), bf16[64,4096]{1,0:T(8,128)(2,1)}) %reduce-scatter.5.cloned.1.call-update) | async-done | bytes 524304 | tf_op jit(solution)/shard_map/reduce_scatter | solution.py:214
  389.4 2.4 fusion.3
  (31 shorter events, 1.0 us)
Async XLA Ops:
  6.5 4.8 %copy-start.2 = (s32[1024]{0:T(1024)S(1)}, s32[1024]{0:T(1024)}, u32[]{:S(2)}) copy-start(s32[1024]{0:T(1024)} %param.9) | copy-start | bytes 12292
  6.5 115.0 %all-gather.3.cloned.1.call-start = ((), (), s32[]{:S(2)}) async-start(), calls=%async_computation.2 | async-start | bytes 9437184 | tf_op jit(solution)/shard_map/all_gather | solution.py:192
  11.3 175.4 %all-gather.5.cloned.1.call-start = ((), (), s32[]{:S(2)}) async-start(), calls=%async_computation.3 | async-start | bytes 8912896 | tf_op jit(solution)/shard_map/all_gather | solution.py:209
  11.5 124.4 %copy-start.1 = (s32[2]{0:T(128)}, s32[2]{0:T(128)S(1)}, u32[]{:S(2)}) copy-start(s32[2]{0:T(128)S(1)} %and_select_fusion.1.ids_ref) | copy-start | bytes 28
  11.5 6.0 %collective-permute-start = (s32[2]{0:T(128)S(1)}, s32[2]{0:T(128)S(1)}, u32[]{:S(2)}, u32[]{:S(2)}) collective-permute-start(s32[2]{0:T(128)S(1)} %and_select_fusion.1.ids_ref), channel_id=1, source_target_pairs={{0,8},{8,16},{16,24},{24,32},{32,40},{40,48},{48,56},{56,64},{64,7... | collective-permute-start | bytes 32 | tf_op jit(solution)/shard_map/ppermute | solution.py:200
  17.6 4.5 %collective-permute-start.1 = (s32[4]{0:T(128)S(1)}, s32[4]{0:T(128)S(1)}, u32[]{:S(2)}, u32[]{:S(2)}) collective-permute-start(s32[4]{0:T(128)S(1)} %pad_add_fusion), channel_id=1, source_target_pairs={{0,16},{8,24},{16,32},{24,40},{32,48},{40,56},{48,64},{56,72},{64,... | collective-permute-start | bytes 56 | tf_op jit(solution)/shard_map/ppermute | solution.py:200
  22.1 4.8 %collective-permute-start.2 = (s32[8]{0:T(128)S(1)}, s32[8]{0:T(128)S(1)}, u32[]{:S(2)}, u32[]{:S(2)}) collective-permute-start(s32[8]{0:T(128)S(1)} %pad_add_fusion.1), channel_id=1, source_target_pairs={{0,32},{8,40},{16,48},{24,56},{32,64},{40,72},{48,80},{56,88},{64,... | collective-permute-start | bytes 104 | tf_op jit(solution)/shard_map/ppermute | solution.py:200
  27.0 2.8 collective-permute-start.3
  135.9 165.7 %reduce-scatter.3.cloned.1.call-start = ((), (), s32[]{:S(2)}) async-start(), calls=%async_computation.4 | async-start | bytes 4718592 | tf_op jit(solution)/shard_map/reduce_scatter | solution.py:214
  186.7 25.2 %copy-start.3 = (bf16[512,4096]{1,0:T(8,128)(2,1)S(1)}, bf16[512,4096]{1,0:T(8,128)(2,1)}, u32[]{:S(2)}) copy-start(bf16[512,4096]{1,0:T(8,128)(2,1)} %param.13) | copy-start | bytes 12582916
  217.3 172.1 %reduce-scatter.5.cloned.1.call-start = ((), (), s32[]{:S(2)}) async-start(), calls=%async_computation.5 | async-start | bytes 4718592 | tf_op jit(solution)/shard_map/reduce_scatter | solution.py:214
  217.4 25.6 %copy-start.4 = (bf16[512,4096]{1,0:T(8,128)(2,1)S(1)}, bf16[512,4096]{1,0:T(8,128)(2,1)}, u32[]{:S(2)}) copy-start(bf16[512,4096]{1,0:T(8,128)(2,1)} %param.13) | copy-start | bytes 12582916
  248.4 141.0 %copy-start = (bf16[128,4096]{1,0:T(8,128)(2,1)S(1)}, bf16[128,4096]{1,0:T(8,128)(2,1)}, u32[]{:S(2)}) copy-start(bf16[128,4096]{1,0:T(8,128)(2,1)} %param.7) | copy-start | bytes 3145732
Sparse Core Ops, SparseCore 0:
  11.4 110.0 all-gather.2
  136.1 50.6 all-gather.4
  217.5 84.1 reduce-scatter.2
  305.8 83.5 reduce-scatter.4

commit v2 on v1

v2 whole, which is shorter than its diff:
```python
import functools
import math

import jax
import jax.numpy as jnp
from jax import lax
from jax.experimental import pallas as pl
from jax.experimental.pallas import tpu as pltpu
from jax.sharding import Mesh
from jax.sharding import PartitionSpec as P

HEAD = 128
SPAN = 512
OWNED = 128
EPS = 1e-05
BASE = 500000.0
NEGATIVE = -1e30
PARTS = 2
PIECE = OWNED // PARTS
DIRECT = 64
TAIL = 16
VMEM_LIMIT = 56 * 2**20
SCORE_SCALE = math.log2(math.e) / HEAD**0.5

AXES = ("y_lo", "x", "core", "z", "y_hi")
CTX = AXES[:3]


def turn(x, by):
    return lax.ppermute(x, "z", [(i, (i + by) % 4) for i in range(4)])


def swap(x):
    return lax.ppermute(x, "y_hi", [(0, 1), (1, 0)])


def rope_tables(positions):
    half = HEAD // 2
    freq = BASE ** (-(jnp.arange(half, dtype=jnp.float32) * 2.0 / HEAD))
    angle = positions.astype(jnp.float32)[:, None] * freq[None, :]
    cosine, sine = jnp.cos(angle), jnp.sin(angle)
    return (
        jnp.concatenate([cosine, cosine], axis=1),
        jnp.concatenate([-sine, sine], axis=1),
    )


def start_pieces(piece_refs, groups, x_ref, sems):
    copies = []
    used = 0
    for k, group in enumerate(groups):
        start = k * OWNED
        here = []
        for rows in group:
            copy = pltpu.make_async_copy(
                piece_refs[used], x_ref.at[pl.ds(start, rows)], sems.at[used]
            )
            copy.start()
            here.append(copy)
            used += 1
            start += rows
        copies.append(here)
    return copies


def rope(u, cosine, sine):
    return u * cosine + pltpu.roll(u, HEAD // 2, 1) * sine


def place_of(z, k):
    return lax.rem(z - (0, 1, 3, 2)[k % 4] + 4, 4)


def table_rows(where, side):
    return pl.ds(pl.multiple_of(where * (2 * OWNED) + side * OWNED, OWNED), OWNED)


def project_kv_kernel(*refs, groups, other, tail):
    count = sum(len(group) for group in groups)
    place_ref = refs[0]
    wk_ref, wv_ref, cos_ref, sin_ref = refs[1 + count : 5 + count]
    kv_ref, x_ref, sems = refs[5 + count :]
    z = place_ref[0]
    side = 1 - place_ref[1] if other else place_ref[1]
    copies = start_pieces(refs[1 : 1 + count], groups, x_ref, sems)
    if tail:
        row = lax.broadcasted_iota(jnp.int32, (TAIL, 2 * HEAD), 0)
        ids = jnp.where(row < TAIL // 2, place_ref[2], place_ref[3])
        kv_ref[4 * OWNED :, :] = ids.astype(jnp.float32).astype(jnp.bfloat16)
    for half in range(2):
        for group in copies[2 * half : 2 * half + 2]:
            for copy in group:
                copy.wait()
        x = x_ref[half * 2 * OWNED : (half + 1) * 2 * OWNED, :]
        keys = jnp.dot(x, wk_ref[...], preferred_element_type=jnp.float32)
        values = jnp.dot(x, wv_ref[...], preferred_element_type=jnp.float32)
        for k in range(2):
            where = place_of(z, 2 * half + k)
            at = table_rows(where, side)
            mine = slice(k * OWNED, (k + 1) * OWNED)
            out = pl.ds(pl.multiple_of(where * OWNED, OWNED), OWNED)
            kv_ref[out, :HEAD] = rope(keys[mine], cos_ref[at, :], sin_ref[at, :]).astype(
                jnp.bfloat16
            )
            kv_ref[out, HEAD:] = values[mine].astype(jnp.bfloat16)


def project_q_kernel(*refs, groups):
    count = sum(len(group) for group in groups)
    place_ref = refs[0]
    wq_ref, cos_ref, sin_ref = refs[1 + count : 4 + count]
    q_ref, x_ref, sems = refs[4 + count :]
    z, side = place_ref[0], place_ref[1]
    copies = start_pieces(refs[1 : 1 + count], groups, x_ref, sems)
    for pair in range(len(groups) // 2):
        for group in copies[2 * pair : 2 * pair + 2]:
            for copy in group:
                copy.wait()
        x = x_ref[pair * 2 * OWNED : (pair + 1) * 2 * OWNED, :]
        query = jnp.dot(x, wq_ref[...], preferred_element_type=jnp.float32)
        for k in range(2):
            other = pair >= 2
            where = place_of(z, 2 * pair + k)
            at = table_rows(where, 1 - side if other else side)
            cosine, sine = cos_ref[at, :], sin_ref[at, :]
            mine = slice(k * OWNED, (k + 1) * OWNED)
            for h in range(query.shape[1] // HEAD):
                turned = rope(query[mine, h * HEAD : (h + 1) * HEAD], cosine, sine)
                turned = (turned * SCORE_SCALE).astype(jnp.bfloat16)
                for part in range(PARTS):
                    q_ref[int(other), part, where, h] = turned[
                        part * PIECE : (part + 1) * PIECE
                    ]


def project(kernel, place, groups, weights, tables, out):
    pieces = [piece for group in groups for piece in group]
    vmem = pl.BlockSpec(memory_space=pltpu.VMEM)
    smem = pl.BlockSpec(memory_space=pltpu.SMEM)
    hbm = pl.BlockSpec(memory_space=pl.ANY)
    width = weights[0].shape[0]
    columns = sum(w.shape[1] for w in weights)
    rows = len(groups) * OWNED
    return pl.pallas_call(
        functools.partial(
            kernel, groups=tuple(tuple(p.shape[0] for p in group) for group in groups)
        ),
        in_specs=[smem] + [hbm] * len(pieces) + [vmem] * (len(weights) + 2),
        out_specs=vmem,
        out_shape=jax.ShapeDtypeStruct(out, jnp.bfloat16),
        scratch_shapes=[
            pltpu.VMEM((rows, width), jnp.bfloat16),
            pltpu.SemaphoreType.DMA((len(pieces),)),
        ],
        compiler_params=pltpu.CompilerParams(vmem_limit_bytes=VMEM_LIMIT),
        cost_estimate=pl.CostEstimate(
            flops=2 * rows * width * columns,
            bytes_accessed=2 * width * (rows + columns),
            transcendentals=0,
        ),
    )(place, *pieces, *weights, *tables)


def attend_pairs(place_ref, off_ref, q_ref, kv_ref, state, tiles, per, heads, pairs, unroll, far):
    max_ref, sum_ref, acc_ref = state
    step = 2 * OWNED
    side = place_ref[1]

    def pair(which, block, masked):
        at = pl.multiple_of(off_ref[int(far), block], 16)
        keys = kv_ref[pl.ds(at, step), :HEAD]
        values = kv_ref[pl.ds(at, step), HEAD:]
        for start, part, other in tiles:
            here = pl.ds(pl.multiple_of(start + which * per, per), per)
            scores = lax.dot_general(
                q_ref[here, :], keys, (((1,), (1,)), ((), ())),
                preferred_element_type=jnp.float32,
            )
            if masked:
                row = lax.broadcasted_iota(jnp.int32, scores.shape, 0)
                row_side = 1 - side if other else side
                row = (
                    (row // (heads * PIECE)) * (2 * OWNED) + row_side * OWNED
                    + part * PIECE + (row & (PIECE - 1))
                )
                col = lax.broadcasted_iota(jnp.int32, scores.shape, 1)
                col_side = 1 - side if far else side
                col = (col // OWNED) * (2 * OWNED) + col_side * OWNED + (col & (OWNED - 1))
                scores = jnp.where(row >= col, scores, NEGATIVE)
            old = max_ref[here, :]
            new = jnp.maximum(old, jnp.max(scores, axis=1, keepdims=True))
            fade = jnp.exp2(old - new)
            weights = jnp.exp2(scores - jnp.concatenate([new] * (step // HEAD), axis=1))
            if masked:
                weights = jnp.where(row >= col, weights, 0.0)
            max_ref[here, :] = new
            added = weights[:, :HEAD]
            for u in range(1, step // HEAD):
                added = added + weights[:, u * HEAD : (u + 1) * HEAD]
            sum_ref[here, :] = sum_ref[here, :] * fade + added
            acc_ref[here, :] = acc_ref[here, :] * fade + jnp.dot(
                weights.astype(jnp.bfloat16), values, preferred_element_type=jnp.float32
            )

    first = place_ref[2]

    def plain(i):
        which = (i >= first).astype(jnp.int32)
        pair(which, i - which * first, False)

    def body(j, carry):
        for u in range(unroll):
            plain(j * unroll + u)
        return carry

    lax.fori_loop(0, pairs // unroll, body, 0)
    for i in range(pairs // unroll * unroll, pairs):
        plain(jnp.int32(i))
    for which in range(2):
        pair(which, place_ref[2 + which], True)


def attend_near_kernel(
    place_ref, off_ref, q_ref, kv_ref, max_ref, sum_ref, acc_ref, *, heads, pairs, unroll
):
    max_ref[...] = jnp.full_like(max_ref, NEGATIVE)
    sum_ref[...] = jnp.zeros_like(sum_ref)
    acc_ref[...] = jnp.zeros_like(acc_ref)
    per = 2 * heads * PIECE
    tiles = [
        ((other * PARTS + part) * 2 * per, part, bool(other))
        for other in range(2) for part in range(PARTS)
    ]
    attend_pairs(
        place_ref, off_ref, q_ref, kv_ref, (max_ref, sum_ref, acc_ref), tiles, per,
        heads, pairs, unroll, False,
    )


def attend_far_kernel(
    place_ref, off_ref, q_ref, kv_ref, max_in, sum_in, acc_in, o_ref,
    max_ref, sum_ref, acc_ref, *, part, other, heads, pairs, unroll,
):
    max_ref[...] = max_in[...]
    sum_ref[...] = sum_in[...]
    acc_ref[...] = acc_in[...]
    per = 2 * heads * PIECE
    attend_pairs(
        place_ref, off_ref, q_ref, kv_ref, (max_ref, sum_ref, acc_ref),
        [(0, part, other)], per, heads, pairs, unroll, True,
    )
    for group in range(4):
        for h in range(heads):
            start = (group * heads + h) * PIECE
            here = slice(start, start + PIECE)
            total = jnp.sum(sum_ref[here, :], axis=1, keepdims=True)
            o_ref[group * PIECE : (group + 1) * PIECE, h * HEAD : (h + 1) * HEAD] = (
                acc_ref[here, :] / total
            ).astype(jnp.bfloat16)


def attend_cost(pairs, rows, kv):
    scores = (pairs + 2) * rows * SPAN // 4
    return pl.CostEstimate(
        flops=scores * HEAD * 8, bytes_accessed=2 * kv.size + 12 * rows * HEAD,
        transcendentals=scores,
    )


def attend_near(place, offsets, query, kv, heads):
    pairs = offsets.shape[1] - 1
    vmem = pl.BlockSpec(memory_space=pltpu.VMEM)
    smem = pl.BlockSpec(memory_space=pltpu.SMEM)
    return pl.pallas_call(
        functools.partial(attend_near_kernel, heads=heads, pairs=pairs, unroll=6),
        in_specs=[smem, smem, vmem, vmem],
        out_specs=[vmem] * 3,
        out_shape=[jax.ShapeDtypeStruct(query.shape, jnp.float32)] * 3,
        compiler_params=pltpu.CompilerParams(vmem_limit_bytes=VMEM_LIMIT),
        cost_estimate=attend_cost(pairs, query.shape[0], kv),
    )(place, offsets, query, kv)


def attend_far(place, offsets, query, kv, state, part, other, heads):
    pairs = offsets.shape[1] - 1
    rows = 4 * heads * PIECE
    which = int(other) * PARTS + part
    chosen = pl.BlockSpec((rows, HEAD), lambda i: (which, 0))
    whole = pl.BlockSpec(kv.shape, lambda i: (0, 0))
    smem = pl.BlockSpec(memory_space=pltpu.SMEM)
    return pl.pallas_call(
        functools.partial(
            attend_far_kernel, part=part, other=other, heads=heads, pairs=pairs,
            unroll=10 if PARTS > 1 else 6,
        ),
        grid=(1,),
        in_specs=[smem, smem, chosen, whole] + [chosen] * 3,
        out_specs=pl.BlockSpec((4 * PIECE, heads * HEAD), lambda i: (0, 0)),
        out_shape=jax.ShapeDtypeStruct((4 * PIECE, heads * HEAD), jnp.bfloat16),
        scratch_shapes=[pltpu.VMEM((rows, HEAD), jnp.float32)] * 3,
        compiler_params=pltpu.CompilerParams(vmem_limit_bytes=VMEM_LIMIT),
        cost_estimate=attend_cost(pairs, rows, kv),
    )(place, offsets, query, kv, *state)


def combine_kernel(mine_ref, theirs_ref, w_mine_ref, w_theirs_ref, out_ref):
    out_ref[...] = (
        jnp.dot(mine_ref[...], w_mine_ref[...], preferred_element_type=jnp.float32)
        + jnp.dot(theirs_ref[...], w_theirs_ref[...], preferred_element_type=jnp.float32)
    ).astype(jnp.bfloat16)


def combine(mine, theirs, w_mine, w_theirs):
    rows, depth = mine.shape
    columns = w_mine.shape[1]
    step = 1024
    whole = lambda i: (0, 0)
    across = lambda i: (0, i)
    return pl.pallas_call(
        combine_kernel,
        grid=(columns // step,),
        in_specs=[
            pl.BlockSpec((rows, depth), whole),
            pl.BlockSpec((rows, depth), whole),
            pl.BlockSpec((depth, step), across),
            pl.BlockSpec((depth, step), across),
        ],
        out_specs=pl.BlockSpec((rows, step), across),
        out_shape=jax.ShapeDtypeStruct((rows, columns), jnp.bfloat16),
        compiler_params=pltpu.CompilerParams(vmem_limit_bytes=VMEM_LIMIT),
        cost_estimate=pl.CostEstimate(
            flops=4 * rows * depth * columns,
            bytes_accessed=4 * depth * columns + 2 * rows * columns,
            transcendentals=0,
        ),
    )(mine, theirs, w_mine, w_theirs)


def per_device(hidden_in, gain, positions, w_query, w_key, w_value, w_out, *, n_ctx):
    ids = positions[::SPAN] // SPAN
    place = jnp.concatenate(
        [jnp.stack([lax.axis_index("z"), lax.axis_index("y_hi")]).astype(jnp.int32), ids]
    )
    slices = 8
    part_rows = w_out.shape[0] // slices
    turn_of = lax.axis_index("x") * 2 + lax.axis_index("core")
    eighth = lax.dynamic_slice_in_dim(w_out, turn_of * part_rows, part_rows, 0)
    eighth = lax.ppermute(eighth, ("y_lo", "y_hi"), [(0, 3), (3, 0), (1, 2), (2, 1)])
    w_theirs = lax.all_gather(eighth, ("x", "core"), axis=0, tiled=True)

    widened = hidden_in.astype(jnp.float32)
    scale_rows = lax.rsqrt(jnp.mean(widened * widened, axis=-1, keepdims=True) + EPS)
    normed = (widened * scale_rows * gain.astype(jnp.float32)).astype(jnp.bfloat16)
    across = swap(normed)
    ahead, behind = turn(normed, 1), turn(normed, 3)
    late, across = lax.optimization_barrier((normed, across))
    near = [normed, ahead, behind, turn(late, 2)]
    crossed = [swap(ahead[DIRECT:]), swap(behind[DIRECT:])]
    tables = rope_tables(positions)
    *near, crossed[0], crossed[1], w_theirs = lax.optimization_barrier(
        (*near, *crossed, w_theirs)
    )
    kv_near = project(
        functools.partial(project_kv_kernel, other=False, tail=True),
        place, [[p] for p in near], (w_key, w_value), tables, (4 * OWNED + TAIL, 2 * HEAD),
    )
    kv_near_all = lax.all_gather(kv_near, CTX, axis=0, tiled=True)
    across, last, kv_near = lax.optimization_barrier((across, near[3], kv_near))
    far = [[across]] + [
        [turn(across[:DIRECT], by), piece]
        for by, piece in zip((1, 3, 2), (*crossed, swap(last[DIRECT:])))
    ]
    kv_far = project(
        functools.partial(project_kv_kernel, other=True, tail=False),
        place, far, (w_key, w_value), tables, (4 * OWNED, 2 * HEAD),
    )
    kv_near = kv_near_all
    kv_far_all = lax.all_gather(kv_far, CTX, axis=0, tiled=True)
    heads = w_query.shape[1] // HEAD
    query = project(
        project_q_kernel, place, [[p] for p in near] + far, (w_query,), tables,
        (2, PARTS, 4, heads, PIECE, HEAD),
    ).reshape(8 * heads * OWNED, HEAD)
    kv_far = kv_far_all

    rows_near = 4 * OWNED + TAIL
    known = kv_near.reshape(n_ctx, rows_near, 2 * HEAD)[:, 4 * OWNED :: TAIL // 2, 0]
    known = known.astype(jnp.int32).reshape(-1)
    owner = jnp.arange(2 * n_ctx, dtype=jnp.int32) // 2
    within = (jnp.arange(2 * n_ctx, dtype=jnp.int32) % 2) * (2 * OWNED)
    at = jnp.stack([owner * rows_near + within, owner * (4 * OWNED) + within])
    slots = jnp.arange(2 * n_ctx, dtype=jnp.int32)
    offsets = jnp.sum(
        jnp.where(known[None, :, None] == slots[None, None, :], at[:, :, None], 0), axis=1
    )

    state = attend_near(place, offsets, query, kv_near, heads)
    terms = []
    for part in range(PARTS):
        sent = attend_far(place, offsets, query, kv_far, state, part, True, heads)
        theirs = swap(sent)
        mine = attend_far(place, offsets, query, kv_far, state, part, False, heads)
        term = combine(mine, theirs, w_out, w_theirs)
        terms.append(lax.psum_scatter(term, "z", scatter_dimension=0, tiled=True))
    summed = jnp.concatenate(terms, axis=0).astype(jnp.float32)
    return (widened + summed).astype(jnp.bfloat16)


def solution(mesh):
    fine = Mesh(mesh.devices.reshape(2, 4, 2, 4, 2), AXES)
    rows = P(AXES, None)
    tp = AXES[3:]
    in_specs = (rows, P(), P(CTX), P(None, tp), P(None, tp), P(None, tp), P(tp, None))
    return jax.shard_map(
        functools.partial(per_device, n_ctx=mesh.shape["ctx"]),
        mesh=fine, in_specs=in_specs, out_specs=rows, check_vma=False,
    )
```

time: 399 us -> 276 us (0.69)
  waiting for transfers between devices: 289 us -> 113 us
  Pallas kernels: 65.2 us -> 105 us
  starting transfers between devices: 5.86 us -> 25.7 us
  matrix products: 10.7 us -> 0 us
  local copies, waits for them, and re-layouts: 2.55 us -> 11.2 us
    all_gather x2 -> x3, waiting for transfers between devices: 139 us -> 26.3 us  [the longest x1 18 us: per_device(): kv_near_all = lax.all_gather(kv_near, CTX, axis=0, tiled=True)]
    reduce_scatter x2, waiting for transfers between devices: 141 us -> 32.6 us  [per_device(): terms.append(lax.psum_scatter(term, 'z', scatter_dimension=0, tiled=True))]
    ppermute x4 -> x13, waiting for transfers between devices: 9.15 us -> 53.6 us  [the longest x6 37.8 us: swap(): return lax.ppermute(x, 'y_hi', [(0, 1), (1, 0)])]
    pallas_call x3 -> x10, Pallas kernels: 65.2 us -> 105 us  [the longest x4 39.7 us: attend_far(): pl.pallas_call(functools.partial(attend_far_kernel, part=part, other=othe...]
    ppermute x4 -> x13, starting transfers between devices: 5.55 us -> 25.6 us  [the longest x6 12.8 us: turn(): return lax.ppermute(x, 'z', [(i, (i + by) % 4) for i in range(4)])]
    dot_general x2 -> x0, matrix products: 10.7 us -> none  [per_device(): jnp.dot(mixed, w_out, preferred_element_type=jnp.float32)]
    unnamed x10 -> x27, local copies, waits for them, and re-layouts: 0.02 us -> 5.07 us
  transfers between devices with their start and end apart: 8 -> 18, of which waited for: 7 -> 10; matrix products, arithmetic and copies ran while one was open for 3% -> 4% of each run, Pallas kernels for 6% -> 30%
where the time goes in v2:
time: 276 us
  waiting for transfers between devices  113 us (41%)
  Pallas kernels  105 us (38%)
  starting transfers between devices  25.7 us (9%)
  between operations  13.3 us (5%)
  local copies, waits for them, and re-layouts  11.2 us (4%)
  other arithmetic  8.37 us (3%)
    pallas_call x4, Pallas kernels, attend_far(): pl.pallas_call(functools.partial(attend_far_kernel, part=part, other=othe...  39.7 us
    ppermute x6, waiting for transfers between devices, swap(): return lax.ppermute(x, 'y_hi', [(0, 1), (1, 0)])  37.8 us
    reduce_scatter x2, waiting for transfers between devices, per_device(): terms.append(lax.psum_scatter(term, 'z', scatter_dimension=0, tiled=True))  32.6 us
    pallas_call x1, Pallas kernels, attend_near(): pl.pallas_call(functools.partial(attend_near_kernel, heads=heads, pairs=p...  27.8 us
    pallas_call x3, Pallas kernels, project(): pl.pallas_call(functools.partial(kernel, groups=tuple((tuple((p.shape[0]...  24 us
    all_gather x1, waiting for transfers between devices, per_device(): kv_near_all = lax.all_gather(kv_near, CTX, axis=0, tiled=True)  18 us
    pallas_call x2, Pallas kernels, combine(): pl.pallas_call(combine_kernel, grid=(columns // step,), in_specs=[pl.Bloc...  13.3 us
    ppermute x6, starting transfers between devices, turn(): return lax.ppermute(x, 'z', [(i, (i + by) % 4) for i in range(4)])  12.8 us
  transfers between devices with their start and end apart: 18, of which 10 were waited for; matrix products, arithmetic and copies ran while one was open for 4% of the time, Pallas kernels for 30%

profile of v2, /device:TPU:1, one launch (start us, length us, event | category | flops | bytes accessed | tf_op | source)
XLA Modules:
  0.0 275.9 jit_solution(7878746171172796025)
XLA Ops:
  7.7 3.6 %collective-permute-start.6 = (bf16[64,4096]{1,0:T(8,128)(2,1)S(1)}, bf16[64,4096]{1,0:T(8,128)(2,1)S(1)}, u32[]{:S(2)}, u32[]{:S(2)}) collective-permute-start(bf16[64,4096]{1,0:T(8,128)(2,1)S(1)} %constant_dynamic-slice_fusion), channel_id=1, source_target_pairs={{0,65},{65,0},{1,64},{64,1},{2,67},{67,2},{3,66},{66,3},{4,69},{69... | collective-permute-start | bytes 1572872 | tf_op jit(solution)/shard_map/ppermute | solution.py:348
  11.4 11.5 %collective-permute-done.6 = bf16[64,4096]{1,0:T(8,128)(2,1)S(1)} collective-permute-done((bf16[64,4096]{1,0:T(8,128)(2,1)S(1)}, bf16[64,4096]{1,0:T(8,128)(2,1)S(1)}, u32[]{:S(2)}, u32[]{:S(2)}) %collective-permute-start.6) | collective-permute-done | bytes 524320 | tf_op jit(solution)/shard_map/ppermute | solution.py:348
  26.7 3.8 %collective-permute-start.1 = (bf16[128,4096]{1,0:T(8,128)(2,1)S(1)}, bf16[128,4096]{1,0:T(8,128)(2,1)S(1)}, u32[]{:S(2)}, u32[]{:S(2)}) collective-permute-start(bf16[128,4096]{1,0:T(8,128)(2,1)S(1)} %fusion.2.refs_1_), channel_id=1, source_target_pairs={{0,6},{2,0},{4,2},{6,4},{1,7},{3,1},{5,3},{7,5},{8,14},{10,8},{12,... | collective-permute-start | bytes 3145736 | tf_op jit(solution)/shard_map/ppermute | solution.py:30
  30.4 19.5 %collective-permute-done.2.refs_5_.refs_1_ = bf16[128,4096]{1,0:T(8,128)(2,1)S(1)} collective-permute-done((bf16[128,4096]{1,0:T(8,128)(2,1)S(1)}, bf16[128,4096]{1,0:T(8,128)(2,1)S(1)}, u32[]{:S(2)}, u32[]{:S(2)}) %collective-permute-start.2) | collective-permute-done | bytes 1048608 | tf_op jit(solution)/shard_map/ppermute | solution.py:34
  51.0 3.4 %collective-permute-start.3 = (bf16[128,4096]{1,0:T(8,128)(2,1)S(1)}, bf16[128,4096]{1,0:T(8,128)(2,1)}, u32[]{:S(2)}, u32[]{:S(2)}) collective-permute-start(bf16[128,4096]{1,0:T(8,128)(2,1)S(1)} %fusion.2.refs_1_), channel_id=1, source_target_pairs={{0,4},{2,6},{4,0},{6,2},{1,5},{3,7},{5,1},{7,3},{8,12},{10,14},{12... | collective-permute-start | bytes 3145736 | tf_op jit(solution)/shard_map/ppermute | solution.py:30
  64.1 3.9 %collective-permute-done.5.refs_9_.refs_5_ = bf16[64,4096]{1,0:T(8,128)(2,1)} collective-permute-done((bf16[64,4096]{1,0:T(8,128)(2,1)}, bf16[64,4096]{1,0:T(8,128)(2,1)}, u32[]{:S(2)}, u32[]{:S(2)}) %collective-permute-start.5) | collective-permute-done | bytes 524320 | tf_op jit(solution)/shard_map/ppermute | solution.py:34
  67.9 8.8 %collective-permute-done.4.refs_7_.refs_3_ = bf16[64,4096]{1,0:T(8,128)(2,1)} collective-permute-done((bf16[64,4096]{1,0:T(8,128)(2,1)}, bf16[64,4096]{1,0:T(8,128)(2,1)}, u32[]{:S(2)}, u32[]{:S(2)}) %collective-permute-start.4) | collective-permute-done | bytes 524320 | tf_op jit(solution)/shard_map/ppermute | solution.py:34
  76.8 6.7 %shard_map.73 = bf16[528,256]{1,0:T(8,128)(2,1)} custom-call(s32[4]{0:T(128)} %pad_add_fusion.1.refs_0_.place_ref, bf16[128,4096]{1,0:T(8,128)(2,1)} %copy-done.1, bf16[128,4096]{1,0:T(8,128)(2,1)} %collective-permute-done.refs_2_, bf16[128,4096]{1,0:T(8,128)(2,1)} %copy-done.2, bf16[128,4096]{1,0:T(8,128)(2,1)} %collective-permute-done.3.refs_4_, ...), custom_call_target="tpu_custom_call" | custom-call | flops 1073741824 | bytes 6291456 | tf_op jit(solution)/shard_map/pallas_call | solution.py:144
  86.4 2.7 collective-permute-start.9
  89.1 2.8 %collective-permute-start.8 = (bf16[64,4096]{1,0:T(8,128)(2,1)S(1)}, bf16[64,4096]{1,0:T(8,128)(2,1)S(1)}, u32[]{:S(2)}, u32[]{:S(2)}) collective-permute-start(bf16[64,4096]{1,0:T(8,128)(2,1)S(1)} %slice.24), channel_id=1, source_target_pairs={{0,6},{2,0},{4,2},{6,4},{1,7},{3,1},{5,3},{7,5},{8,14},{10,8},{12,... | collective-permute-start | bytes 1572872 | tf_op jit(solution)/shard_map/ppermute | solution.py:30
  91.9 5.5 %collective-permute-done.10.refs_11_.refs_7_ = bf16[64,4096]{1,0:T(8,128)(2,1)S(1)} collective-permute-done((bf16[64,4096]{1,0:T(8,128)(2,1)S(1)}, bf16[64,4096]{1,0:T(8,128)(2,1)S(1)}, u32[]{:S(2)}, u32[]{:S(2)}) %collective-permute-start.10) | collective-permute-done | bytes 524320 | tf_op jit(solution)/shard_map/ppermute | solution.py:34
  97.5 4.3 %collective-permute-done.8.refs_8_.refs_4_ = bf16[64,4096]{1,0:T(8,128)(2,1)S(1)} collective-permute-done((bf16[64,4096]{1,0:T(8,128)(2,1)S(1)}, bf16[64,4096]{1,0:T(8,128)(2,1)S(1)}, u32[]{:S(2)}, u32[]{:S(2)}) %collective-permute-start.8) | collective-permute-done | bytes 524320 | tf_op jit(solution)/shard_map/ppermute | solution.py:30
  103.4 6.6 %shard_map.75 = bf16[512,256]{1,0:T(8,128)(2,1)} custom-call(s32[4]{0:T(128)} %pad_add_fusion.1.refs_0_.place_ref, bf16[128,4096]{1,0:T(8,128)(2,1)} %copy-done.3, bf16[64,4096]{1,0:T(8,128)(2,1)} %copy-done.9, bf16[64,4096]{1,0:T(8,128)(2,1)} %collective-permute-done.4.refs_7_.refs_3_, bf16[64,4096]{1,0:T(8,128)(2,1)} %copy-done.8, ...), custom_call_target="tpu_custom_call" | custom-call | flops 1073741824 | bytes 6291456 | tf_op jit(solution)/shard_map/pallas_call | solution.py:144
  110.1 10.7 %shard_map.74 = bf16[2,2,4,4,64,128]{5,4,3,2,1,0:T(8,128)(2,1)} custom-call(s32[4]{0:T(128)} %pad_add_fusion.1.refs_0_.place_ref, bf16[128,4096]{1,0:T(8,128)(2,1)} %copy-done.1, bf16[128,4096]{1,0:T(8,128)(2,1)} %collective-permute-done.refs_2_, bf16[128,4096]{1,0:T(8,128)(2,1)} %copy-done.2, bf16[128,4096]{1,0:T(8,128)(2,1)} %collective-permute-done.3.refs_4_, ...), custom_call_target="tpu_custom_call" | custom-call | flops 4294967296 | bytes 12582912 | tf_op jit(solution)/shard_map/pallas_call | solution.py:144
  120.8 18.0 %all-gather.6.cloned.1.call-done.kv_ref = bf16[8448,256]{1,0:T(8,128)(2,1)} async-done(((bf16[528,256]{1,0:T(8,128)(2,1)}), bf16[8448,256]{1,0:T(8,128)(2,1)}) %all-gather.6.cloned.1.call-update) | async-done | bytes 4325392 | tf_op jit(solution)/shard_map/all_gather | solution.py:367
  140.7 27.8 %shard_map.76 = (f32[4096,128]{1,0:T(8,128)}, f32[4096,128]{1,0:T(8,128)}, f32[4096,128]{1,0:T(8,128)}) custom-call(s32[4]{0:T(128)} %pad_add_fusion.1.refs_0_.place_ref, s32[2,32]{1,0:T(2,128)} %select_reduce_fusion.off_ref, bf16[4096,128]{1,0:T(8,128)(2,1)} %bitcast.7, bf16[8448,256]{1,0:T(8,128)(2,1)} %all-gather.6.cloned.1.call-done.kv_ref), custom_call_target="tpu_custom_call" | custom-call | flops 17716740096 | bytes 10616832 | tf_op jit(solution)/shard_map/pallas_call | solution.py:274
  168.4 8.3 %all-gather.8.cloned.1.call-done.kv_ref = bf16[8192,256]{1,0:T(8,128)(2,1)} async-done(((bf16[512,256]{1,0:T(8,128)(2,1)}), bf16[8192,256]{1,0:T(8,128)(2,1)}) %all-gather.8.cloned.1.call-update) | async-done | bytes 4194320 | tf_op jit(solution)/shard_map/all_gather | solution.py:378
  176.7 9.8 %shard_map.78 = bf16[256,512]{1,0:T(8,128)(2,1)} custom-call(s32[4]{0:T(128)} %pad_add_fusion.1.refs_0_.place_ref, s32[2,32]{1,0:T(2,128)} %select_reduce_fusion.off_ref, bf16[4096,128]{1,0:T(8,128)(2,1)} %bitcast.8, bf16[8192,256]{1,0:T(8,128)(2,1)} %all-gather.8.cloned.1.call-done.kv_ref, f32[4096,128]{1,0:T(8,128)} %get-tuple-element.29.max_in, ...), custom_call_target="tpu_custom_call" | custom-call | flops 4429185024 | bytes 5767168 | tf_op jit(solution)/shard_map/pallas_call | solution.py:291
  189.1 10.1 %shard_map.77.mine_ref = bf16[256,512]{1,0:T(8,128)(2,1)} custom-call(s32[4]{0:T(128)} %pad_add_fusion.1.refs_0_.place_ref, s32[2,32]{1,0:T(2,128)} %select_reduce_fusion.off_ref, bf16[4096,128]{1,0:T(8,128)(2,1)} %bitcast.9, bf16[8192,256]{1,0:T(8,128)(2,1)} %all-gather.8.cloned.1.call-done.kv_ref, f32[4096,128]{1,0:T(8,128)} %get-tuple-element.29.max_in, ...), custom_call_target="tpu_custom_call" | custom-call | flops 4429185024 | bytes 5767168 | tf_op jit(solution)/shard_map/pallas_call | solution.py:291
  199.9 6.6 %shard_map.79 = bf16[256,4096]{1,0:T(8,128)(2,1)} custom-call(bf16[256,512]{1,0:T(8,128)(2,1)} %shard_map.77.mine_ref, bf16[256,512]{1,0:T(8,128)(2,1)} %copy-done.11, bf16[512,4096]{1,0:T(8,128)(2,1)} %w_mine_ref.3, bf16[512,4096]{1,0:T(8,128)(2,1)} %all-gather.4.cloned.1.call-done.w_theirs_ref), custom_call_target="tpu_custom_call" | custom-call | flops 2147483648 | bytes 10485760 | tf_op jit(solution)/shard_map/pallas_call | solution.py:319
  206.6 9.9 %shard_map.81 = bf16[256,512]{1,0:T(8,128)(2,1)} custom-call(s32[4]{0:T(128)} %pad_add_fusion.1.refs_0_.place_ref, s32[2,32]{1,0:T(2,128)} %select_reduce_fusion.off_ref, bf16[4096,128]{1,0:T(8,128)(2,1)} %bitcast.10, bf16[8192,256]{1,0:T(8,128)(2,1)} %all-gather.8.cloned.1.call-done.kv_ref, f32[4096,128]{1,0:T(8,128)} %get-tuple-element.29.max_in, ...), custom_call_target="tpu_custom_call" | custom-call | flops 4429185024 | bytes 5767168 | tf_op jit(solution)/shard_map/pallas_call | solution.py:291
  217.0 9.9 %shard_map.80.mine_ref = bf16[256,512]{1,0:T(8,128)(2,1)} custom-call(s32[4]{0:T(128)} %pad_add_fusion.1.refs_0_.place_ref, s32[2,32]{1,0:T(2,128)} %select_reduce_fusion.off_ref, bf16[4096,128]{1,0:T(8,128)(2,1)} %bitcast.11, bf16[8192,256]{1,0:T(8,128)(2,1)} %all-gather.8.cloned.1.call-done.kv_ref, f32[4096,128]{1,0:T(8,128)} %get-tuple-element.29.max_in, ...), custom_call_target="tpu_custom_call" | custom-call | flops 4429185024 | bytes 5767168 | tf_op jit(solution)/shard_map/pallas_call | solution.py:291
  227.6 6.7 %shard_map.82 = bf16[256,4096]{1,0:T(8,128)(2,1)} custom-call(bf16[256,512]{1,0:T(8,128)(2,1)} %shard_map.80.mine_ref, bf16[256,512]{1,0:T(8,128)(2,1)} %copy-done.10, bf16[512,4096]{1,0:T(8,128)(2,1)} %w_mine_ref.3, bf16[512,4096]{1,0:T(8,128)(2,1)} %all-gather.4.cloned.1.call-done.w_theirs_ref), custom_call_target="tpu_custom_call" | custom-call | flops 2147483648 | bytes 10485760 | tf_op jit(solution)/shard_map/pallas_call | solution.py:319
  235.1 31.9 %reduce-scatter.5.cloned.1.call-done = bf16[64,4096]{1,0:T(8,128)(2,1)} async-done(((bf16[256,4096]{1,0:T(8,128)(2,1)}), bf16[64,4096]{1,0:T(8,128)(2,1)}) %reduce-scatter.5.cloned.1.call-update) | async-done | bytes 524304 | tf_op jit(solution)/shard_map/reduce_scatter | solution.py:404
  (78 shorter events, 29.7 us)
Async XLA Ops:
  6.5 17.9 %copy-start = (bf16[128,4096]{1,0:T(8,128)(2,1)S(1)}, bf16[128,4096]{1,0:T(8,128)(2,1)}, u32[]{:S(2)}) copy-start(bf16[128,4096]{1,0:T(8,128)(2,1)} %param.7) | copy-start | bytes 3145732
  6.5 70.2 %all-gather.4.cloned.1.call-start = ((), (), s32[]{:S(2)}) async-start(), calls=%async_computation.2 | async-start | bytes 4718592 | tf_op jit(solution)/shard_map/all_gather | solution.py:349
  7.7 46.7 %copy-start.12 = (s32[1024]{0:T(1024)S(1)}, s32[1024]{0:T(1024)}, u32[]{:S(2)}) copy-start(s32[1024]{0:T(1024)} %param.9) | copy-start | bytes 12292
  7.7 15.1 %collective-permute-start.6 = (bf16[64,4096]{1,0:T(8,128)(2,1)S(1)}, bf16[64,4096]{1,0:T(8,128)(2,1)S(1)}, u32[]{:S(2)}, u32[]{:S(2)}) collective-permute-start(bf16[64,4096]{1,0:T(8,128)(2,1)S(1)} %constant_dynamic-slice_fusion), channel_id=1, source_target_pairs={{0,65},{65,0},{1,64},{64,1},{2,67},{67,2},{3,66},{66,3},{4,69},{69... | collective-permute-start | bytes 1572872 | tf_op jit(solution)/shard_map/ppermute | solution.py:348
  23.7 115.0 %all-gather.6.cloned.1.call-start = ((), (), s32[]{:S(2)}) async-start(), calls=%async_computation.3 | async-start | bytes 4595712 | tf_op jit(solution)/shard_map/all_gather | solution.py:367
  25.1 38.9 %copy-start.1 = (bf16[128,4096]{1,0:T(8,128)(2,1)}, bf16[128,4096]{1,0:T(8,128)(2,1)S(1)}, u32[]{:S(2)}) copy-start(bf16[128,4096]{1,0:T(8,128)(2,1)S(1)} %fusion.2.refs_1_) | copy-start | bytes 3145732
  25.1 24.9 %collective-permute-start.2 = (bf16[128,4096]{1,0:T(8,128)(2,1)S(1)}, bf16[128,4096]{1,0:T(8,128)(2,1)S(1)}, u32[]{:S(2)}, u32[]{:S(2)}) collective-permute-start(bf16[128,4096]{1,0:T(8,128)(2,1)S(1)} %fusion.2.refs_1_), channel_id=1, source_target_pairs={{0,1},{1,0},{2,3},{3,2},{4,5},{5,4},{6,7},{7,6},{8,9},{9,8},{10,11... | collective-permute-start | bytes 3145736 | tf_op jit(solution)/shard_map/ppermute | solution.py:34
  26.7 27.8 %collective-permute-start.1 = (bf16[128,4096]{1,0:T(8,128)(2,1)S(1)}, bf16[128,4096]{1,0:T(8,128)(2,1)S(1)}, u32[]{:S(2)}, u32[]{:S(2)}) collective-permute-start(bf16[128,4096]{1,0:T(8,128)(2,1)S(1)} %fusion.2.refs_1_), channel_id=1, source_target_pairs={{0,6},{2,0},{4,2},{6,4},{1,7},{3,1},{5,3},{7,5},{8,14},{10,8},{12,... | collective-permute-start | bytes 3145736 | tf_op jit(solution)/shard_map/ppermute | solution.py:30
  30.4 26.5 %collective-permute-start = (bf16[128,4096]{1,0:T(8,128)(2,1)S(1)}, bf16[128,4096]{1,0:T(8,128)(2,1)}, u32[]{:S(2)}, u32[]{:S(2)}) collective-permute-start(bf16[128,4096]{1,0:T(8,128)(2,1)S(1)} %fusion.2.refs_1_), channel_id=1, source_target_pairs={{0,2},{2,4},{4,6},{6,0},{1,3},{3,5},{5,7},{7,1},{8,10},{10,12},{12... | collective-permute-start | bytes 3145736 | tf_op jit(solution)/shard_map/ppermute | solution.py:30
  51.0 25.8 %collective-permute-start.3 = (bf16[128,4096]{1,0:T(8,128)(2,1)S(1)}, bf16[128,4096]{1,0:T(8,128)(2,1)}, u32[]{:S(2)}, u32[]{:S(2)}) collective-permute-start(bf16[128,4096]{1,0:T(8,128)(2,1)S(1)} %fusion.2.refs_1_), channel_id=1, source_target_pairs={{0,4},{2,6},{4,0},{6,2},{1,5},{3,7},{5,1},{7,3},{8,12},{10,14},{12... | collective-permute-start | bytes 3145736 | tf_op jit(solution)/shard_map/ppermute | solution.py:30
  54.5 9.6 %copy-start.2 = (bf16[128,4096]{1,0:T(8,128)(2,1)}, bf16[128,4096]{1,0:T(8,128)(2,1)S(1)}, u32[]{:S(2)}) copy-start(bf16[128,4096]{1,0:T(8,128)(2,1)S(1)} %collective-permute-done.1.refs_3_) | copy-start | bytes 3145732
  55.4 12.6 %collective-permute-start.5 = (bf16[64,4096]{1,0:T(8,128)(2,1)}, bf16[64,4096]{1,0:T(8,128)(2,1)}, u32[]{:S(2)}, u32[]{:S(2)}) collective-permute-start(bf16[64,4096]{1,0:T(8,128)(2,1)} %slice.27), channel_id=1, source_target_pairs={{0,1},{1,0},{2,3},{3,2},{4,5},{5,4},{6,7},{7,6},{8,9},{9,8},{10,11... | collective-permute-start | bytes 1572872 | tf_op jit(solution)/shard_map/ppermute | solution.py:34
  58.8 17.9 %collective-permute-start.4 = (bf16[64,4096]{1,0:T(8,128)(2,1)}, bf16[64,4096]{1,0:T(8,128)(2,1)}, u32[]{:S(2)}, u32[]{:S(2)}) collective-permute-start(bf16[64,4096]{1,0:T(8,128)(2,1)} %slice.26), channel_id=1, source_target_pairs={{0,1},{1,0},{2,3},{3,2},{4,5},{5,4},{6,7},{7,6},{8,9},{9,8},{10,11... | collective-permute-start | bytes 1572872 | tf_op jit(solution)/shard_map/ppermute | solution.py:34
  76.8 6.8 %copy-start.4 = (bf16[128,4096]{1,0:T(8,128)(2,1)S(1)}, bf16[128,4096]{1,0:T(8,128)(2,1)}, u32[]{:S(2)}) copy-start(bf16[128,4096]{1,0:T(8,128)(2,1)} %copy-done.3) | copy-start | bytes 3145732
  83.5 93.2 %all-gather.8.cloned.1.call-start = ((), (), s32[]{:S(2)}) async-start(), calls=%async_computation.4 | async-start | bytes 4456448 | tf_op jit(solution)/shard_map/all_gather | solution.py:378
  84.7 12.8 %collective-permute-start.10 = (bf16[64,4096]{1,0:T(8,128)(2,1)S(1)}, bf16[64,4096]{1,0:T(8,128)(2,1)S(1)}, u32[]{:S(2)}, u32[]{:S(2)}) collective-permute-start(bf16[64,4096]{1,0:T(8,128)(2,1)S(1)} %slice.25), channel_id=1, source_target_pairs={{0,1},{1,0},{2,3},{3,2},{4,5},{5,4},{6,7},{7,6},{8,9},{9,8},{10,11... | collective-permute-start | bytes 1572872 | tf_op jit(solution)/shard_map/ppermute | solution.py:34
  86.4 11.1 %collective-permute-start.9 = (bf16[64,4096]{1,0:T(8,128)(2,1)S(1)}, bf16[64,4096]{1,0:T(8,128)(2,1)S(1)}, u32[]{:S(2)}, u32[]{:S(2)}) collective-permute-start(bf16[64,4096]{1,0:T(8,128)(2,1)S(1)} %slice.24), channel_id=1, source_target_pairs={{0,4},{2,6},{4,0},{6,2},{1,5},{3,7},{5,1},{7,3},{8,12},{10,14},{12... | collective-permute-start | bytes 1572872 | tf_op jit(solution)/shard_map/ppermute | solution.py:30
  89.1 12.7 %collective-permute-start.8 = (bf16[64,4096]{1,0:T(8,128)(2,1)S(1)}, bf16[64,4096]{1,0:T(8,128)(2,1)S(1)}, u32[]{:S(2)}, u32[]{:S(2)}) collective-permute-start(bf16[64,4096]{1,0:T(8,128)(2,1)S(1)} %slice.24), channel_id=1, source_target_pairs={{0,6},{2,0},{4,2},{6,4},{1,7},{3,1},{5,3},{7,5},{8,14},{10,8},{12,... | collective-permute-start | bytes 1572872 | tf_op jit(solution)/shard_map/ppermute | solution.py:30
  91.9 9.8 %collective-permute-start.7 = (bf16[64,4096]{1,0:T(8,128)(2,1)S(1)}, bf16[64,4096]{1,0:T(8,128)(2,1)S(1)}, u32[]{:S(2)}, u32[]{:S(2)}) collective-permute-start(bf16[64,4096]{1,0:T(8,128)(2,1)S(1)} %slice.24), channel_id=1, source_target_pairs={{0,2},{2,4},{4,6},{6,0},{1,3},{3,5},{5,7},{7,1},{8,10},{10,12},{12... | collective-permute-start | bytes 1572872 | tf_op jit(solution)/shard_map/ppermute | solution.py:30
  97.5 4.3 %copy-start.6 = (bf16[64,4096]{1,0:T(8,128)(2,1)}, bf16[64,4096]{1,0:T(8,128)(2,1)S(1)}, u32[]{:S(2)}) copy-start(bf16[64,4096]{1,0:T(8,128)(2,1)S(1)} %collective-permute-done.10.refs_11_.refs_7_) | copy-start | bytes 1572868
  110.0 125.0 %reduce-scatter.3.cloned.1.call-start = ((), (), s32[]{:S(2)}) async-start(), calls=%async_computation.5 | async-start | bytes 2621440 | tf_op jit(solution)/shard_map/reduce_scatter | solution.py:404
  186.6 12.6 %collective-permute-start.11 = (bf16[256,512]{1,0:T(8,128)(2,1)}, bf16[256,512]{1,0:T(8,128)(2,1)S(1)}, u32[]{:S(2)}, u32[]{:S(2)}) collective-permute-start(bf16[256,512]{1,0:T(8,128)(2,1)} %shard_map.78), channel_id=1, source_target_pairs={{0,1},{1,0},{2,3},{3,2},{4,5},{5,4},{6,7},{7,6},{8,9},{9,8},{10,11... | collective-permute-start | bytes 786440 | tf_op jit(solution)/shard_map/ppermute | solution.py:34
  206.5 60.4 %reduce-scatter.5.cloned.1.call-start = ((), (), s32[]{:S(2)}) async-start(), calls=%async_computation.6 | async-start | bytes 2621440 | tf_op jit(solution)/shard_map/reduce_scatter | solution.py:404
  216.5 10.4 %collective-permute-start.12 = (bf16[256,512]{1,0:T(8,128)(2,1)}, bf16[256,512]{1,0:T(8,128)(2,1)S(1)}, u32[]{:S(2)}, u32[]{:S(2)}) collective-permute-start(bf16[256,512]{1,0:T(8,128)(2,1)} %shard_map.81), channel_id=1, source_target_pairs={{0,1},{1,0},{2,3},{3,2},{4,5},{5,4},{6,7},{7,6},{8,9},{9,8},{10,11... | collective-permute-start | bytes 786440 | tf_op jit(solution)/shard_map/ppermute | solution.py:34
  (7 other events, 9.1 us)
Sparse Core Ops, SparseCore 0:
  23.8 35.3 all-gather.3
  83.6 55.0 all-gather.5
  140.5 36.2 all-gather.7
  206.6 28.3 reduce-scatter.2
  237.4 29.4 reduce-scatter.4

commit v3 on v2

v3 whole, which is shorter than its diff:
```python
import functools
import math

import jax
import jax.numpy as jnp
from jax import lax
from jax.experimental import pallas as pl
from jax.experimental.pallas import tpu as pltpu
from jax.sharding import Mesh
from jax.sharding import PartitionSpec as P

HEAD = 128
SPAN = 512
OWNED = 128
EPS = 1e-05
BASE = 500000.0
NEGATIVE = -1e30
HALF = OWNED // 2
DIRECT = (64, 96, 80)
TAIL = 16
VMEM_LIMIT = 56 * 2**20
SCORE_SCALE = math.log2(math.e) / HEAD**0.5

AXES = ("y_lo", "x", "core", "z", "y_hi")
CTX = AXES[:3]


def turn(x, by):
    return lax.ppermute(x, "z", [(i, (i + by) % 4) for i in range(4)])


def swap(x):
    return lax.ppermute(x, "y_hi", [(0, 1), (1, 0)])


def rope_tables(positions):
    half = HEAD // 2
    freq = BASE ** (-(jnp.arange(half, dtype=jnp.float32) * 2.0 / HEAD))
    angle = positions.astype(jnp.float32)[:, None] * freq[None, :]
    cosine, sine = jnp.cos(angle), jnp.sin(angle)
    return (
        jnp.concatenate([cosine, cosine], axis=1),
        jnp.concatenate([-sine, sine], axis=1),
    )


def start_pieces(piece_refs, groups, x_ref, sems):
    copies = []
    used = 0
    for k, group in enumerate(groups):
        start = k * OWNED
        here = []
        for rows in group:
            copy = pltpu.make_async_copy(
                piece_refs[used], x_ref.at[pl.ds(start, rows)], sems.at[used]
            )
            copy.start()
            here.append(copy)
            used += 1
            start += rows
        copies.append(here)
    return copies


def rope(u, cosine, sine):
    return u * cosine + pltpu.roll(u, HEAD // 2, 1) * sine


def place_of(z, k):
    return lax.rem(z - (0, 1, 3, 2)[k % 4] + 4, 4)


def table_rows(where, side):
    return pl.ds(pl.multiple_of(where * (2 * OWNED) + side * OWNED, OWNED), OWNED)


def project_kv_kernel(*refs, groups, other, tail):
    count = sum(len(group) for group in groups)
    place_ref = refs[0]
    w_ref, cos_ref, sin_ref = refs[1 + count : 4 + count]
    kv_ref, x_ref, sems = refs[4 + count :]
    z = place_ref[0]
    side = 1 - place_ref[1] if other else place_ref[1]
    copies = start_pieces(refs[1 : 1 + count], groups, x_ref, sems)
    if tail:
        row = lax.broadcasted_iota(jnp.int32, (TAIL, 2 * HEAD), 0)
        ids = jnp.where(row < TAIL // 2, place_ref[2], place_ref[3])
        kv_ref[4 * OWNED :, :] = ids.astype(jnp.float32).astype(jnp.bfloat16)
    for half in range(2):
        for group in copies[2 * half : 2 * half + 2]:
            for copy in group:
                copy.wait()
        x = x_ref[half * 2 * OWNED : (half + 1) * 2 * OWNED, :]
        both = jnp.dot(x, w_ref[...], preferred_element_type=jnp.float32)
        for k in range(2):
            where = place_of(z, 2 * half + k)
            at = table_rows(where, side)
            mine = slice(k * OWNED, (k + 1) * OWNED)
            out = pl.ds(pl.multiple_of(where * OWNED, OWNED), OWNED)
            kv_ref[out, :HEAD] = rope(both[mine, :HEAD], cos_ref[at, :], sin_ref[at, :]).astype(
                jnp.bfloat16
            )
            kv_ref[out, HEAD:] = both[mine, HEAD:].astype(jnp.bfloat16)


def project_q_kernel(*refs, groups, other):
    count = sum(len(group) for group in groups)
    place_ref = refs[0]
    wq_ref, cos_ref, sin_ref = refs[1 + count : 4 + count]
    q_ref, x_ref, sems = refs[4 + count :]
    z = place_ref[0]
    side = 1 - place_ref[1] if other else place_ref[1]
    copies = start_pieces(refs[1 : 1 + count], groups, x_ref, sems)
    for half in range(2):
        for group in copies[2 * half : 2 * half + 2]:
            for copy in group:
                copy.wait()
        x = x_ref[half * 2 * OWNED : (half + 1) * 2 * OWNED, :]
        query = jnp.dot(x, wq_ref[...], preferred_element_type=jnp.float32)
        for k in range(2):
            where = place_of(z, 2 * half + k)
            at = table_rows(where, side)
            cosine, sine = cos_ref[at, :], sin_ref[at, :]
            mine = slice(k * OWNED, (k + 1) * OWNED)
            for h in range(query.shape[1] // HEAD):
                turned = rope(query[mine, h * HEAD : (h + 1) * HEAD], cosine, sine)
                q_ref[where, h] = (turned * SCORE_SCALE).astype(jnp.bfloat16)


def project(kernel, place, groups, weights, tables, out):
    pieces = [piece for group in groups for piece in group]
    vmem = pl.BlockSpec(memory_space=pltpu.VMEM)
    smem = pl.BlockSpec(memory_space=pltpu.SMEM)
    hbm = pl.BlockSpec(memory_space=pl.ANY)
    width = weights[0].shape[0]
    columns = sum(w.shape[1] for w in weights)
    rows = len(groups) * OWNED
    return pl.pallas_call(
        functools.partial(
            kernel, groups=tuple(tuple(p.shape[0] for p in group) for group in groups)
        ),
        in_specs=[smem] + [hbm] * len(pieces) + [vmem] * (len(weights) + 2),
        out_specs=vmem,
        out_shape=jax.ShapeDtypeStruct(out, jnp.bfloat16),
        scratch_shapes=[
            pltpu.VMEM((rows, width), jnp.bfloat16),
            pltpu.SemaphoreType.DMA((len(pieces),)),
        ],
        compiler_params=pltpu.CompilerParams(vmem_limit_bytes=VMEM_LIMIT),
        cost_estimate=pl.CostEstimate(
            flops=2 * rows * width * columns,
            bytes_accessed=2 * width * (rows + columns),
            transcendentals=0,
        ),
    )(place, *pieces, *weights, *tables)


def attend_pairs(place_ref, off_ref, kv_ref, tiles, heads, pairs, unroll, far):
    per = 2 * heads * OWNED
    step = 2 * OWNED
    side = place_ref[1]

    def pair(which, block, masked):
        at = pl.multiple_of(off_ref[int(far), block], 16)
        keys = kv_ref[pl.ds(at, step), :HEAD]
        values = kv_ref[pl.ds(at, step), HEAD:]
        for other, q_ref, max_ref, sum_ref, acc_ref in tiles:
            here = pl.ds(pl.multiple_of(which * per, per), per)
            scores = lax.dot_general(
                q_ref[here, :], keys, (((1,), (1,)), ((), ())),
                preferred_element_type=jnp.float32,
            )
            if masked:
                row = lax.broadcasted_iota(jnp.int32, scores.shape, 0)
                row_side = 1 - side if other else side
                row = (
                    (row // (heads * OWNED)) * (2 * OWNED) + row_side * OWNED
                    + (row & (OWNED - 1))
                )
                col = lax.broadcasted_iota(jnp.int32, scores.shape, 1)
                col_side = 1 - side if far else side
                col = (col // OWNED) * (2 * OWNED) + col_side * OWNED + (col & (OWNED - 1))
                scores = jnp.where(row >= col, scores, NEGATIVE)
            old = max_ref[here, :]
            new = jnp.maximum(old, jnp.max(scores, axis=1, keepdims=True))
            fade = jnp.exp2(old - new)
            weights = jnp.exp2(scores - jnp.concatenate([new] * (step // HEAD), axis=1))
            if masked:
                weights = jnp.where(row >= col, weights, 0.0)
            max_ref[here, :] = new
            added = weights[:, :HEAD]
            for u in range(1, step // HEAD):
                added = added + weights[:, u * HEAD : (u + 1) * HEAD]
            sum_ref[here, :] = sum_ref[here, :] * fade + added
            acc_ref[here, :] = acc_ref[here, :] * fade + jnp.dot(
                weights.astype(jnp.bfloat16), values, preferred_element_type=jnp.float32
            )

    first = place_ref[2]

    def plain(i):
        which = (i >= first).astype(jnp.int32)
        pair(which, i - which * first, False)

    def body(j, carry):
        for u in range(unroll):
            plain(j * unroll + u)
        return carry

    lax.fori_loop(0, pairs // unroll, body, 0)
    for i in range(pairs // unroll * unroll, pairs):
        plain(jnp.int32(i))
    for which in range(2):
        pair(which, place_ref[2 + which], True)


def attend_near_kernel(
    place_ref, off_ref, q_near_ref, q_far_ref, kv_ref, *state_refs, heads, pairs, unroll
):
    for start in range(0, len(state_refs), 3):
        max_ref, sum_ref, acc_ref = state_refs[start : start + 3]
        max_ref[...] = jnp.full_like(max_ref, NEGATIVE)
        sum_ref[...] = jnp.zeros_like(sum_ref)
        acc_ref[...] = jnp.zeros_like(acc_ref)
    tiles = [(True, q_far_ref, *state_refs[3:]), (False, q_near_ref, *state_refs[:3])]
    attend_pairs(place_ref, off_ref, kv_ref, tiles, heads, pairs, unroll, False)


def attend_far_kernel(
    place_ref, off_ref, q_ref, kv_ref, max_in, sum_in, acc_in, o_ref,
    max_ref, sum_ref, acc_ref, *, other, heads, pairs, unroll,
):
    max_ref[...] = max_in[...]
    sum_ref[...] = sum_in[...]
    acc_ref[...] = acc_in[...]
    tiles = [(other, q_ref, max_ref, sum_ref, acc_ref)]
    attend_pairs(place_ref, off_ref, kv_ref, tiles, heads, pairs, unroll, True)
    for group in range(4):
        for h in range(heads):
            start = (group * heads + h) * OWNED
            here = slice(start, start + OWNED)
            total = jnp.sum(sum_ref[here, :], axis=1, keepdims=True)
            o_ref[group * OWNED : (group + 1) * OWNED, h * HEAD : (h + 1) * HEAD] = (
                acc_ref[here, :] / total
            ).astype(jnp.bfloat16)


def attend_cost(pairs, rows, kv):
    scores = (pairs + 2) * rows * SPAN // 4
    return pl.CostEstimate(
        flops=scores * HEAD * 8, bytes_accessed=2 * kv.size + 12 * rows * HEAD,
        transcendentals=scores,
    )


def attend_near(place, offsets, q_near, q_far, kv, heads):
    pairs = offsets.shape[1] - 1
    vmem = pl.BlockSpec(memory_space=pltpu.VMEM)
    smem = pl.BlockSpec(memory_space=pltpu.SMEM)
    return pl.pallas_call(
        functools.partial(attend_near_kernel, heads=heads, pairs=pairs, unroll=6),
        in_specs=[smem, smem, vmem, vmem, vmem],
        out_specs=[vmem] * 6,
        out_shape=[jax.ShapeDtypeStruct(q_near.shape, jnp.float32)] * 6,
        compiler_params=pltpu.CompilerParams(vmem_limit_bytes=VMEM_LIMIT),
        cost_estimate=attend_cost(pairs, 2 * q_near.shape[0], kv),
    )(place, offsets, q_near, q_far, kv)


def attend_far(place, offsets, query, kv, state, other, heads):
    pairs = offsets.shape[1] - 1
    vmem = pl.BlockSpec(memory_space=pltpu.VMEM)
    smem = pl.BlockSpec(memory_space=pltpu.SMEM)
    return pl.pallas_call(
        functools.partial(
            attend_far_kernel, other=other, heads=heads, pairs=pairs, unroll=10
        ),
        in_specs=[smem, smem] + [vmem] * 5,
        out_specs=vmem,
        out_shape=jax.ShapeDtypeStruct((4 * OWNED, heads * HEAD), jnp.bfloat16),
        scratch_shapes=[pltpu.VMEM(query.shape, jnp.float32)] * 3,
        compiler_params=pltpu.CompilerParams(vmem_limit_bytes=VMEM_LIMIT),
        cost_estimate=attend_cost(pairs, query.shape[0], kv),
    )(place, offsets, query, kv, *state)


def combine_kernel(mine_ref, theirs_ref, w_mine_ref, w_theirs_ref, out_ref):
    out_ref[...] = (
        jnp.dot(mine_ref[...], w_mine_ref[...], preferred_element_type=jnp.float32)
        + jnp.dot(theirs_ref[...], w_theirs_ref[...], preferred_element_type=jnp.float32)
    ).astype(jnp.bfloat16)


def combine(mine, theirs, w_mine, w_theirs):
    rows, depth = mine.shape
    columns = w_mine.shape[1]
    step = 512
    whole = lambda i: (0, 0)
    across = lambda i: (0, i)
    return pl.pallas_call(
        combine_kernel,
        grid=(columns // step,),
        in_specs=[
            pl.BlockSpec((rows, depth), whole),
            pl.BlockSpec((rows, depth), whole),
            pl.BlockSpec((depth, step), across),
            pl.BlockSpec((depth, step), across),
        ],
        out_specs=pl.BlockSpec((rows, step), lambda i: (0, i)),
        out_shape=jax.ShapeDtypeStruct((rows, columns), jnp.bfloat16),
        compiler_params=pltpu.CompilerParams(vmem_limit_bytes=VMEM_LIMIT),
        cost_estimate=pl.CostEstimate(
            flops=4 * rows * depth * columns,
            bytes_accessed=4 * depth * columns + 2 * rows * columns,
            transcendentals=0,
        ),
    )(mine, theirs, w_mine, w_theirs)


def per_device(hidden_in, gain, positions, w_query, w_key, w_value, w_out, *, n_ctx):
    ids = positions[::SPAN] // SPAN
    place = jnp.concatenate(
        [jnp.stack([lax.axis_index("z"), lax.axis_index("y_hi")]).astype(jnp.int32), ids]
    )
    widened = hidden_in.astype(jnp.float32)
    scale_rows = lax.rsqrt(jnp.mean(widened * widened, axis=-1, keepdims=True) + EPS)
    normed = (widened * scale_rows * gain.astype(jnp.float32)).astype(jnp.bfloat16)
    across, ahead, behind = lax.optimization_barrier(
        (swap(normed), turn(normed, 1), turn(normed, 3))
    )
    opposite = [turn(ahead[:HALF], 1), turn(behind[HALF:], 3)]
    near = [[normed], [ahead], [behind], opposite]
    crossed = swap(ahead[DIRECT[0] :])
    tables = rope_tables(positions)
    w_kv = jnp.concatenate([w_key, w_value], axis=1)
    near, crossed, w_kv = lax.optimization_barrier((near, crossed, w_kv))
    kv_near = project(
        functools.partial(project_kv_kernel, other=False, tail=True),
        place, near, (w_kv,), tables, (4 * OWNED + TAIL, 2 * HEAD),
    )
    kv_near_all = lax.all_gather(kv_near, CTX, axis=0, tiled=True)
    across, near, kv_near = lax.optimization_barrier((across, near, kv_near))
    far = [
        [across],
        [turn(across[: DIRECT[0]], 1), crossed],
        [turn(across[: DIRECT[1]], 3), swap(near[2][0][DIRECT[1] :])],
        [turn(across[: DIRECT[2]], 2), swap(near[3][1][DIRECT[2] - HALF :])],
    ]
    heads = w_query.shape[1] // HEAD

    def queries(groups, other):
        return project(
            functools.partial(project_q_kernel, other=other),
            place, groups, (w_query,), tables, (4, heads, OWNED, HEAD),
        ).reshape(4 * heads * OWNED, HEAD)

    q_near = queries(near, False)
    far, q_near = lax.optimization_barrier((far, q_near))
    kv_far = project(
        functools.partial(project_kv_kernel, other=True, tail=False),
        place, far, (w_kv,), tables, (4 * OWNED, 2 * HEAD),
    )
    kv_near = kv_near_all
    kv_far_all = lax.all_gather(kv_far, CTX, axis=0, tiled=True)
    q_far = queries(far, True)
    slices = 8
    part_rows = w_out.shape[0] // slices
    turn_of = lax.axis_index("x") * 2 + lax.axis_index("core")
    eighth = lax.dynamic_slice_in_dim(w_out, turn_of * part_rows, part_rows, 0)
    eighth, _ = lax.optimization_barrier((eighth, kv_far))
    eighth = lax.ppermute(eighth, ("y_lo", "y_hi"), [(0, 3), (3, 0), (1, 2), (2, 1)])
    eighth, q_far = lax.optimization_barrier((eighth, q_far))
    kv_far = kv_far_all
    w_theirs = lax.all_gather(eighth, ("x", "core"), axis=0, tiled=True)

    rows_near = 4 * OWNED + TAIL
    known = kv_near.reshape(n_ctx, rows_near, 2 * HEAD)[:, 4 * OWNED :: TAIL // 2, 0]
    known = known.astype(jnp.int32).reshape(-1)
    owner = jnp.arange(2 * n_ctx, dtype=jnp.int32) // 2
    within = (jnp.arange(2 * n_ctx, dtype=jnp.int32) % 2) * (2 * OWNED)
    at = jnp.stack([owner * rows_near + within, owner * (4 * OWNED) + within])
    slots = jnp.arange(2 * n_ctx, dtype=jnp.int32)
    offsets = jnp.sum(
        jnp.where(known[None, :, None] == slots[None, None, :], at[:, :, None], 0), axis=1
    )

    state = attend_near(place, offsets, q_near, q_far, kv_near, heads)
    sent = attend_far(place, offsets, q_far, kv_far, state[3:], True, heads)
    theirs = swap(sent)
    mine = attend_far(place, offsets, q_near, kv_far, state[:3], False, heads)
    term = combine(mine, theirs, w_out, w_theirs)
    summed = lax.psum_scatter(term, "z", scatter_dimension=0, tiled=True)
    return (widened + summed.astype(jnp.float32)).astype(jnp.bfloat16)


def solution(mesh):
    fine = Mesh(mesh.devices.reshape(2, 4, 2, 4, 2), AXES)
    rows = P(AXES, None)
    tp = AXES[3:]
    in_specs = (rows, P(), P(CTX), P(None, tp), P(None, tp), P(None, tp), P(tp, None))
    return jax.shard_map(
        functools.partial(per_device, n_ctx=mesh.shape["ctx"]),
        mesh=fine, in_specs=in_specs, out_specs=rows, check_vma=False,
    )
```

time: 276 us -> 248 us (0.90)
  waiting for transfers between devices: 113 us -> 92.8 us
  Pallas kernels: 105 us -> 97.5 us
  other arithmetic: 8.37 us -> 12.5 us
  local copies, waits for them, and re-layouts: 11.2 us -> 8.4 us
    ppermute x6 -> x7, waiting for transfers between devices: 4.3 us -> 23.3 us  [turn(): return lax.ppermute(x, 'z', [(i, (i + by) % 4) for i in range(4)])]
    ppermute x6 -> x5, waiting for transfers between devices: 37.8 us -> 19.4 us  [swap(): return lax.ppermute(x, 'y_hi', [(0, 1), (1, 0)])]
    all_gather x1, waiting for transfers between devices: 18 us -> 0.02 us  [per_device(): kv_near_all = lax.all_gather(kv_near, CTX, axis=0, tiled=True)]
    reduce_scatter x2 -> x1, waiting for transfers between devices: 32.6 us -> 46.8 us  [per_device(): summed = lax.psum_scatter(term, 'z', scatter_dimension=0, tiled=True)]
    ppermute x1, waiting for transfers between devices: 11.5 us -> 2.92 us  [per_device(): lax.ppermute(eighth, ('y_lo', 'y_hi'), [(0, 3), (3, 0), (1, 2), (2, 1)])]
    pallas_call x4 -> x2, Pallas kernels: 39.7 us -> 31.4 us  [attend_far(): pl.pallas_call(functools.partial(attend_far_kernel, other=other, heads=he...]
    all_gather x1, waiting for transfers between devices: 8.3 us -> 0.12 us  [per_device(): kv_far_all = lax.all_gather(kv_far, CTX, axis=0, tiled=True)]
    pallas_call x3 -> x4, Pallas kernels: 24 us -> 28.8 us  [project(): pl.pallas_call(functools.partial(kernel, groups=tuple((tuple((p.shape[0]...]
  transfers between devices with their start and end apart: 18 -> 17, of which waited for: 10 -> 10; matrix products, arithmetic and copies ran while one was open for 4% -> 4% of each run, Pallas kernels for 30% -> 32%
where the time goes in v3:
time: 248 us
  Pallas kernels  97.5 us (39%)
  waiting for transfers between devices  92.8 us (37%)
  starting transfers between devices  23.1 us (9%)
  between operations  13.3 us (5%)
  other arithmetic  12.5 us (5%)
  local copies, waits for them, and re-layouts  8.4 us (3%)
    reduce_scatter x1, waiting for transfers between devices, per_device(): summed = lax.psum_scatter(term, 'z', scatter_dimension=0, tiled=True)  46.8 us
    pallas_call x2, Pallas kernels, attend_far(): pl.pallas_call(functools.partial(attend_far_kernel, other=other, heads=he...  31.4 us
    pallas_call x4, Pallas kernels, project(): pl.pallas_call(functools.partial(kernel, groups=tuple((tuple((p.shape[0]...  28.8 us
    pallas_call x1, Pallas kernels, attend_near(): pl.pallas_call(functools.partial(attend_near_kernel, heads=heads, pairs=p...  26.9 us
    ppermute x7, waiting for transfers between devices, turn(): return lax.ppermute(x, 'z', [(i, (i + by) % 4) for i in range(4)])  23.3 us
    ppermute x5, waiting for transfers between devices, swap(): return lax.ppermute(x, 'y_hi', [(0, 1), (1, 0)])  19.4 us
    ppermute x7, starting transfers between devices, turn(): return lax.ppermute(x, 'z', [(i, (i + by) % 4) for i in range(4)])  11 us
    pallas_call x1, Pallas kernels, combine(): pl.pallas_call(combine_kernel, grid=(columns // step,), in_specs=[pl.Bloc...  10.4 us
  transfers between devices with their start and end apart: 17, of which 10 were waited for; matrix products, arithmetic and copies ran while one was open for 4% of the time, Pallas kernels for 32%

profile of v3, /device:TPU:1, one launch (start us, length us, event | category | flops | bytes accessed | tf_op | source)
XLA Modules:
  0.0 247.6 jit_solution(10079433218005598948)
XLA Ops:
  10.3 3.8 %collective-permute-start = (bf16[128,4096]{1,0:T(8,128)(2,1)S(1)}, bf16[128,4096]{1,0:T(8,128)(2,1)S(1)}, u32[]{:S(2)}, u32[]{:S(2)}) collective-permute-start(bf16[128,4096]{1,0:T(8,128)(2,1)S(1)} %fusion.2.refs_1_), channel_id=1, source_target_pairs={{0,1},{1,0},{2,3},{3,2},{4,5},{5,4},{6,7},{7,6},{8,9},{9,8},{10,11... | collective-permute-start | bytes 3145736 | tf_op jit(solution)/shard_map/ppermute | solution.py:33
  15.8 2.1 collective-permute-start.2
  18.0 1.9 fusion.4
  21.3 15.5 %collective-permute-done.refs_1_ = bf16[128,4096]{1,0:T(8,128)(2,1)S(1)} collective-permute-done((bf16[128,4096]{1,0:T(8,128)(2,1)S(1)}, bf16[128,4096]{1,0:T(8,128)(2,1)S(1)}, u32[]{:S(2)}, u32[]{:S(2)}) %collective-permute-start) | collective-permute-done | bytes 1048608 | tf_op jit(solution)/shard_map/ppermute | solution.py:33
  36.8 3.7 %collective-permute-done.1.refs_2_ = bf16[128,4096]{1,0:T(8,128)(2,1)S(1)} collective-permute-done((bf16[128,4096]{1,0:T(8,128)(2,1)S(1)}, bf16[128,4096]{1,0:T(8,128)(2,1)S(1)}, u32[]{:S(2)}, u32[]{:S(2)}) %collective-permute-start.1) | collective-permute-done | bytes 1048608 | tf_op jit(solution)/shard_map/ppermute | solution.py:29
  42.6 2.4 collective-permute-start.4
  47.2 6.6 %collective-permute-done.3.refs_4_ = bf16[64,4096]{1,0:T(8,128)(2,1)S(1)} collective-permute-done((bf16[64,4096]{1,0:T(8,128)(2,1)S(1)}, bf16[64,4096]{1,0:T(8,128)(2,1)S(1)}, u32[]{:S(2)}, u32[]{:S(2)}) %collective-permute-start.3) | collective-permute-done | bytes 524320 | tf_op jit(solution)/shard_map/ppermute | solution.py:29
  55.3 6.7 %shard_map.73 = bf16[528,256]{1,0:T(8,128)(2,1)} custom-call(s32[4]{0:T(128)} %pad_add_fusion.1.refs_0_.place_ref, bf16[128,4096]{1,0:T(8,128)(2,1)} %copy-done.1, bf16[128,4096]{1,0:T(8,128)(2,1)} %copy-done.2, bf16[128,4096]{1,0:T(8,128)(2,1)} %collective-permute-done.2.refs_3_, bf16[64,4096]{1,0:T(8,128)(2,1)} %copy-done.8, bf16[64,4096]{1,0:T(8,128)(2,1)} %copy-done.4, ...), custom_call_target="tpu_custom_call" | custom-call | flops 1073741824 | bytes 6291456 | tf_op jit(solution)/shard_map/pallas_call | solution.py:138
  62.2 3.4 %collective-permute-start.7 = (bf16[96,4096]{1,0:T(8,128)(2,1)S(1)}, bf16[96,4096]{1,0:T(8,128)(2,1)S(1)}, u32[]{:S(2)}, u32[]{:S(2)}) collective-permute-start(bf16[96,4096]{1,0:T(8,128)(2,1)S(1)} %slice.36), channel_id=1, source_target_pairs={{0,6},{2,0},{4,2},{6,4},{1,7},{3,1},{5,3},{7,5},{8,14},{10,8},{12,... | collective-permute-start | bytes 2359304 | tf_op jit(solution)/shard_map/ppermute | solution.py:29
  66.7 1.9 collective-permute-start.10
  71.0 7.6 %shard_map.74 = bf16[4,4,128,128]{3,2,1,0:T(8,128)(2,1)} custom-call(s32[4]{0:T(128)} %pad_add_fusion.1.refs_0_.place_ref, bf16[128,4096]{1,0:T(8,128)(2,1)} %copy-done.1, bf16[128,4096]{1,0:T(8,128)(2,1)} %copy-done.2, bf16[128,4096]{1,0:T(8,128)(2,1)} %collective-permute-done.2.refs_3_, bf16[64,4096]{1,0:T(8,128)(2,1)} %copy-done.8, ...), custom_call_target="tpu_custom_call" | custom-call | flops 2147483648 | bytes 8388608 | tf_op jit(solution)/shard_map/pallas_call | solution.py:138
  78.7 3.9 %collective-permute-done.8.refs_5_ = bf16[32,4096]{1,0:T(8,128)(2,1)S(1)} collective-permute-done((bf16[32,4096]{1,0:T(8,128)(2,1)S(1)}, bf16[32,4096]{1,0:T(8,128)(2,1)S(1)}, u32[]{:S(2)}, u32[]{:S(2)}) %collective-permute-start.8) | collective-permute-done | bytes 262176 | tf_op jit(solution)/shard_map/ppermute | solution.py:33
  82.6 12.3 %collective-permute-done.6.refs_2_ = bf16[64,4096]{1,0:T(8,128)(2,1)S(1)} collective-permute-done((bf16[64,4096]{1,0:T(8,128)(2,1)S(1)}, bf16[64,4096]{1,0:T(8,128)(2,1)S(1)}, u32[]{:S(2)}, u32[]{:S(2)}) %collective-permute-start.6) | collective-permute-done | bytes 524320 | tf_op jit(solution)/shard_map/ppermute | solution.py:29
  96.1 6.8 %shard_map.75 = bf16[512,256]{1,0:T(8,128)(2,1)} custom-call(s32[4]{0:T(128)} %pad_add_fusion.1.refs_0_.place_ref, bf16[128,4096]{1,0:T(8,128)(2,1)} %copy-done, bf16[64,4096]{1,0:T(8,128)(2,1)} %copy-done.10, bf16[64,4096]{1,0:T(8,128)(2,1)} %copy-done.9, bf16[96,4096]{1,0:T(8,128)(2,1)} %copy-done.6, bf16[32,4096]{1,0:T(8,128)(2,1)} %copy-done.12, ...), custom_call_target="tpu_custom_call" | custom-call | flops 1073741824 | bytes 6291456 | tf_op jit(solution)/shard_map/pallas_call | solution.py:138
  104.1 1.9 collective-permute-start.11
  106.0 7.6 %shard_map.76 = bf16[4,4,128,128]{3,2,1,0:T(8,128)(2,1)} custom-call(s32[4]{0:T(128)} %pad_add_fusion.1.refs_0_.place_ref, bf16[128,4096]{1,0:T(8,128)(2,1)} %copy-done, bf16[64,4096]{1,0:T(8,128)(2,1)} %copy-done.10, bf16[64,4096]{1,0:T(8,128)(2,1)} %copy-done.9, bf16[96,4096]{1,0:T(8,128)(2,1)} %copy-done.6, bf16[32,4096]{1,0:T(8,128)(2,1)} %copy-done.12, ...), custom_call_target="tpu_custom_call" | custom-call | flops 2147483648 | bytes 8388608 | tf_op jit(solution)/shard_map/pallas_call | solution.py:138
  113.7 2.9 %collective-permute-done.11 = bf16[64,4096]{1,0:T(8,128)(2,1)S(1)} collective-permute-done((bf16[64,4096]{1,0:T(8,128)(2,1)S(1)}, bf16[64,4096]{1,0:T(8,128)(2,1)S(1)}, u32[]{:S(2)}, u32[]{:S(2)}) %collective-permute-start.11) | collective-permute-done | bytes 524320 | tf_op jit(solution)/shard_map/ppermute | solution.py:371
  119.5 26.9 %shard_map.77 = (f32[2048,128]{1,0:T(8,128)}, f32[2048,128]{1,0:T(8,128)}, f32[2048,128]{1,0:T(8,128)}, f32[2048,128]{1,0:T(8,128)}, f32[2048,128]{1,0:T(8,128)}, /*index=5*/f32[2048,128]{1,0:T(8,128)}) custom-call(s32[4]{0:T(128)} %pad_add_fusion.1.refs_0_.place_ref, s32[2,32]{1,0:T(2,128)} %select_reduce_fusion.off_ref, bf16[2048,128]{1,0:T(8,128)(2,1)} %bitcast.7, ...), custom_call_target="tpu_custom_call" | custom-call | flops 17716740096 | bytes 10616832 | tf_op jit(solution)/shard_map/pallas_call | solution.py:260
  146.5 15.4 %shard_map.79 = bf16[512,512]{1,0:T(8,128)(2,1)} custom-call(s32[4]{0:T(128)} %pad_add_fusion.1.refs_0_.place_ref, s32[2,32]{1,0:T(2,128)} %select_reduce_fusion.off_ref, bf16[2048,128]{1,0:T(8,128)(2,1)} %bitcast.10, bf16[8192,256]{1,0:T(8,128)(2,1)} %all-gather.6.cloned.1.call-done.kv_ref, f32[2048,128]{1,0:T(8,128)} %get-tuple-element.67.max_in, ...), custom_call_target="tpu_custom_call" | custom-call | flops 8858370048 | bytes 7340032 | tf_op jit(solution)/shard_map/pallas_call | solution.py:274
  162.0 2.5 collective-permute-start.12
  164.4 15.9 %shard_map.78.mine_ref = bf16[512,512]{1,0:T(8,128)(2,1)} custom-call(s32[4]{0:T(128)} %pad_add_fusion.1.refs_0_.place_ref, s32[2,32]{1,0:T(2,128)} %select_reduce_fusion.off_ref, bf16[2048,128]{1,0:T(8,128)(2,1)} %bitcast.8, bf16[8192,256]{1,0:T(8,128)(2,1)} %all-gather.6.cloned.1.call-done.kv_ref, f32[2048,128]{1,0:T(8,128)} %get-tuple-element.64.max_in, ...), custom_call_target="tpu_custom_call" | custom-call | flops 8858370048 | bytes 7340032 | tf_op jit(solution)/shard_map/pallas_call | solution.py:274
  181.4 10.4 %shard_map.80 = bf16[512,4096]{1,0:T(8,128)(2,1)} custom-call(bf16[512,512]{1,0:T(8,128)(2,1)} %shard_map.78.mine_ref, bf16[512,512]{1,0:T(8,128)(2,1)} %copy-done.17, bf16[512,4096]{1,0:T(8,128)(2,1)} %w_mine_ref.1, bf16[512,4096]{1,0:T(8,128)(2,1)} %all-gather.8.cloned.1.call-done.w_theirs_ref), custom_call_target="tpu_custom_call" | custom-call | flops 4294967296 | bytes 12582912 | tf_op jit(solution)/shard_map/pallas_call | solution.py:300
  191.8 46.8 %reduce-scatter.2.cloned.1.call-done = bf16[128,4096]{1,0:T(8,128)(2,1)} async-done(((bf16[512,4096]{1,0:T(8,128)(2,1)}), bf16[128,4096]{1,0:T(8,128)(2,1)}) %reduce-scatter.2.cloned.1.call-update) | async-done | bytes 1048592 | tf_op jit(solution)/shard_map/reduce_scatter | solution.py:392
  238.6 2.4 fusion.3
  (87 shorter events, 22.8 us)
Async XLA Ops:
  6.5 11.4 %copy-start.16 = (s32[1024]{0:T(1024)S(1)}, s32[1024]{0:T(1024)}, u32[]{:S(2)}) copy-start(s32[1024]{0:T(1024)} %param.9) | copy-start | bytes 12292
  6.5 111.0 %all-gather.4.cloned.1.call-start = ((), (), s32[]{:S(2)}) async-start(), calls=%async_computation.1 | async-start | bytes 4595712 | tf_op jit(solution)/shard_map/all_gather | solution.py:341
  10.3 26.4 %collective-permute-start = (bf16[128,4096]{1,0:T(8,128)(2,1)S(1)}, bf16[128,4096]{1,0:T(8,128)(2,1)S(1)}, u32[]{:S(2)}, u32[]{:S(2)}) collective-permute-start(bf16[128,4096]{1,0:T(8,128)(2,1)S(1)} %fusion.2.refs_1_), channel_id=1, source_target_pairs={{0,1},{1,0},{2,3},{3,2},{4,5},{5,4},{6,7},{7,6},{8,9},{9,8},{10,11... | collective-permute-start | bytes 3145736 | tf_op jit(solution)/shard_map/ppermute | solution.py:33
  14.2 26.3 %collective-permute-start.1 = (bf16[128,4096]{1,0:T(8,128)(2,1)S(1)}, bf16[128,4096]{1,0:T(8,128)(2,1)S(1)}, u32[]{:S(2)}, u32[]{:S(2)}) collective-permute-start(bf16[128,4096]{1,0:T(8,128)(2,1)S(1)} %fusion.2.refs_1_), channel_id=1, source_target_pairs={{0,2},{2,4},{4,6},{6,0},{1,3},{3,5},{5,7},{7,1},{8,10},{10,12},{12... | collective-permute-start | bytes 3145736 | tf_op jit(solution)/shard_map/ppermute | solution.py:29
  15.8 24.7 %collective-permute-start.2 = (bf16[128,4096]{1,0:T(8,128)(2,1)S(1)}, bf16[128,4096]{1,0:T(8,128)(2,1)}, u32[]{:S(2)}, u32[]{:S(2)}) collective-permute-start(bf16[128,4096]{1,0:T(8,128)(2,1)S(1)} %fusion.2.refs_1_), channel_id=1, source_target_pairs={{0,6},{2,0},{4,2},{6,4},{1,7},{3,1},{5,3},{7,5},{8,14},{10,8},{12,... | collective-permute-start | bytes 3145736 | tf_op jit(solution)/shard_map/ppermute | solution.py:29
  21.3 24.3 %copy-start.13 = (bf16[4096,128]{1,0:T(8,128)(2,1)S(1)}, bf16[4096,128]{1,0:T(8,128)(2,1)}, u32[]{:S(2)}) copy-start(bf16[4096,128]{1,0:T(8,128)(2,1)} %param.12) | copy-start | bytes 3145732
  21.3 24.3 %copy-start.14 = (bf16[4096,128]{1,0:T(8,128)(2,1)S(1)}, bf16[4096,128]{1,0:T(8,128)(2,1)}, u32[]{:S(2)}) copy-start(bf16[4096,128]{1,0:T(8,128)(2,1)} %param.11) | copy-start | bytes 3145732
  36.8 29.0 %copy-start = (bf16[128,4096]{1,0:T(8,128)(2,1)}, bf16[128,4096]{1,0:T(8,128)(2,1)S(1)}, u32[]{:S(2)}) copy-start(bf16[128,4096]{1,0:T(8,128)(2,1)S(1)} %collective-permute-done.refs_1_) | copy-start | bytes 3145732
  40.6 13.2 %collective-permute-start.3 = (bf16[64,4096]{1,0:T(8,128)(2,1)S(1)}, bf16[64,4096]{1,0:T(8,128)(2,1)S(1)}, u32[]{:S(2)}, u32[]{:S(2)}) collective-permute-start(bf16[64,4096]{1,0:T(8,128)(2,1)S(1)} %get-tuple-element.72), channel_id=1, source_target_pairs={{0,2},{2,4},{4,6},{6,0},{1,3},{3,5},{5,7},{7,1},{8,10},{10,12},{12... | collective-permute-start | bytes 1572872 | tf_op jit(solution)/shard_map/ppermute | solution.py:29
  41.1 12.6 %collective-permute-start.5 = (bf16[64,4096]{1,0:T(8,128)(2,1)S(1)}, bf16[64,4096]{1,0:T(8,128)(2,1)S(1)}, u32[]{:S(2)}, u32[]{:S(2)}) collective-permute-start(bf16[64,4096]{1,0:T(8,128)(2,1)S(1)} %get-tuple-element.71), channel_id=1, source_target_pairs={{0,1},{1,0},{2,3},{3,2},{4,5},{5,4},{6,7},{7,6},{8,9},{9,8},{10,11... | collective-permute-start | bytes 1572872 | tf_op jit(solution)/shard_map/ppermute | solution.py:33
  42.6 11.9 %collective-permute-start.4 = (bf16[64,4096]{1,0:T(8,128)(2,1)S(1)}, bf16[64,4096]{1,0:T(8,128)(2,1)S(1)}, u32[]{:S(2)}, u32[]{:S(2)}) collective-permute-start(bf16[64,4096]{1,0:T(8,128)(2,1)S(1)} %slice.32), channel_id=1, source_target_pairs={{0,6},{2,0},{4,2},{6,4},{1,7},{3,1},{5,3},{7,5},{8,14},{10,8},{12,... | collective-permute-start | bytes 1572872 | tf_op jit(solution)/shard_map/ppermute | solution.py:29
  62.1 84.4 %all-gather.6.cloned.1.call-start = ((), (), s32[]{:S(2)}) async-start(), calls=%async_computation.2 | async-start | bytes 4456448 | tf_op jit(solution)/shard_map/all_gather | solution.py:364
  62.2 32.6 %collective-permute-start.7 = (bf16[96,4096]{1,0:T(8,128)(2,1)S(1)}, bf16[96,4096]{1,0:T(8,128)(2,1)S(1)}, u32[]{:S(2)}, u32[]{:S(2)}) collective-permute-start(bf16[96,4096]{1,0:T(8,128)(2,1)S(1)} %slice.36), channel_id=1, source_target_pairs={{0,6},{2,0},{4,2},{6,4},{1,7},{3,1},{5,3},{7,5},{8,14},{10,8},{12,... | collective-permute-start | bytes 2359304 | tf_op jit(solution)/shard_map/ppermute | solution.py:29
  65.7 29.2 %collective-permute-start.9 = (bf16[80,4096]{1,0:T(8,128)(2,1)S(1)}, bf16[80,4096]{1,0:T(8,128)(2,1)S(1)}, u32[]{:S(2)}, u32[]{:S(2)}) collective-permute-start(bf16[80,4096]{1,0:T(8,128)(2,1)S(1)} %slice.38), channel_id=1, source_target_pairs={{0,4},{2,6},{4,0},{6,2},{1,5},{3,7},{5,1},{7,3},{8,12},{10,14},{12... | collective-permute-start | bytes 1966088 | tf_op jit(solution)/shard_map/ppermute | solution.py:29
  65.8 29.0 %collective-permute-start.6 = (bf16[64,4096]{1,0:T(8,128)(2,1)S(1)}, bf16[64,4096]{1,0:T(8,128)(2,1)S(1)}, u32[]{:S(2)}, u32[]{:S(2)}) collective-permute-start(bf16[64,4096]{1,0:T(8,128)(2,1)S(1)} %slice.35), channel_id=1, source_target_pairs={{0,2},{2,4},{4,6},{6,0},{1,3},{3,5},{5,7},{7,1},{8,10},{10,12},{12... | collective-permute-start | bytes 1572872 | tf_op jit(solution)/shard_map/ppermute | solution.py:29
  66.7 15.8 %collective-permute-start.10 = (bf16[48,4096]{1,0:T(8,128)(2,1)S(1)}, bf16[48,4096]{1,0:T(8,128)(2,1)S(1)}, u32[]{:S(2)}, u32[]{:S(2)}) collective-permute-start(bf16[48,4096]{1,0:T(8,128)(2,1)S(1)} %slice.39), channel_id=1, source_target_pairs={{0,1},{1,0},{2,3},{3,2},{4,5},{5,4},{6,7},{7,6},{8,9},{9,8},{10,11... | collective-permute-start | bytes 1179656 | tf_op jit(solution)/shard_map/ppermute | solution.py:33
  69.6 12.9 %collective-permute-start.8 = (bf16[32,4096]{1,0:T(8,128)(2,1)S(1)}, bf16[32,4096]{1,0:T(8,128)(2,1)S(1)}, u32[]{:S(2)}, u32[]{:S(2)}) collective-permute-start(bf16[32,4096]{1,0:T(8,128)(2,1)S(1)} %slice.37), channel_id=1, source_target_pairs={{0,1},{1,0},{2,3},{3,2},{4,5},{5,4},{6,7},{7,6},{8,9},{9,8},{10,11... | collective-permute-start | bytes 786440 | tf_op jit(solution)/shard_map/ppermute | solution.py:33
  82.6 12.3 %copy-start.12 = (bf16[32,4096]{1,0:T(8,128)(2,1)}, bf16[32,4096]{1,0:T(8,128)(2,1)S(1)}, u32[]{:S(2)}) copy-start(bf16[32,4096]{1,0:T(8,128)(2,1)S(1)} %collective-permute-done.8.refs_5_) | copy-start | bytes 786436
  82.6 12.3 %copy-start.11 = (bf16[48,4096]{1,0:T(8,128)(2,1)}, bf16[48,4096]{1,0:T(8,128)(2,1)S(1)}, u32[]{:S(2)}) copy-start(bf16[48,4096]{1,0:T(8,128)(2,1)S(1)} %collective-permute-done.10.refs_7_) | copy-start | bytes 1179652
  102.9 77.7 %all-gather.8.cloned.1.call-start = ((), (), s32[]{:S(2)}) async-start(), calls=%async_computation.3 | async-start | bytes 4718592 | tf_op jit(solution)/shard_map/all_gather | solution.py:374
  104.1 12.5 %collective-permute-start.11 = (bf16[64,4096]{1,0:T(8,128)(2,1)S(1)}, bf16[64,4096]{1,0:T(8,128)(2,1)S(1)}, u32[]{:S(2)}, u32[]{:S(2)}) collective-permute-start(bf16[64,4096]{1,0:T(8,128)(2,1)S(1)} %constant_dynamic-slice_fusion), channel_id=1, source_target_pairs={{0,65},{65,0},{1,64},{64,1},{2,67},{67,2},{3,66},{66,3},{4,69},{69... | collective-permute-start | bytes 1572872 | tf_op jit(solution)/shard_map/ppermute | solution.py:371
  117.4 121.2 %reduce-scatter.2.cloned.1.call-start = ((), (), s32[]{:S(2)}) async-start(), calls=%async_computation.4 | async-start | bytes 5242880 | tf_op jit(solution)/shard_map/reduce_scatter | solution.py:392
  162.0 18.6 %collective-permute-start.12 = (bf16[512,512]{1,0:T(8,128)(2,1)}, bf16[512,512]{1,0:T(8,128)(2,1)S(1)}, u32[]{:S(2)}, u32[]{:S(2)}) collective-permute-start(bf16[512,512]{1,0:T(8,128)(2,1)} %shard_map.79), channel_id=1, source_target_pairs={{0,1},{1,0},{2,3},{3,2},{4,5},{5,4},{6,7},{7,6},{8,9},{9,8},{10,11... | collective-permute-start | bytes 1572872 | tf_op jit(solution)/shard_map/ppermute | solution.py:33
  191.8 46.8 %copy-start.3 = (bf16[128,4096]{1,0:T(8,128)(2,1)S(1)}, bf16[128,4096]{1,0:T(8,128)(2,1)}, u32[]{:S(2)}) copy-start(bf16[128,4096]{1,0:T(8,128)(2,1)} %param.7) | copy-start | bytes 3145732
  (11 other events, 29.5 us)
Sparse Core Ops, SparseCore 0:
  62.2 46.9 all-gather.3
  111.0 35.5 all-gather.5
  148.3 32.2 all-gather.7
  191.9 46.6 reduce-scatter.1

commit v4 on v3

--- a/solution.py
+++ b/solution.py
@@ -16,6 +16,8 @@
 BASE = 500000.0
 NEGATIVE = -1e30
 HALF = OWNED // 2
+PARTS = 1
+PIECE = OWNED // PARTS
 DIRECT = (64, 96, 80)
 TAIL = 16
 VMEM_LIMIT = 56 * 2**20
@@ -124,7 +126,9 @@
             mine = slice(k * OWNED, (k + 1) * OWNED)
             for h in range(query.shape[1] // HEAD):
                 turned = rope(query[mine, h * HEAD : (h + 1) * HEAD], cosine, sine)
-                q_ref[where, h] = (turned * SCORE_SCALE).astype(jnp.bfloat16)
+                turned = (turned * SCORE_SCALE).astype(jnp.bfloat16)
+                for part in range(PARTS):
+                    q_ref[part, where, h] = turned[part * PIECE : (part + 1) * PIECE]
 
 
 def project(kernel, place, groups, weights, tables, out):
@@ -155,16 +159,37 @@
     )(place, *pieces, *weights, *tables)
 
 
-def attend_pairs(place_ref, off_ref, kv_ref, tiles, heads, pairs, unroll, far):
-    per = 2 * heads * OWNED
+def start_keys(place_ref, kv_ref, held_ref, sems, n_ctx):
+    stride = kv_ref.shape[0] // n_ctx
+    copies = []
+    for t in range(n_ctx):
+        at = pl.multiple_of(lax.rem(place_ref[4] + 1 + t, n_ctx) * stride, 16)
+        rows = pl.ds(at, stride)
+        copy = pltpu.make_async_copy(kv_ref.at[rows], held_ref.at[rows], sems.at[t])
+        copy.start()
+        copies.append(copy)
+    return copies
+
+
+def attend_pairs(place_ref, known_ref, kv_ref, held_ref, sems, tiles, heads, far):
+    per = 2 * heads * PIECE
     step = 2 * OWNED
     side = place_ref[1]
-
-    def pair(which, block, masked):
-        at = pl.multiple_of(off_ref[int(far), block], 16)
-        keys = kv_ref[pl.ds(at, step), :HEAD]
-        values = kv_ref[pl.ds(at, step), HEAD:]
-        for other, q_ref, max_ref, sum_ref, acc_ref in tiles:
+    n_ctx = sems.shape[0]
+    stride = kv_ref.shape[0] // n_ctx
+    me = place_ref[4]
+    early = (place_ref[2] > place_ref[3]).astype(jnp.int32)
+    earliest = jnp.minimum(place_ref[2], place_ref[3])
+
+    def peer(i):
+        one, two = known_ref[2 * i], known_ref[2 * i + 1]
+        return (one > two).astype(jnp.int32), jnp.minimum(one, two)
+
+    def pair(which, i, half, masked):
+        at = pl.multiple_of(i * stride + half * step, 16)
+        keys = held_ref[pl.ds(at, step), :HEAD]
+        values = held_ref[pl.ds(at, step), HEAD:]
+        for other, part, q_ref, max_ref, sum_ref, acc_ref in tiles:
             here = pl.ds(pl.multiple_of(which * per, per), per)
             scores = lax.dot_general(
                 q_ref[here, :], keys, (((1,), (1,)), ((), ())),
@@ -174,8 +199,8 @@
                 row = lax.broadcasted_iota(jnp.int32, scores.shape, 0)
                 row_side = 1 - side if other else side
                 row = (
-                    (row // (heads * OWNED)) * (2 * OWNED) + row_side * OWNED
-                    + (row & (OWNED - 1))
+                    (row // (heads * PIECE)) * (2 * OWNED) + row_side * OWNED
+                    + part * PIECE + (row & (PIECE - 1))
                 )
                 col = lax.broadcasted_iota(jnp.int32, scores.shape, 1)
                 col_side = 1 - side if far else side
@@ -196,131 +221,162 @@
                 weights.astype(jnp.bfloat16), values, preferred_element_type=jnp.float32
             )
 
-    first = place_ref[2]
-
-    def plain(i):
-        which = (i >= first).astype(jnp.int32)
-        pair(which, i - which * first, False)
+    group = 5 if (n_ctx - 1) % 5 == 0 else 1
+
+    def wait(t):
+        rows = pl.ds(0, stride)
+        pltpu.make_async_copy(kv_ref.at[rows], held_ref.at[rows], sems.at[t]).wait()
 
     def body(j, carry):
-        for u in range(unroll):
-            plain(j * unroll + u)
+        for u in range(group):
+            wait(j * group + u)
+        for u in range(group):
+            i = lax.rem(me + 1 + j * group + u, n_ctx)
+            lower, least = peer(i)
+            pair(1 - early, i, lower, False)
+            before = (least < earliest).astype(jnp.int32)
+            pair(
+                before * early + (1 - before) * (1 - early),
+                i, before * lower + (1 - before) * (1 - lower), False,
+            )
         return carry
 
-    lax.fori_loop(0, pairs // unroll, body, 0)
-    for i in range(pairs // unroll * unroll, pairs):
-        plain(jnp.int32(i))
+    lax.fori_loop(0, (n_ctx - 1) // group, body, 0)
+    wait(n_ctx - 1)
+    pair(1 - early, me, early, False)
     for which in range(2):
-        pair(which, place_ref[2 + which], True)
+        pair(which, me, which, True)
 
 
 def attend_near_kernel(
-    place_ref, off_ref, q_near_ref, q_far_ref, kv_ref, *state_refs, heads, pairs, unroll
+    place_ref, known_ref, q_near_ref, q_far_ref, kv_ref, *refs, heads, n_ctx
 ):
-    for start in range(0, len(state_refs), 3):
-        max_ref, sum_ref, acc_ref = state_refs[start : start + 3]
+    state_refs, (held_ref, sems) = refs[:-2], refs[-2:]
+    start_keys(place_ref, kv_ref, held_ref, sems, n_ctx)
+    tiles = []
+    for index in range(2 * PARTS):
+        max_ref, sum_ref, acc_ref = state_refs[3 * index : 3 * index + 3]
         max_ref[...] = jnp.full_like(max_ref, NEGATIVE)
         sum_ref[...] = jnp.zeros_like(sum_ref)
         acc_ref[...] = jnp.zeros_like(acc_ref)
-    tiles = [(True, q_far_ref, *state_refs[3:]), (False, q_near_ref, *state_refs[:3])]
-    attend_pairs(place_ref, off_ref, kv_ref, tiles, heads, pairs, unroll, False)
+        other, part = index >= PARTS, index % PARTS
+        q_ref = (q_far_ref if other else q_near_ref).at[part]
+        tiles.append((other, part, q_ref, max_ref, sum_ref, acc_ref))
+    attend_pairs(place_ref, known_ref, kv_ref, held_ref, sems, tiles, heads, False)
 
 
 def attend_far_kernel(
-    place_ref, off_ref, q_ref, kv_ref, max_in, sum_in, acc_in, o_ref,
-    max_ref, sum_ref, acc_ref, *, other, heads, pairs, unroll,
+    place_ref, known_ref, q_ref, kv_ref, max_in, sum_in, acc_in, o_ref,
+    max_ref, sum_ref, acc_ref, held_ref, sems, *, other, part, heads, n_ctx,
 ):
+    start_keys(place_ref, kv_ref, held_ref, sems, n_ctx)
     max_ref[...] = max_in[...]
     sum_ref[...] = sum_in[...]
     acc_ref[...] = acc_in[...]
-    tiles = [(other, q_ref, max_ref, sum_ref, acc_ref)]
-    attend_pairs(place_ref, off_ref, kv_ref, tiles, heads, pairs, unroll, True)
+    tiles = [(other, part, q_ref, max_ref, sum_ref, acc_ref)]
+    attend_pairs(place_ref, known_ref, kv_ref, held_ref, sems, tiles, heads, True)
     for group in range(4):
         for h in range(heads):
-            start = (group * heads + h) * OWNED
-            here = slice(start, start + OWNED)
+            start = (group * heads + h) * PIECE
+            here = slice(start, start + PIECE)
             total = jnp.sum(sum_ref[here, :], axis=1, keepdims=True)
-            o_ref[group * OWNED : (group + 1) * OWNED, h * HEAD : (h + 1) * HEAD] = (
+            o_ref[group * PIECE : (group + 1) * PIECE, h * HEAD : (h + 1) * HEAD] = (
                 acc_ref[here, :] / total
             ).astype(jnp.bfloat16)
 
 
-def attend_cost(pairs, rows, kv):
-    scores = (pairs + 2) * rows * SPAN // 4
+def attend_cost(n_ctx, rows, kv):
+    scores = (2 * n_ctx + 1) * rows * SPAN // 4
     return pl.CostEstimate(
         flops=scores * HEAD * 8, bytes_accessed=2 * kv.size + 12 * rows * HEAD,
         transcendentals=scores,
     )
 
 
-def attend_near(place, offsets, q_near, q_far, kv, heads):
-    pairs = offsets.shape[1] - 1
+def attend_near(place, known, q_near, q_far, kv, heads):
+    n_ctx = known.shape[0] // 2
     vmem = pl.BlockSpec(memory_space=pltpu.VMEM)
     smem = pl.BlockSpec(memory_space=pltpu.SMEM)
     return pl.pallas_call(
-        functools.partial(attend_near_kernel, heads=heads, pairs=pairs, unroll=6),
-        in_specs=[smem, smem, vmem, vmem, vmem],
-        out_specs=[vmem] * 6,
-        out_shape=[jax.ShapeDtypeStruct(q_near.shape, jnp.float32)] * 6,
+        functools.partial(attend_near_kernel, heads=heads, n_ctx=n_ctx),
+        in_specs=[smem, smem, vmem, vmem, pl.BlockSpec(memory_space=pl.ANY)],
+        out_specs=[vmem] * (6 * PARTS),
+        out_shape=[jax.ShapeDtypeStruct(q_near.shape[1:], jnp.float32)] * (6 * PARTS),
+        scratch_shapes=[
+            pltpu.VMEM(kv.shape, jnp.bfloat16), pltpu.SemaphoreType.DMA((n_ctx,)),
+        ],
         compiler_params=pltpu.CompilerParams(vmem_limit_bytes=VMEM_LIMIT),
-        cost_estimate=attend_cost(pairs, 2 * q_near.shape[0], kv),
-    )(place, offsets, q_near, q_far, kv)
-
-
-def attend_far(place, offsets, query, kv, state, other, heads):
-    pairs = offsets.shape[1] - 1
+        cost_estimate=attend_cost(n_ctx, 2 * PARTS * q_near.shape[1], kv),
+    )(place, known, q_near, q_far, kv)
+
+
+def attend_far(place, known, query, kv, state, other, part, heads):
+    n_ctx = known.shape[0] // 2
     vmem = pl.BlockSpec(memory_space=pltpu.VMEM)
     smem = pl.BlockSpec(memory_space=pltpu.SMEM)
     return pl.pallas_call(
         functools.partial(
-            attend_far_kernel, other=other, heads=heads, pairs=pairs, unroll=10
+            attend_far_kernel, other=other, part=part, heads=heads, n_ctx=n_ctx
         ),
-        in_specs=[smem, smem] + [vmem] * 5,
+        in_specs=[smem, smem, vmem, pl.BlockSpec(memory_space=pl.ANY)] + [vmem] * 3,
         out_specs=vmem,
-        out_shape=jax.ShapeDtypeStruct((4 * OWNED, heads * HEAD), jnp.bfloat16),
-        scratch_shapes=[pltpu.VMEM(query.shape, jnp.float32)] * 3,
+        out_shape=jax.ShapeDtypeStruct((4 * PIECE, heads * HEAD), jnp.bfloat16),
+        scratch_shapes=[pltpu.VMEM(query.shape, jnp.float32)] * 3 + [
+            pltpu.VMEM(kv.shape, jnp.bfloat16), pltpu.SemaphoreType.DMA((n_ctx,)),
+        ],
         compiler_params=pltpu.CompilerParams(vmem_limit_bytes=VMEM_LIMIT),
-        cost_estimate=attend_cost(pairs, query.shape[0], kv),
-    )(place, offsets, query, kv, *state)
-
-
-def combine_kernel(mine_ref, theirs_ref, w_mine_ref, w_theirs_ref, out_ref):
+        cost_estimate=attend_cost(n_ctx, query.shape[0], kv),
+    )(place, known, query, kv, *state)
+
+
+def combine_kernel(core_ref, mine_ref, theirs_ref, w_mine_ref, w_own_ref, w_other_ref, out_ref):
+    half = theirs_ref.shape[1] // 2
+    theirs = theirs_ref[...]
+    low = core_ref[0] == 0
+    own = jnp.where(low, theirs[:, :half], theirs[:, half:])
+    other = jnp.where(low, theirs[:, half:], theirs[:, :half])
     out_ref[...] = (
         jnp.dot(mine_ref[...], w_mine_ref[...], preferred_element_type=jnp.float32)
-        + jnp.dot(theirs_ref[...], w_theirs_ref[...], preferred_element_type=jnp.float32)
+        + jnp.dot(own, w_own_ref[...], preferred_element_type=jnp.float32)
+        + jnp.dot(other, w_other_ref[...], preferred_element_type=jnp.float32)
     ).astype(jnp.bfloat16)
 
 
-def combine(mine, theirs, w_mine, w_theirs):
+def combine(core, mine, theirs, w_mine, w_own, w_other):
     rows, depth = mine.shape
     columns = w_mine.shape[1]
-    step = 512
+    step = 1024
     whole = lambda i: (0, 0)
     across = lambda i: (0, i)
     return pl.pallas_call(
         combine_kernel,
         grid=(columns // step,),
         in_specs=[
+            pl.BlockSpec(memory_space=pltpu.SMEM),
             pl.BlockSpec((rows, depth), whole),
             pl.BlockSpec((rows, depth), whole),
             pl.BlockSpec((depth, step), across),
-            pl.BlockSpec((depth, step), across),
+            pl.BlockSpec((depth // 2, step), across),
+            pl.BlockSpec((depth // 2, step), across),
         ],
-        out_specs=pl.BlockSpec((rows, step), lambda i: (0, i)),
+        out_specs=pl.BlockSpec((rows, step), across),
         out_shape=jax.ShapeDtypeStruct((rows, columns), jnp.bfloat16),
-        compiler_params=pltpu.CompilerParams(vmem_limit_bytes=VMEM_LIMIT),
+        compiler_params=pltpu.CompilerParams(vmem_limit_bytes=14 * 2**20),
         cost_estimate=pl.CostEstimate(
             flops=4 * rows * depth * columns,
             bytes_accessed=4 * depth * columns + 2 * rows * columns,
             transcendentals=0,
         ),
-    )(mine, theirs, w_mine, w_theirs)
+    )(core, mine, theirs, w_mine, w_own, w_other)
 
 
 def per_device(hidden_in, gain, positions, w_query, w_key, w_value, w_out, *, n_ctx):
     ids = positions[::SPAN] // SPAN
     place = jnp.concatenate(
-        [jnp.stack([lax.axis_index("z"), lax.axis_index("y_hi")]).astype(jnp.int32), ids]
+        [
+            jnp.stack([lax.axis_index("z"), lax.axis_index("y_hi")]).astype(jnp.int32), ids,
+            lax.axis_index(CTX).astype(jnp.int32).reshape(1),
+        ]
     )
     widened = hidden_in.astype(jnp.float32)
     scale_rows = lax.rsqrt(jnp.mean(widened * widened, axis=-1, keepdims=True) + EPS)
@@ -351,8 +407,8 @@
     def queries(groups, other):
         return project(
             functools.partial(project_q_kernel, other=other),
-            place, groups, (w_query,), tables, (4, heads, OWNED, HEAD),
-        ).reshape(4 * heads * OWNED, HEAD)
+            place, groups, (w_query,), tables, (PARTS, 4, heads, PIECE, HEAD),
+        ).reshape(PARTS, 4 * heads * PIECE, HEAD)
 
     q_near = queries(near, False)
     far, q_near = lax.optimization_barrier((far, q_near))
@@ -363,34 +419,30 @@
     kv_near = kv_near_all
     kv_far_all = lax.all_gather(kv_far, CTX, axis=0, tiled=True)
     q_far = queries(far, True)
-    slices = 8
-    part_rows = w_out.shape[0] // slices
-    turn_of = lax.axis_index("x") * 2 + lax.axis_index("core")
-    eighth = lax.dynamic_slice_in_dim(w_out, turn_of * part_rows, part_rows, 0)
-    eighth, _ = lax.optimization_barrier((eighth, kv_far))
-    eighth = lax.ppermute(eighth, ("y_lo", "y_hi"), [(0, 3), (3, 0), (1, 2), (2, 1)])
-    eighth, q_far = lax.optimization_barrier((eighth, q_far))
+    kv_far, q_far = lax.optimization_barrier((kv_far, q_far))
+    core = lax.axis_index("core").astype(jnp.int32)
+    half_rows = w_out.shape[0] // 2
+    w_own = lax.dynamic_slice_in_dim(w_out, core * half_rows, half_rows, 0)
+    w_own, _ = lax.optimization_barrier((w_own, far))
+    w_own = lax.ppermute(w_own, ("y_lo", "y_hi"), [(0, 3), (3, 0), (1, 2), (2, 1)])
     kv_far = kv_far_all
-    w_theirs = lax.all_gather(eighth, ("x", "core"), axis=0, tiled=True)
-
     rows_near = 4 * OWNED + TAIL
     known = kv_near.reshape(n_ctx, rows_near, 2 * HEAD)[:, 4 * OWNED :: TAIL // 2, 0]
     known = known.astype(jnp.int32).reshape(-1)
-    owner = jnp.arange(2 * n_ctx, dtype=jnp.int32) // 2
-    within = (jnp.arange(2 * n_ctx, dtype=jnp.int32) % 2) * (2 * OWNED)
-    at = jnp.stack([owner * rows_near + within, owner * (4 * OWNED) + within])
-    slots = jnp.arange(2 * n_ctx, dtype=jnp.int32)
-    offsets = jnp.sum(
-        jnp.where(known[None, :, None] == slots[None, None, :], at[:, :, None], 0), axis=1
-    )
-
-    state = attend_near(place, offsets, q_near, q_far, kv_near, heads)
-    sent = attend_far(place, offsets, q_far, kv_far, state[3:], True, heads)
-    theirs = swap(sent)
-    mine = attend_far(place, offsets, q_near, kv_far, state[:3], False, heads)
-    term = combine(mine, theirs, w_out, w_theirs)
-    summed = lax.psum_scatter(term, "z", scatter_dimension=0, tiled=True)
-    return (widened + summed.astype(jnp.float32)).astype(jnp.bfloat16)
+    state = attend_near(place, known, q_near, q_far, kv_near, heads)
+    terms = []
+    for part in range(PARTS):
+        mine, sent = state[3 * part : 3 * part + 3], state[3 * (PARTS + part) :][:3]
+        sent = attend_far(place, known, q_far[part], kv_far, sent, True, part, heads)
+        if part == 0:
+            sent, w_own = lax.optimization_barrier((sent, w_own))
+            w_other = lax.ppermute(w_own, "core", [(0, 1), (1, 0)])
+        theirs = swap(sent)
+        mine = attend_far(place, known, q_near[part], kv_far, mine, False, part, heads)
+        term = combine(core.reshape(1), mine, theirs, w_out, w_own, w_other)
+        terms.append(lax.psum_scatter(term, "z", scatter_dimension=0, tiled=True))
+    summed = jnp.concatenate(terms, axis=0).astype(jnp.float32)
+    return (widened + summed).astype(jnp.bfloat16)
 
 
 def solution(mesh):

time: 248 us -> 245 us (0.988)
  Pallas kernels: 97.5 us -> 92.5 us
  local copies, waits for them, and re-layouts: 8.4 us -> 12.4 us
    pallas_call x1, Pallas kernels: 10.4 us -> 6.63 us  [combine(): pl.pallas_call(combine_kernel, grid=(columns // step,), in_specs=[pl.Bloc...]
    all_gather x1, waiting for transfers between devices: 0.12 us -> 3.35 us  [per_device(): kv_far_all = lax.all_gather(kv_far, CTX, axis=0, tiled=True)]
    ppermute x1 -> x2, waiting for transfers between devices: 2.92 us -> 0.01 us  [the longest x1 0.01 us: per_device(): lax.ppermute(w_own, ('y_lo', 'y_hi'), [(0, 3), (3, 0), (1, 2), (2, 1)])]
    unnamed x37 -> x39, local copies, waits for them, and re-layouts: 3.96 us -> 5.42 us
  transfers between devices with their start and end apart: 17 -> 17, of which waited for: 10 -> 8; matrix products, arithmetic and copies ran while one was open for 4% -> 5% of each run, Pallas kernels for 32% -> 32%
where the time goes in v4:
time: 245 us
  Pallas kernels  92.5 us (38%)
  waiting for transfers between devices  91.6 us (37%)
  starting transfers between devices  23.3 us (10%)
  between operations  13.4 us (5%)
  local copies, waits for them, and re-layouts  12.4 us (5%)
  other arithmetic  11.8 us (5%)
    reduce_scatter x1, waiting for transfers between devices, per_device(): terms.append(lax.psum_scatter(term, 'z', scatter_dimension=0, tiled=True))  45.6 us
    pallas_call x2, Pallas kernels, attend_far(): pl.pallas_call(functools.partial(attend_far_kernel, other=other, part=par...  31.2 us
    pallas_call x4, Pallas kernels, project(): pl.pallas_call(functools.partial(kernel, groups=tuple((tuple((p.shape[0]...  28.8 us
    pallas_call x1, Pallas kernels, attend_near(): pl.pallas_call(functools.partial(attend_near_kernel, heads=heads, n_ctx=n...  25.8 us
    ppermute x7, waiting for transfers between devices, turn(): return lax.ppermute(x, 'z', [(i, (i + by) % 4) for i in range(4)])  23.2 us
    ppermute x5, waiting for transfers between devices, swap(): return lax.ppermute(x, 'y_hi', [(0, 1), (1, 0)])  19.3 us
    ppermute x7, starting transfers between devices, turn(): return lax.ppermute(x, 'z', [(i, (i + by) % 4) for i in range(4)])  11 us
    ppermute x5, starting transfers between devices, swap(): return lax.ppermute(x, 'y_hi', [(0, 1), (1, 0)])  9.98 us
  transfers between devices with their start and end apart: 17, of which 8 were waited for; matrix products, arithmetic and copies ran while one was open for 5% of the time, Pallas kernels for 32%

profile of v4, /device:TPU:1, one launch (start us, length us, event | category | flops | bytes accessed | tf_op | source)
XLA Modules:
  0.0 244.9 jit_solution(2558445282068014225)
XLA Ops:
  10.3 3.8 %collective-permute-start = (bf16[128,4096]{1,0:T(8,128)(2,1)S(1)}, bf16[128,4096]{1,0:T(8,128)(2,1)S(1)}, u32[]{:S(2)}, u32[]{:S(2)}) collective-permute-start(bf16[128,4096]{1,0:T(8,128)(2,1)S(1)} %fusion.2.refs_1_), channel_id=1, source_target_pairs={{0,1},{1,0},{2,3},{3,2},{4,5},{5,4},{6,7},{7,6},{8,9},{9,8},{10,11... | collective-permute-start | bytes 3145736 | tf_op jit(solution)/shard_map/ppermute | solution.py:35
  15.8 2.1 collective-permute-start.2
  21.4 15.4 %collective-permute-done.refs_1_ = bf16[128,4096]{1,0:T(8,128)(2,1)S(1)} collective-permute-done((bf16[128,4096]{1,0:T(8,128)(2,1)S(1)}, bf16[128,4096]{1,0:T(8,128)(2,1)S(1)}, u32[]{:S(2)}, u32[]{:S(2)}) %collective-permute-start) | collective-permute-done | bytes 1048608 | tf_op jit(solution)/shard_map/ppermute | solution.py:35
  36.8 3.7 %collective-permute-done.1.refs_2_ = bf16[128,4096]{1,0:T(8,128)(2,1)S(1)} collective-permute-done((bf16[128,4096]{1,0:T(8,128)(2,1)S(1)}, bf16[128,4096]{1,0:T(8,128)(2,1)S(1)}, u32[]{:S(2)}, u32[]{:S(2)}) %collective-permute-start.1) | collective-permute-done | bytes 1048608 | tf_op jit(solution)/shard_map/ppermute | solution.py:31
  42.6 2.4 collective-permute-start.4
  47.2 6.5 %collective-permute-done.3.refs_4_ = bf16[64,4096]{1,0:T(8,128)(2,1)S(1)} collective-permute-done((bf16[64,4096]{1,0:T(8,128)(2,1)S(1)}, bf16[64,4096]{1,0:T(8,128)(2,1)S(1)}, u32[]{:S(2)}, u32[]{:S(2)}) %collective-permute-start.3) | collective-permute-done | bytes 524320 | tf_op jit(solution)/shard_map/ppermute | solution.py:31
  55.4 6.7 %shard_map.73 = bf16[528,256]{1,0:T(8,128)(2,1)} custom-call(s32[5]{0:T(128)} %pad_add_fusion.refs_0_.place_ref, bf16[128,4096]{1,0:T(8,128)(2,1)} %copy-done.4, bf16[128,4096]{1,0:T(8,128)(2,1)} %copy-done.5, bf16[128,4096]{1,0:T(8,128)(2,1)} %collective-permute-done.2.refs_3_, bf16[64,4096]{1,0:T(8,128)(2,1)} %copy-done.11, bf16[64,4096]{1,0:T(8,128)(2,1)} %copy-done.7, ...), custom_call_target="tpu_custom_call" | custom-call | flops 1073741824 | bytes 6291456 | tf_op jit(solution)/shard_map/pallas_call | solution.py:142
  62.3 3.4 %collective-permute-start.7 = (bf16[96,4096]{1,0:T(8,128)(2,1)S(1)}, bf16[96,4096]{1,0:T(8,128)(2,1)S(1)}, u32[]{:S(2)}, u32[]{:S(2)}) collective-permute-start(bf16[96,4096]{1,0:T(8,128)(2,1)S(1)} %slice.36), channel_id=1, source_target_pairs={{0,6},{2,0},{4,2},{6,4},{1,7},{3,1},{5,3},{7,5},{8,14},{10,8},{12,... | collective-permute-start | bytes 2359304 | tf_op jit(solution)/shard_map/ppermute | solution.py:31
  66.8 1.9 collective-permute-start.10
  71.0 7.7 %shard_map.74 = bf16[1,4,4,128,128]{4,3,2,1,0:T(8,128)(2,1)} custom-call(s32[5]{0:T(128)} %pad_add_fusion.refs_0_.place_ref, bf16[128,4096]{1,0:T(8,128)(2,1)} %copy-done.4, bf16[128,4096]{1,0:T(8,128)(2,1)} %copy-done.5, bf16[128,4096]{1,0:T(8,128)(2,1)} %collective-permute-done.2.refs_3_, bf16[64,4096]{1,0:T(8,128)(2,1)} %copy-done.11, ...), custom_call_target="tpu_custom_call" | custom-call | flops 2147483648 | bytes 8388608 | tf_op jit(solution)/shard_map/pallas_call | solution.py:142
  78.7 3.9 %collective-permute-done.8.refs_5_ = bf16[32,4096]{1,0:T(8,128)(2,1)S(1)} collective-permute-done((bf16[32,4096]{1,0:T(8,128)(2,1)S(1)}, bf16[32,4096]{1,0:T(8,128)(2,1)S(1)}, u32[]{:S(2)}, u32[]{:S(2)}) %collective-permute-start.8) | collective-permute-done | bytes 262176 | tf_op jit(solution)/shard_map/ppermute | solution.py:35
  82.6 12.3 %collective-permute-done.6.refs_2_ = bf16[64,4096]{1,0:T(8,128)(2,1)S(1)} collective-permute-done((bf16[64,4096]{1,0:T(8,128)(2,1)S(1)}, bf16[64,4096]{1,0:T(8,128)(2,1)S(1)}, u32[]{:S(2)}, u32[]{:S(2)}) %collective-permute-start.6) | collective-permute-done | bytes 524320 | tf_op jit(solution)/shard_map/ppermute | solution.py:31
  96.1 6.8 %shard_map.75 = bf16[512,256]{1,0:T(8,128)(2,1)} custom-call(s32[5]{0:T(128)} %pad_add_fusion.refs_0_.place_ref, bf16[128,4096]{1,0:T(8,128)(2,1)} %copy-done.3, bf16[64,4096]{1,0:T(8,128)(2,1)} %copy-done.13, bf16[64,4096]{1,0:T(8,128)(2,1)} %copy-done.12, bf16[96,4096]{1,0:T(8,128)(2,1)} %copy-done.9, bf16[32,4096]{1,0:T(8,128)(2,1)} %copy-done.15, ...), custom_call_target="tpu_custom_call" | custom-call | flops 1073741824 | bytes 6291456 | tf_op jit(solution)/shard_map/pallas_call | solution.py:142
  103.0 3.1 %constant_dynamic-slice_fusion = bf16[256,4096]{1,0:T(8,128)(2,1)} fusion(bf16[512,4096]{1,0:T(8,128)(2,1)} %w_mine_ref.1, s32[]{:T(128)S(6)} %select_n.9), kind=kLoop, calls=%fused_computation.20 | loop fusion | bytes 4194308 | tf_op jit(solution)/shard_map/dynamic_slice | solution.py:425
  108.0 7.6 %shard_map.76 = bf16[1,4,4,128,128]{4,3,2,1,0:T(8,128)(2,1)} custom-call(s32[5]{0:T(128)} %pad_add_fusion.refs_0_.place_ref, bf16[128,4096]{1,0:T(8,128)(2,1)} %copy-done.3, bf16[64,4096]{1,0:T(8,128)(2,1)} %copy-done.13, bf16[64,4096]{1,0:T(8,128)(2,1)} %copy-done.12, bf16[96,4096]{1,0:T(8,128)(2,1)} %copy-done.9, bf16[32,4096]{1,0:T(8,128)(2,1)} %copy-done.15, ...), custom_call_target="tpu_custom_call" | custom-call | flops 2147483648 | bytes 8388608 | tf_op jit(solution)/shard_map/pallas_call | solution.py:142
  117.4 25.8 %shard_map.77 = (f32[2048,128]{1,0:T(8,128)}, f32[2048,128]{1,0:T(8,128)}, f32[2048,128]{1,0:T(8,128)}, f32[2048,128]{1,0:T(8,128)}, f32[2048,128]{1,0:T(8,128)}, /*index=5*/f32[2048,128]{1,0:T(8,128)}) custom-call(s32[5]{0:T(128)} %pad_add_fusion.refs_0_.place_ref, s32[32]{0:T(128)} %reshape.40.known_ref, bf16[1,2048,128]{2,1,0:T(8,128)(2,1)} %bitcast.11, ...), custom_call_target="tpu_custom_call" | custom-call | flops 17716740096 | bytes 10616832 | tf_op jit(solution)/shard_map/pallas_call | solution.py:300
  143.2 3.3 %all-gather.5.cloned.1.call-done.kv_ref = bf16[8192,256]{1,0:T(8,128)(2,1)} async-done(((bf16[512,256]{1,0:T(8,128)(2,1)}), bf16[8192,256]{1,0:T(8,128)(2,1)}) %all-gather.5.cloned.1.call-update) | async-done | bytes 4194320 | tf_op jit(solution)/shard_map/all_gather | solution.py:420
  146.6 15.4 %shard_map.79 = bf16[512,512]{1,0:T(8,128)(2,1)} custom-call(s32[5]{0:T(128)} %pad_add_fusion.refs_0_.place_ref, s32[32]{0:T(128)} %reshape.40.known_ref, bf16[2048,128]{1,0:T(8,128)(2,1)} %bitcast.14, bf16[8192,256]{1,0:T(8,128)(2,1)} %all-gather.5.cloned.1.call-done.kv_ref, f32[2048,128]{1,0:T(8,128)} %get-tuple-element.67.max_in, ...), custom_call_target="tpu_custom_call" | custom-call | flops 8858370048 | bytes 7340032 | tf_op jit(solution)/shard_map/pallas_call | solution.py:317
  162.4 2.5 %collective-permute-start.12 = (bf16[512,512]{1,0:T(8,128)(2,1)}, bf16[512,512]{1,0:T(8,128)(2,1)S(1)}, u32[]{:S(2)}, u32[]{:S(2)}) collective-permute-start(bf16[512,512]{1,0:T(8,128)(2,1)} %shard_map.79), channel_id=1, source_target_pairs={{0,1},{1,0},{2,3},{3,2},{4,5},{5,4},{6,7},{7,6},{8,9},{9,8},{10,11... | collective-permute-start | bytes 1572872 | tf_op jit(solution)/shard_map/ppermute | solution.py:35
  164.9 15.8 %shard_map.78.mine_ref = bf16[512,512]{1,0:T(8,128)(2,1)} custom-call(s32[5]{0:T(128)} %pad_add_fusion.refs_0_.place_ref, s32[32]{0:T(128)} %reshape.40.known_ref, bf16[2048,128]{1,0:T(8,128)(2,1)} %bitcast.12, bf16[8192,256]{1,0:T(8,128)(2,1)} %all-gather.5.cloned.1.call-done.kv_ref, f32[2048,128]{1,0:T(8,128)} %get-tuple-element.64.max_in, ...), custom_call_target="tpu_custom_call" | custom-call | flops 8858370048 | bytes 7340032 | tf_op jit(solution)/shard_map/pallas_call | solution.py:317
  181.7 6.6 %shard_map.80 = bf16[512,4096]{1,0:T(8,128)(2,1)S(1)} custom-call(s32[1]{0:T(128)} %bitcast.core_ref, bf16[512,512]{1,0:T(8,128)(2,1)S(1)} %copy-done.2, bf16[512,512]{1,0:T(8,128)(2,1)S(1)} %collective-permute-done.12.theirs_ref, bf16[512,4096]{1,0:T(8,128)(2,1)S(1)} %copy-done.1, bf16[256,4096]{1,0:T(8,128)(2,1)S(1)} %collective-permute-done.11.w_own_ref, ...), custom_call_target="tpu_custom_call" | custom-call | flops 4294967296 | bytes 12582912 | tf_op jit(solution)/shard_map/pallas_call | solution.py:351
  188.3 2.0 copy-done
  190.3 45.6 %reduce-scatter.2.cloned.1.call-done = bf16[128,4096]{1,0:T(8,128)(2,1)} async-done(((bf16[512,4096]{1,0:T(8,128)(2,1)}), bf16[128,4096]{1,0:T(8,128)(2,1)}) %reduce-scatter.2.cloned.1.call-update) | async-done | bytes 1048592 | tf_op jit(solution)/shard_map/reduce_scatter | solution.py:443
  236.0 2.4 fusion.3
  (84 shorter events, 24.7 us)
Async XLA Ops:
  6.5 109.1 %all-gather.3.cloned.1.call-start = ((), (), s32[]{:S(2)}) async-start(), calls=%async_computation.1 | async-start | bytes 4595712 | tf_op jit(solution)/shard_map/all_gather | solution.py:397
  10.3 26.4 %collective-permute-start = (bf16[128,4096]{1,0:T(8,128)(2,1)S(1)}, bf16[128,4096]{1,0:T(8,128)(2,1)S(1)}, u32[]{:S(2)}, u32[]{:S(2)}) collective-permute-start(bf16[128,4096]{1,0:T(8,128)(2,1)S(1)} %fusion.2.refs_1_), channel_id=1, source_target_pairs={{0,1},{1,0},{2,3},{3,2},{4,5},{5,4},{6,7},{7,6},{8,9},{9,8},{10,11... | collective-permute-start | bytes 3145736 | tf_op jit(solution)/shard_map/ppermute | solution.py:35
  14.2 26.3 %collective-permute-start.1 = (bf16[128,4096]{1,0:T(8,128)(2,1)S(1)}, bf16[128,4096]{1,0:T(8,128)(2,1)S(1)}, u32[]{:S(2)}, u32[]{:S(2)}) collective-permute-start(bf16[128,4096]{1,0:T(8,128)(2,1)S(1)} %fusion.2.refs_1_), channel_id=1, source_target_pairs={{0,2},{2,4},{4,6},{6,0},{1,3},{3,5},{5,7},{7,1},{8,10},{10,12},{12... | collective-permute-start | bytes 3145736 | tf_op jit(solution)/shard_map/ppermute | solution.py:31
  15.8 24.7 %collective-permute-start.2 = (bf16[128,4096]{1,0:T(8,128)(2,1)S(1)}, bf16[128,4096]{1,0:T(8,128)(2,1)}, u32[]{:S(2)}, u32[]{:S(2)}) collective-permute-start(bf16[128,4096]{1,0:T(8,128)(2,1)S(1)} %fusion.2.refs_1_), channel_id=1, source_target_pairs={{0,6},{2,0},{4,2},{6,4},{1,7},{3,1},{5,3},{7,5},{8,14},{10,8},{12,... | collective-permute-start | bytes 3145736 | tf_op jit(solution)/shard_map/ppermute | solution.py:31
  21.3 24.3 %copy-start.16 = (bf16[4096,128]{1,0:T(8,128)(2,1)S(1)}, bf16[4096,128]{1,0:T(8,128)(2,1)}, u32[]{:S(2)}) copy-start(bf16[4096,128]{1,0:T(8,128)(2,1)} %param.12) | copy-start | bytes 3145732
  21.3 24.3 %copy-start.17 = (bf16[4096,128]{1,0:T(8,128)(2,1)S(1)}, bf16[4096,128]{1,0:T(8,128)(2,1)}, u32[]{:S(2)}) copy-start(bf16[4096,128]{1,0:T(8,128)(2,1)} %param.11) | copy-start | bytes 3145732
  36.8 29.0 %copy-start.3 = (bf16[128,4096]{1,0:T(8,128)(2,1)}, bf16[128,4096]{1,0:T(8,128)(2,1)S(1)}, u32[]{:S(2)}) copy-start(bf16[128,4096]{1,0:T(8,128)(2,1)S(1)} %collective-permute-done.refs_1_) | copy-start | bytes 3145732
  40.6 13.2 %collective-permute-start.3 = (bf16[64,4096]{1,0:T(8,128)(2,1)S(1)}, bf16[64,4096]{1,0:T(8,128)(2,1)S(1)}, u32[]{:S(2)}, u32[]{:S(2)}) collective-permute-start(bf16[64,4096]{1,0:T(8,128)(2,1)S(1)} %get-tuple-element.74), channel_id=1, source_target_pairs={{0,2},{2,4},{4,6},{6,0},{1,3},{3,5},{5,7},{7,1},{8,10},{10,12},{12... | collective-permute-start | bytes 1572872 | tf_op jit(solution)/shard_map/ppermute | solution.py:31
  41.1 12.6 %collective-permute-start.5 = (bf16[64,4096]{1,0:T(8,128)(2,1)S(1)}, bf16[64,4096]{1,0:T(8,128)(2,1)S(1)}, u32[]{:S(2)}, u32[]{:S(2)}) collective-permute-start(bf16[64,4096]{1,0:T(8,128)(2,1)S(1)} %get-tuple-element.73), channel_id=1, source_target_pairs={{0,1},{1,0},{2,3},{3,2},{4,5},{5,4},{6,7},{7,6},{8,9},{9,8},{10,11... | collective-permute-start | bytes 1572872 | tf_op jit(solution)/shard_map/ppermute | solution.py:35
  42.6 11.9 %collective-permute-start.4 = (bf16[64,4096]{1,0:T(8,128)(2,1)S(1)}, bf16[64,4096]{1,0:T(8,128)(2,1)S(1)}, u32[]{:S(2)}, u32[]{:S(2)}) collective-permute-start(bf16[64,4096]{1,0:T(8,128)(2,1)S(1)} %slice.32), channel_id=1, source_target_pairs={{0,6},{2,0},{4,2},{6,4},{1,7},{3,1},{5,3},{7,5},{8,14},{10,8},{12,... | collective-permute-start | bytes 1572872 | tf_op jit(solution)/shard_map/ppermute | solution.py:31
  62.2 84.4 %all-gather.5.cloned.1.call-start = ((), (), s32[]{:S(2)}) async-start(), calls=%async_computation.2 | async-start | bytes 4456448 | tf_op jit(solution)/shard_map/all_gather | solution.py:420
  62.3 32.6 %collective-permute-start.7 = (bf16[96,4096]{1,0:T(8,128)(2,1)S(1)}, bf16[96,4096]{1,0:T(8,128)(2,1)S(1)}, u32[]{:S(2)}, u32[]{:S(2)}) collective-permute-start(bf16[96,4096]{1,0:T(8,128)(2,1)S(1)} %slice.36), channel_id=1, source_target_pairs={{0,6},{2,0},{4,2},{6,4},{1,7},{3,1},{5,3},{7,5},{8,14},{10,8},{12,... | collective-permute-start | bytes 2359304 | tf_op jit(solution)/shard_map/ppermute | solution.py:31
  65.7 29.2 %collective-permute-start.9 = (bf16[80,4096]{1,0:T(8,128)(2,1)S(1)}, bf16[80,4096]{1,0:T(8,128)(2,1)S(1)}, u32[]{:S(2)}, u32[]{:S(2)}) collective-permute-start(bf16[80,4096]{1,0:T(8,128)(2,1)S(1)} %slice.38), channel_id=1, source_target_pairs={{0,4},{2,6},{4,0},{6,2},{1,5},{3,7},{5,1},{7,3},{8,12},{10,14},{12... | collective-permute-start | bytes 1966088 | tf_op jit(solution)/shard_map/ppermute | solution.py:31
  65.8 29.0 %collective-permute-start.6 = (bf16[64,4096]{1,0:T(8,128)(2,1)S(1)}, bf16[64,4096]{1,0:T(8,128)(2,1)S(1)}, u32[]{:S(2)}, u32[]{:S(2)}) collective-permute-start(bf16[64,4096]{1,0:T(8,128)(2,1)S(1)} %slice.35), channel_id=1, source_target_pairs={{0,2},{2,4},{4,6},{6,0},{1,3},{3,5},{5,7},{7,1},{8,10},{10,12},{12... | collective-permute-start | bytes 1572872 | tf_op jit(solution)/shard_map/ppermute | solution.py:31
  66.8 15.8 %collective-permute-start.10 = (bf16[48,4096]{1,0:T(8,128)(2,1)S(1)}, bf16[48,4096]{1,0:T(8,128)(2,1)S(1)}, u32[]{:S(2)}, u32[]{:S(2)}) collective-permute-start(bf16[48,4096]{1,0:T(8,128)(2,1)S(1)} %slice.39), channel_id=1, source_target_pairs={{0,1},{1,0},{2,3},{3,2},{4,5},{5,4},{6,7},{7,6},{8,9},{9,8},{10,11... | collective-permute-start | bytes 1179656 | tf_op jit(solution)/shard_map/ppermute | solution.py:35
  69.6 12.9 %collective-permute-start.8 = (bf16[32,4096]{1,0:T(8,128)(2,1)S(1)}, bf16[32,4096]{1,0:T(8,128)(2,1)S(1)}, u32[]{:S(2)}, u32[]{:S(2)}) collective-permute-start(bf16[32,4096]{1,0:T(8,128)(2,1)S(1)} %slice.37), channel_id=1, source_target_pairs={{0,1},{1,0},{2,3},{3,2},{4,5},{5,4},{6,7},{7,6},{8,9},{9,8},{10,11... | collective-permute-start | bytes 786440 | tf_op jit(solution)/shard_map/ppermute | solution.py:35
  82.6 12.3 %copy-start.15 = (bf16[32,4096]{1,0:T(8,128)(2,1)}, bf16[32,4096]{1,0:T(8,128)(2,1)S(1)}, u32[]{:S(2)}) copy-start(bf16[32,4096]{1,0:T(8,128)(2,1)S(1)} %collective-permute-done.8.refs_5_) | copy-start | bytes 786436
  82.6 12.3 %copy-start.14 = (bf16[48,4096]{1,0:T(8,128)(2,1)}, bf16[48,4096]{1,0:T(8,128)(2,1)S(1)}, u32[]{:S(2)}) copy-start(bf16[48,4096]{1,0:T(8,128)(2,1)S(1)} %collective-permute-done.10.refs_7_) | copy-start | bytes 1179652
  103.0 133.0 %reduce-scatter.2.cloned.1.call-start = ((), (), s32[]{:S(2)}) async-start(), calls=%async_computation.3 | async-start | bytes 5242880 | tf_op jit(solution)/shard_map/reduce_scatter | solution.py:443
  106.2 55.9 %collective-permute-start.11 = (bf16[256,4096]{1,0:T(8,128)(2,1)}, bf16[256,4096]{1,0:T(8,128)(2,1)S(1)}, u32[]{:S(2)}, u32[]{:S(2)}) collective-permute-start(bf16[256,4096]{1,0:T(8,128)(2,1)} %constant_dynamic-slice_fusion), channel_id=1, source_target_pairs={{0,65},{65,0},{1,64},{64,1},{2,67},{67,2},{3,66},{66,3},{4,69},{69... | collective-permute-start | bytes 6291464 | tf_op jit(solution)/shard_map/ppermute | solution.py:427
  162.0 18.6 %collective-permute-start.13 = (bf16[256,4096]{1,0:T(8,128)(2,1)S(1)}, bf16[256,4096]{1,0:T(8,128)(2,1)}, u32[]{:S(2)}, u32[]{:S(2)}) collective-permute-start(bf16[256,4096]{1,0:T(8,128)(2,1)S(1)} %collective-permute-done.11.w_own_ref), channel_id=1, source_target_pairs={{0,8},{8,0},{1,9},{9,1},{2,10},{10,2},{3,11},{11,3},{4,12},{12,4},... | collective-permute-start | bytes 6291464 | tf_op jit(solution)/shard_map/ppermute | solution.py:439
  162.4 18.2 %collective-permute-start.12 = (bf16[512,512]{1,0:T(8,128)(2,1)}, bf16[512,512]{1,0:T(8,128)(2,1)S(1)}, u32[]{:S(2)}, u32[]{:S(2)}) collective-permute-start(bf16[512,512]{1,0:T(8,128)(2,1)} %shard_map.79), channel_id=1, source_target_pairs={{0,1},{1,0},{2,3},{3,2},{4,5},{5,4},{6,7},{7,6},{8,9},{9,8},{10,11... | collective-permute-start | bytes 1572872 | tf_op jit(solution)/shard_map/ppermute | solution.py:35
  164.9 15.8 %copy-start.1 = (bf16[512,4096]{1,0:T(8,128)(2,1)S(1)}, bf16[512,4096]{1,0:T(8,128)(2,1)}, u32[]{:S(2)}) copy-start(bf16[512,4096]{1,0:T(8,128)(2,1)} %w_mine_ref.1) | copy-start | bytes 12582916
  190.3 45.6 %copy-start.6 = (bf16[128,4096]{1,0:T(8,128)(2,1)S(1)}, bf16[128,4096]{1,0:T(8,128)(2,1)}, u32[]{:S(2)}) copy-start(bf16[128,4096]{1,0:T(8,128)(2,1)} %param.7) | copy-start | bytes 3145732
  (12 other events, 42.5 us)
Sparse Core Ops, SparseCore 0:
  62.3 46.9 all-gather.2
  111.0 35.5 all-gather.4
  190.5 45.4 reduce-scatter.1

commit v5 on v4

--- a/solution.py
+++ b/solution.py
@@ -389,7 +389,10 @@
     crossed = swap(ahead[DIRECT[0] :])
     tables = rope_tables(positions)
     w_kv = jnp.concatenate([w_key, w_value], axis=1)
-    near, crossed, w_kv = lax.optimization_barrier((near, crossed, w_kv))
+    core = lax.axis_index("core").astype(jnp.int32)
+    half_rows = w_out.shape[0] // 2
+    w_own = lax.dynamic_slice_in_dim(w_out, core * half_rows, half_rows, 0)
+    near, crossed, w_kv, w_own = lax.optimization_barrier((near, crossed, w_kv, w_own))
     kv_near = project(
         functools.partial(project_kv_kernel, other=False, tail=True),
         place, near, (w_kv,), tables, (4 * OWNED + TAIL, 2 * HEAD),
@@ -420,9 +423,6 @@
     kv_far_all = lax.all_gather(kv_far, CTX, axis=0, tiled=True)
     q_far = queries(far, True)
     kv_far, q_far = lax.optimization_barrier((kv_far, q_far))
-    core = lax.axis_index("core").astype(jnp.int32)
-    half_rows = w_out.shape[0] // 2
-    w_own = lax.dynamic_slice_in_dim(w_out, core * half_rows, half_rows, 0)
     w_own, _ = lax.optimization_barrier((w_own, far))
     w_own = lax.ppermute(w_own, ("y_lo", "y_hi"), [(0, 3), (3, 0), (1, 2), (2, 1)])
     kv_far = kv_far_all

time: 245 us -> 245 us (level)
    all_gather x1, waiting for transfers between devices: 3.35 us -> 6.54 us  [per_device(): kv_far_all = lax.all_gather(kv_far, CTX, axis=0, tiled=True)]
    unnamed x39 -> x41, local copies, waits for them, and re-layouts: 5.42 us -> 5.3 us
where the time goes in v5:
time: 245 us
  waiting for transfers between devices  93.5 us (38%)
  Pallas kernels  92.3 us (38%)
  starting transfers between devices  23.3 us (10%)
  between operations  13.4 us (5%)
  other arithmetic  11.7 us (5%)
  local copies, waits for them, and re-layouts  10.8 us (4%)
    reduce_scatter x1, waiting for transfers between devices, per_device(): terms.append(lax.psum_scatter(term, 'z', scatter_dimension=0, tiled=True))  45.6 us
    pallas_call x2, Pallas kernels, attend_far(): pl.pallas_call(functools.partial(attend_far_kernel, other=other, part=par...  31.2 us
    pallas_call x4, Pallas kernels, project(): pl.pallas_call(functools.partial(kernel, groups=tuple((tuple((p.shape[0]...  28.8 us
    pallas_call x1, Pallas kernels, attend_near(): pl.pallas_call(functools.partial(attend_near_kernel, heads=heads, n_ctx=n...  25.6 us
    ppermute x7, waiting for transfers between devices, turn(): return lax.ppermute(x, 'z', [(i, (i + by) % 4) for i in range(4)])  23.2 us
    ppermute x5, waiting for transfers between devices, swap(): return lax.ppermute(x, 'y_hi', [(0, 1), (1, 0)])  18 us
    ppermute x7, starting transfers between devices, turn(): return lax.ppermute(x, 'z', [(i, (i + by) % 4) for i in range(4)])  10.9 us
    ppermute x5, starting transfers between devices, swap(): return lax.ppermute(x, 'y_hi', [(0, 1), (1, 0)])  9.97 us
  transfers between devices with their start and end apart: 17, of which 8 were waited for; matrix products, arithmetic and copies ran while one was open for 5% of the time, Pallas kernels for 32%

profile of v5, /device:TPU:1, one launch (start us, length us, event | category | flops | bytes accessed | tf_op | source)
XLA Modules:
  0.0 244.9 jit_solution(14106620807425166530)
XLA Ops:
  10.3 3.8 %collective-permute-start = (bf16[128,4096]{1,0:T(8,128)(2,1)S(1)}, bf16[128,4096]{1,0:T(8,128)(2,1)S(1)}, u32[]{:S(2)}, u32[]{:S(2)}) collective-permute-start(bf16[128,4096]{1,0:T(8,128)(2,1)S(1)} %fusion.2.refs_1_), channel_id=1, source_target_pairs={{0,1},{1,0},{2,3},{3,2},{4,5},{5,4},{6,7},{7,6},{8,9},{9,8},{10,11... | collective-permute-start | bytes 3145736 | tf_op jit(solution)/shard_map/ppermute | solution.py:35
  15.8 2.1 collective-permute-start.2
  22.9 13.9 %collective-permute-done.refs_1_ = bf16[128,4096]{1,0:T(8,128)(2,1)S(1)} collective-permute-done((bf16[128,4096]{1,0:T(8,128)(2,1)S(1)}, bf16[128,4096]{1,0:T(8,128)(2,1)S(1)}, u32[]{:S(2)}, u32[]{:S(2)}) %collective-permute-start) | collective-permute-done | bytes 1048608 | tf_op jit(solution)/shard_map/ppermute | solution.py:35
  36.8 3.7 %collective-permute-done.1.refs_2_ = bf16[128,4096]{1,0:T(8,128)(2,1)S(1)} collective-permute-done((bf16[128,4096]{1,0:T(8,128)(2,1)S(1)}, bf16[128,4096]{1,0:T(8,128)(2,1)S(1)}, u32[]{:S(2)}, u32[]{:S(2)}) %collective-permute-start.1) | collective-permute-done | bytes 1048608 | tf_op jit(solution)/shard_map/ppermute | solution.py:31
  42.6 2.4 collective-permute-start.4
  47.2 6.5 %collective-permute-done.3.refs_4_ = bf16[64,4096]{1,0:T(8,128)(2,1)S(1)} collective-permute-done((bf16[64,4096]{1,0:T(8,128)(2,1)S(1)}, bf16[64,4096]{1,0:T(8,128)(2,1)S(1)}, u32[]{:S(2)}, u32[]{:S(2)}) %collective-permute-start.3) | collective-permute-done | bytes 524320 | tf_op jit(solution)/shard_map/ppermute | solution.py:31
  55.3 6.7 %shard_map.73 = bf16[528,256]{1,0:T(8,128)(2,1)} custom-call(s32[5]{0:T(128)} %pad_add_fusion.refs_0_.place_ref, bf16[128,4096]{1,0:T(8,128)(2,1)} %copy-done.5, bf16[128,4096]{1,0:T(8,128)(2,1)} %copy-done.6, bf16[128,4096]{1,0:T(8,128)(2,1)} %collective-permute-done.2.refs_3_, bf16[64,4096]{1,0:T(8,128)(2,1)} %copy-done.12, bf16[64,4096]{1,0:T(8,128)(2,1)} %copy-done.8, ...), custom_call_target="tpu_custom_call" | custom-call | flops 1073741824 | bytes 6291456 | tf_op jit(solution)/shard_map/pallas_call | solution.py:142
  62.2 3.5 %collective-permute-start.7 = (bf16[96,4096]{1,0:T(8,128)(2,1)S(1)}, bf16[96,4096]{1,0:T(8,128)(2,1)S(1)}, u32[]{:S(2)}, u32[]{:S(2)}) collective-permute-start(bf16[96,4096]{1,0:T(8,128)(2,1)S(1)} %slice.36), channel_id=1, source_target_pairs={{0,6},{2,0},{4,2},{6,4},{1,7},{3,1},{5,3},{7,5},{8,14},{10,8},{12,... | collective-permute-start | bytes 2359304 | tf_op jit(solution)/shard_map/ppermute | solution.py:31
  66.5 2.2 collective-permute-start.10
  70.8 7.7 %shard_map.74 = bf16[1,4,4,128,128]{4,3,2,1,0:T(8,128)(2,1)} custom-call(s32[5]{0:T(128)} %pad_add_fusion.refs_0_.place_ref, bf16[128,4096]{1,0:T(8,128)(2,1)} %copy-done.5, bf16[128,4096]{1,0:T(8,128)(2,1)} %copy-done.6, bf16[128,4096]{1,0:T(8,128)(2,1)} %collective-permute-done.2.refs_3_, bf16[64,4096]{1,0:T(8,128)(2,1)} %copy-done.12, ...), custom_call_target="tpu_custom_call" | custom-call | flops 2147483648 | bytes 8388608 | tf_op jit(solution)/shard_map/pallas_call | solution.py:142
  78.4 4.2 %collective-permute-done.8.refs_5_ = bf16[32,4096]{1,0:T(8,128)(2,1)S(1)} collective-permute-done((bf16[32,4096]{1,0:T(8,128)(2,1)S(1)}, bf16[32,4096]{1,0:T(8,128)(2,1)S(1)}, u32[]{:S(2)}, u32[]{:S(2)}) %collective-permute-start.8) | collective-permute-done | bytes 262176 | tf_op jit(solution)/shard_map/ppermute | solution.py:35
  82.6 12.2 %collective-permute-done.6.refs_2_ = bf16[64,4096]{1,0:T(8,128)(2,1)S(1)} collective-permute-done((bf16[64,4096]{1,0:T(8,128)(2,1)S(1)}, bf16[64,4096]{1,0:T(8,128)(2,1)S(1)}, u32[]{:S(2)}, u32[]{:S(2)}) %collective-permute-start.6) | collective-permute-done | bytes 524320 | tf_op jit(solution)/shard_map/ppermute | solution.py:31
  96.1 6.8 %shard_map.75 = bf16[512,256]{1,0:T(8,128)(2,1)} custom-call(s32[5]{0:T(128)} %pad_add_fusion.refs_0_.place_ref, bf16[128,4096]{1,0:T(8,128)(2,1)} %copy-done.4, bf16[64,4096]{1,0:T(8,128)(2,1)} %copy-done.14, bf16[64,4096]{1,0:T(8,128)(2,1)} %copy-done.13, bf16[96,4096]{1,0:T(8,128)(2,1)} %copy-done.10, bf16[32,4096]{1,0:T(8,128)(2,1)} %copy-done.16, ...), custom_call_target="tpu_custom_call" | custom-call | flops 1073741824 | bytes 6291456 | tf_op jit(solution)/shard_map/pallas_call | solution.py:142
  103.0 2.0 collective-permute-start.11
  105.0 7.6 %shard_map.76 = bf16[1,4,4,128,128]{4,3,2,1,0:T(8,128)(2,1)} custom-call(s32[5]{0:T(128)} %pad_add_fusion.refs_0_.place_ref, bf16[128,4096]{1,0:T(8,128)(2,1)} %copy-done.4, bf16[64,4096]{1,0:T(8,128)(2,1)} %copy-done.14, bf16[64,4096]{1,0:T(8,128)(2,1)} %copy-done.13, bf16[96,4096]{1,0:T(8,128)(2,1)} %copy-done.10, bf16[32,4096]{1,0:T(8,128)(2,1)} %copy-done.16, ...), custom_call_target="tpu_custom_call" | custom-call | flops 2147483648 | bytes 8388608 | tf_op jit(solution)/shard_map/pallas_call | solution.py:142
  114.4 25.6 %shard_map.77 = (f32[2048,128]{1,0:T(8,128)}, f32[2048,128]{1,0:T(8,128)}, f32[2048,128]{1,0:T(8,128)}, f32[2048,128]{1,0:T(8,128)}, f32[2048,128]{1,0:T(8,128)}, /*index=5*/f32[2048,128]{1,0:T(8,128)}) custom-call(s32[5]{0:T(128)} %pad_add_fusion.refs_0_.place_ref, s32[32]{0:T(128)} %reshape.40.known_ref, bf16[1,2048,128]{2,1,0:T(8,128)(2,1)} %bitcast.11, ...), custom_call_target="tpu_custom_call" | custom-call | flops 17716740096 | bytes 10616832 | tf_op jit(solution)/shard_map/pallas_call | solution.py:300
  140.0 6.5 %all-gather.5.cloned.1.call-done.kv_ref = bf16[8192,256]{1,0:T(8,128)(2,1)} async-done(((bf16[512,256]{1,0:T(8,128)(2,1)}), bf16[8192,256]{1,0:T(8,128)(2,1)}) %all-gather.5.cloned.1.call-update) | async-done | bytes 4194320 | tf_op jit(solution)/shard_map/all_gather | solution.py:423
  146.6 15.4 %shard_map.79 = bf16[512,512]{1,0:T(8,128)(2,1)} custom-call(s32[5]{0:T(128)} %pad_add_fusion.refs_0_.place_ref, s32[32]{0:T(128)} %reshape.40.known_ref, bf16[2048,128]{1,0:T(8,128)(2,1)} %bitcast.14, bf16[8192,256]{1,0:T(8,128)(2,1)} %all-gather.5.cloned.1.call-done.kv_ref, f32[2048,128]{1,0:T(8,128)} %get-tuple-element.68.max_in, ...), custom_call_target="tpu_custom_call" | custom-call | flops 8858370048 | bytes 7340032 | tf_op jit(solution)/shard_map/pallas_call | solution.py:317
  162.4 2.4 collective-permute-start.12
  164.8 15.8 %shard_map.78.mine_ref = bf16[512,512]{1,0:T(8,128)(2,1)} custom-call(s32[5]{0:T(128)} %pad_add_fusion.refs_0_.place_ref, s32[32]{0:T(128)} %reshape.40.known_ref, bf16[2048,128]{1,0:T(8,128)(2,1)} %bitcast.12, bf16[8192,256]{1,0:T(8,128)(2,1)} %all-gather.5.cloned.1.call-done.kv_ref, f32[2048,128]{1,0:T(8,128)} %get-tuple-element.65.max_in, ...), custom_call_target="tpu_custom_call" | custom-call | flops 8858370048 | bytes 7340032 | tf_op jit(solution)/shard_map/pallas_call | solution.py:317
  181.7 6.6 %shard_map.80 = bf16[512,4096]{1,0:T(8,128)(2,1)S(1)} custom-call(s32[1]{0:T(128)} %bitcast.core_ref, bf16[512,512]{1,0:T(8,128)(2,1)S(1)} %copy-done.3, bf16[512,512]{1,0:T(8,128)(2,1)S(1)} %collective-permute-done.12.theirs_ref, bf16[512,4096]{1,0:T(8,128)(2,1)S(1)} %copy-done.2, bf16[256,4096]{1,0:T(8,128)(2,1)S(1)} %collective-permute-done.11.w_own_ref, ...), custom_call_target="tpu_custom_call" | custom-call | flops 4294967296 | bytes 12582912 | tf_op jit(solution)/shard_map/pallas_call | solution.py:351
  188.3 2.0 copy-done
  190.3 45.6 %reduce-scatter.2.cloned.1.call-done = bf16[128,4096]{1,0:T(8,128)(2,1)} async-done(((bf16[512,4096]{1,0:T(8,128)(2,1)}), bf16[128,4096]{1,0:T(8,128)(2,1)}) %reduce-scatter.2.cloned.1.call-update) | async-done | bytes 1048592 | tf_op jit(solution)/shard_map/reduce_scatter | solution.py:443
  235.9 2.4 fusion.3
  (86 shorter events, 23.8 us)
Async XLA Ops:
  6.5 106.1 %all-gather.3.cloned.1.call-start = ((), (), s32[]{:S(2)}) async-start(), calls=%async_computation.1 | async-start | bytes 4595712 | tf_op jit(solution)/shard_map/all_gather | solution.py:400
  10.3 26.4 %collective-permute-start = (bf16[128,4096]{1,0:T(8,128)(2,1)S(1)}, bf16[128,4096]{1,0:T(8,128)(2,1)S(1)}, u32[]{:S(2)}, u32[]{:S(2)}) collective-permute-start(bf16[128,4096]{1,0:T(8,128)(2,1)S(1)} %fusion.2.refs_1_), channel_id=1, source_target_pairs={{0,1},{1,0},{2,3},{3,2},{4,5},{5,4},{6,7},{7,6},{8,9},{9,8},{10,11... | collective-permute-start | bytes 3145736 | tf_op jit(solution)/shard_map/ppermute | solution.py:35
  14.2 26.3 %collective-permute-start.1 = (bf16[128,4096]{1,0:T(8,128)(2,1)S(1)}, bf16[128,4096]{1,0:T(8,128)(2,1)S(1)}, u32[]{:S(2)}, u32[]{:S(2)}) collective-permute-start(bf16[128,4096]{1,0:T(8,128)(2,1)S(1)} %fusion.2.refs_1_), channel_id=1, source_target_pairs={{0,2},{2,4},{4,6},{6,0},{1,3},{3,5},{5,7},{7,1},{8,10},{10,12},{12... | collective-permute-start | bytes 3145736 | tf_op jit(solution)/shard_map/ppermute | solution.py:31
  15.8 24.7 %collective-permute-start.2 = (bf16[128,4096]{1,0:T(8,128)(2,1)S(1)}, bf16[128,4096]{1,0:T(8,128)(2,1)}, u32[]{:S(2)}, u32[]{:S(2)}) collective-permute-start(bf16[128,4096]{1,0:T(8,128)(2,1)S(1)} %fusion.2.refs_1_), channel_id=1, source_target_pairs={{0,6},{2,0},{4,2},{6,4},{1,7},{3,1},{5,3},{7,5},{8,14},{10,8},{12,... | collective-permute-start | bytes 3145736 | tf_op jit(solution)/shard_map/ppermute | solution.py:31
  22.9 22.7 %copy-start.17 = (bf16[4096,128]{1,0:T(8,128)(2,1)S(1)}, bf16[4096,128]{1,0:T(8,128)(2,1)}, u32[]{:S(2)}) copy-start(bf16[4096,128]{1,0:T(8,128)(2,1)} %param.12) | copy-start | bytes 3145732
  22.9 22.7 %copy-start.18 = (bf16[4096,128]{1,0:T(8,128)(2,1)S(1)}, bf16[4096,128]{1,0:T(8,128)(2,1)}, u32[]{:S(2)}) copy-start(bf16[4096,128]{1,0:T(8,128)(2,1)} %param.11) | copy-start | bytes 3145732
  36.8 29.0 %copy-start.4 = (bf16[128,4096]{1,0:T(8,128)(2,1)}, bf16[128,4096]{1,0:T(8,128)(2,1)S(1)}, u32[]{:S(2)}) copy-start(bf16[128,4096]{1,0:T(8,128)(2,1)S(1)} %collective-permute-done.refs_1_) | copy-start | bytes 3145732
  40.6 13.2 %collective-permute-start.3 = (bf16[64,4096]{1,0:T(8,128)(2,1)S(1)}, bf16[64,4096]{1,0:T(8,128)(2,1)S(1)}, u32[]{:S(2)}, u32[]{:S(2)}) collective-permute-start(bf16[64,4096]{1,0:T(8,128)(2,1)S(1)} %get-tuple-element.76), channel_id=1, source_target_pairs={{0,2},{2,4},{4,6},{6,0},{1,3},{3,5},{5,7},{7,1},{8,10},{10,12},{12... | collective-permute-start | bytes 1572872 | tf_op jit(solution)/shard_map/ppermute | solution.py:31
  41.1 12.6 %collective-permute-start.5 = (bf16[64,4096]{1,0:T(8,128)(2,1)S(1)}, bf16[64,4096]{1,0:T(8,128)(2,1)S(1)}, u32[]{:S(2)}, u32[]{:S(2)}) collective-permute-start(bf16[64,4096]{1,0:T(8,128)(2,1)S(1)} %get-tuple-element.75), channel_id=1, source_target_pairs={{0,1},{1,0},{2,3},{3,2},{4,5},{5,4},{6,7},{7,6},{8,9},{9,8},{10,11... | collective-permute-start | bytes 1572872 | tf_op jit(solution)/shard_map/ppermute | solution.py:35
  42.6 11.9 %collective-permute-start.4 = (bf16[64,4096]{1,0:T(8,128)(2,1)S(1)}, bf16[64,4096]{1,0:T(8,128)(2,1)S(1)}, u32[]{:S(2)}, u32[]{:S(2)}) collective-permute-start(bf16[64,4096]{1,0:T(8,128)(2,1)S(1)} %slice.32), channel_id=1, source_target_pairs={{0,6},{2,0},{4,2},{6,4},{1,7},{3,1},{5,3},{7,5},{8,14},{10,8},{12,... | collective-permute-start | bytes 1572872 | tf_op jit(solution)/shard_map/ppermute | solution.py:31
  53.7 12.8 %copy-start.13 = (bf16[64,4096]{1,0:T(8,128)(2,1)}, bf16[64,4096]{1,0:T(8,128)(2,1)S(1)}, u32[]{:S(2)}) copy-start(bf16[64,4096]{1,0:T(8,128)(2,1)S(1)} %collective-permute-done.5.refs_3_) | copy-start | bytes 1572868
  62.0 84.5 %all-gather.5.cloned.1.call-start = ((), (), s32[]{:S(2)}) async-start(), calls=%async_computation.2 | async-start | bytes 4456448 | tf_op jit(solution)/shard_map/all_gather | solution.py:423
  62.2 32.7 %collective-permute-start.7 = (bf16[96,4096]{1,0:T(8,128)(2,1)S(1)}, bf16[96,4096]{1,0:T(8,128)(2,1)S(1)}, u32[]{:S(2)}, u32[]{:S(2)}) collective-permute-start(bf16[96,4096]{1,0:T(8,128)(2,1)S(1)} %slice.36), channel_id=1, source_target_pairs={{0,6},{2,0},{4,2},{6,4},{1,7},{3,1},{5,3},{7,5},{8,14},{10,8},{12,... | collective-permute-start | bytes 2359304 | tf_op jit(solution)/shard_map/ppermute | solution.py:31
  65.7 29.2 %collective-permute-start.9 = (bf16[80,4096]{1,0:T(8,128)(2,1)S(1)}, bf16[80,4096]{1,0:T(8,128)(2,1)S(1)}, u32[]{:S(2)}, u32[]{:S(2)}) collective-permute-start(bf16[80,4096]{1,0:T(8,128)(2,1)S(1)} %slice.38), channel_id=1, source_target_pairs={{0,4},{2,6},{4,0},{6,2},{1,5},{3,7},{5,1},{7,3},{8,12},{10,14},{12... | collective-permute-start | bytes 1966088 | tf_op jit(solution)/shard_map/ppermute | solution.py:31
  65.8 29.0 %collective-permute-start.6 = (bf16[64,4096]{1,0:T(8,128)(2,1)S(1)}, bf16[64,4096]{1,0:T(8,128)(2,1)S(1)}, u32[]{:S(2)}, u32[]{:S(2)}) collective-permute-start(bf16[64,4096]{1,0:T(8,128)(2,1)S(1)} %slice.35), channel_id=1, source_target_pairs={{0,2},{2,4},{4,6},{6,0},{1,3},{3,5},{5,7},{7,1},{8,10},{10,12},{12... | collective-permute-start | bytes 1572872 | tf_op jit(solution)/shard_map/ppermute | solution.py:31
  66.5 16.1 %collective-permute-start.10 = (bf16[48,4096]{1,0:T(8,128)(2,1)S(1)}, bf16[48,4096]{1,0:T(8,128)(2,1)S(1)}, u32[]{:S(2)}, u32[]{:S(2)}) collective-permute-start(bf16[48,4096]{1,0:T(8,128)(2,1)S(1)} %slice.39), channel_id=1, source_target_pairs={{0,1},{1,0},{2,3},{3,2},{4,5},{5,4},{6,7},{7,6},{8,9},{9,8},{10,11... | collective-permute-start | bytes 1179656 | tf_op jit(solution)/shard_map/ppermute | solution.py:35
  69.6 13.0 %collective-permute-start.8 = (bf16[32,4096]{1,0:T(8,128)(2,1)S(1)}, bf16[32,4096]{1,0:T(8,128)(2,1)S(1)}, u32[]{:S(2)}, u32[]{:S(2)}) collective-permute-start(bf16[32,4096]{1,0:T(8,128)(2,1)S(1)} %slice.37), channel_id=1, source_target_pairs={{0,1},{1,0},{2,3},{3,2},{4,5},{5,4},{6,7},{7,6},{8,9},{9,8},{10,11... | collective-permute-start | bytes 786440 | tf_op jit(solution)/shard_map/ppermute | solution.py:35
  82.6 12.3 %copy-start.15 = (bf16[48,4096]{1,0:T(8,128)(2,1)}, bf16[48,4096]{1,0:T(8,128)(2,1)S(1)}, u32[]{:S(2)}) copy-start(bf16[48,4096]{1,0:T(8,128)(2,1)S(1)} %collective-permute-done.10.refs_7_) | copy-start | bytes 1179652
  103.0 133.0 %reduce-scatter.2.cloned.1.call-start = ((), (), s32[]{:S(2)}) async-start(), calls=%async_computation.3 | async-start | bytes 5242880 | tf_op jit(solution)/shard_map/reduce_scatter | solution.py:443
  103.0 59.0 %collective-permute-start.11 = (bf16[256,4096]{1,0:T(8,128)(2,1)}, bf16[256,4096]{1,0:T(8,128)(2,1)S(1)}, u32[]{:S(2)}, u32[]{:S(2)}) collective-permute-start(bf16[256,4096]{1,0:T(8,128)(2,1)} %constant_dynamic-slice_fusion), channel_id=1, source_target_pairs={{0,65},{65,0},{1,64},{64,1},{2,67},{67,2},{3,66},{66,3},{4,69},{69... | collective-permute-start | bytes 6291464 | tf_op jit(solution)/shard_map/ppermute | solution.py:427
  162.0 18.6 %collective-permute-start.13 = (bf16[256,4096]{1,0:T(8,128)(2,1)S(1)}, bf16[256,4096]{1,0:T(8,128)(2,1)}, u32[]{:S(2)}, u32[]{:S(2)}) collective-permute-start(bf16[256,4096]{1,0:T(8,128)(2,1)S(1)} %collective-permute-done.11.w_own_ref), channel_id=1, source_target_pairs={{0,8},{8,0},{1,9},{9,1},{2,10},{10,2},{3,11},{11,3},{4,12},{12,4},... | collective-permute-start | bytes 6291464 | tf_op jit(solution)/shard_map/ppermute | solution.py:439
  162.4 18.2 %collective-permute-start.12 = (bf16[512,512]{1,0:T(8,128)(2,1)}, bf16[512,512]{1,0:T(8,128)(2,1)S(1)}, u32[]{:S(2)}, u32[]{:S(2)}) collective-permute-start(bf16[512,512]{1,0:T(8,128)(2,1)} %shard_map.79), channel_id=1, source_target_pairs={{0,1},{1,0},{2,3},{3,2},{4,5},{5,4},{6,7},{7,6},{8,9},{9,8},{10,11... | collective-permute-start | bytes 1572872 | tf_op jit(solution)/shard_map/ppermute | solution.py:35
  164.8 15.8 %copy-start.2 = (bf16[512,4096]{1,0:T(8,128)(2,1)S(1)}, bf16[512,4096]{1,0:T(8,128)(2,1)}, u32[]{:S(2)}) copy-start(bf16[512,4096]{1,0:T(8,128)(2,1)} %w_mine_ref.1) | copy-start | bytes 12582916
  190.3 45.6 %copy-start.7 = (bf16[128,4096]{1,0:T(8,128)(2,1)S(1)}, bf16[128,4096]{1,0:T(8,128)(2,1)}, u32[]{:S(2)}) copy-start(bf16[128,4096]{1,0:T(8,128)(2,1)} %param.7) | copy-start | bytes 3145732
  (13 other events, 56.9 us)
Sparse Core Ops, SparseCore 0:
  62.2 47.0 all-gather.2
  111.0 35.5 all-gather.4
  190.4 45.4 reduce-scatter.1
